TPU v7x, 32 devices: a whole 2x2x4 slice. The times are simulated.
32 devices in a mesh: tx: 4 (over y, core), ty: 8 (over z, x).
Axes of the slice: x: 2, y: 2, z: 4, core: 2. Of those that a mesh axis runs over, the one named last changes fastest.
Arguments:
- increments: bfloat16 [3, 8, 576, 2048], P(None, None, 'tx', 'ty'), may hold values from -6 to 6
- remap_weights: bfloat16 [4, 8, 144, 2, 128, 256], P('tx', 'ty'), may hold values from -0.375 to 0.375
- dest_offset: int32 [4, 8, 144, 2], P('tx', 'ty'), may hold values from 0 to 3, as said below
- slot_patch: int32 [4, 8, 4, 108], P('tx', 'ty'), may hold values from 0 to 143, as said below
- rotation: int32 [2, 4], replicated, may hold values from 0 to 3
- basis: float32 [4, 384, 1536], P(None, 'ty', 'tx'), may hold values from -4 to 4
- inv_metric_diag: float32 [2, 384, 1536], P(None, 'ty', 'tx'), may hold values from 0.7 to 1.7
- inv_metric_cross: float32 [384, 1536], P('ty', 'tx'), may hold values from -0.5 to 0.5
- thickness: float32 [8, 384, 1536], P(None, 'ty', 'tx'), may hold values from -6 to 6
- wind_first: float32 [8, 384, 1536], P(None, 'ty', 'tx'), may hold values from -6 to 6
- wind_second: float32 [8, 384, 1536], P(None, 'ty', 'tx'), may hold values from -6 to 6
Outputs:
- thickness_new: float32 [8, 384, 1536], P(None, 'ty', 'tx')
- wind_first_new: float32 [8, 384, 1536], P(None, 'ty', 'tx')
- wind_second_new: float32 [8, 384, 1536], P(None, 'ty', 'tx')
Inputs may be any that keep to these rules, and one draw needn't show every extreme that they name: `dest_offset`: the intersections of one block name every one of the 4 distances at least 36 and at most 108 times, and one of them exactly 108 times. In every tx row some tile owner receives exactly 108 intersections from each of the 4 blocks that send to it. `slot_patch`: slots past the number of intersections that arrive from a sender receive nothing. The used slots of one tile owner name every one of its 144 patches at least once.
All inputs are finite; a program needn't handle non-finite values.
Results may differ from a plain program's by a relative error of at most 0.0003.
Values sent between devices are 32-bit elements; how exact they have to be, the bound alone decides.
No kernel may reach another device: no remote copies, remote signals or barrier semaphores. Data moves between devices by JAX's collectives and lax.ppermute only.
A program may use at most 192 MiB of HBM per device.

v0:
```python
import jax
import jax.numpy as jnp
from jax import lax
from jax.sharding import PartitionSpec as P

PANELS = 4
STEPS = 4
TPATCH = 128


COURANT = 0.15
GRADIENT = 0.3


def from_behind(array, axis, by):
    size = lax.axis_size(axis)
    return lax.ppermute(array, axis, [(i, (i + by) % size) for i in range(size)])


def padded(cells, sides, width, closed):
    for axis, dim in sides:
        count = lax.axis_size(axis)
        ends = count if closed else count - 1
        head = lax.slice_in_dim(cells, 0, width, axis=dim)
        tail = lax.slice_in_dim(cells, cells.shape[dim] - width, cells.shape[dim], axis=dim)
        cells = jnp.concatenate(
            [
                lax.ppermute(tail, axis, [(i, (i + 1) % count) for i in range(ends)]),
                cells,
                lax.ppermute(head, axis, [((i + 1) % count, i) for i in range(ends)]),
            ],
            axis=dim,
        )
    return cells


def quarter_turn(code):
    cosine = (code == 0).astype(jnp.float32) - (code == 2).astype(jnp.float32)
    sine_value = (code == 1).astype(jnp.float32) - (code == 3).astype(jnp.float32)
    return (cosine, sine_value)


def advance(
    depth,
    cov_first,
    cov_second,
    con_first,
    con_second,
    depth_below,
    second_below,
    depth_above,
    second_above,
    depth_left,
    first_left,
    depth_right,
    first_right,
    wall_left,
    wall_right,
):
    face_below = 0.5 * (con_second + second_below)
    flux_below = jnp.maximum(face_below, 0.0) * depth_below + jnp.minimum(face_below, 0.0) * depth
    face_above = 0.5 * (con_second + second_above)
    flux_above = jnp.maximum(face_above, 0.0) * depth + jnp.minimum(face_above, 0.0) * depth_above
    face_left = 0.5 * (con_first + first_left) * wall_left
    flux_left = jnp.maximum(face_left, 0.0) * depth_left + jnp.minimum(face_left, 0.0) * depth
    face_right = 0.5 * (con_first + first_right) * wall_right
    flux_right = jnp.maximum(face_right, 0.0) * depth + jnp.minimum(face_right, 0.0) * depth_right
    new_depth = depth - COURANT * (flux_right - flux_left + (flux_above - flux_below))
    new_first = cov_first - GRADIENT * 0.5 * (depth_right - depth_left)
    new_second = cov_second - GRADIENT * 0.5 * (depth_above - depth_below)
    return (new_depth, new_first, new_second)


def rotation_codes(global_rows, total_rows, rotation):
    panel_rows = total_rows // PANELS
    panel = global_rows // panel_rows
    panel_iota = jnp.arange(PANELS, dtype=jnp.int32)
    matches = panel_iota[None, :] == panel[:, None]
    lower_code = jnp.sum(jnp.where(matches, rotation[0][None, :], 0), axis=1)
    upper_code = jnp.sum(jnp.where(matches, rotation[1][None, :], 0), axis=1)
    below_codes = jnp.where(global_rows % panel_rows == 0, lower_code, 0)
    above_codes = jnp.where(global_rows % panel_rows == panel_rows - 1, upper_code, 0)
    return (below_codes[:, None], above_codes[:, None])


def body(
    increments,
    remap_weights,
    dest_offset,
    slot_patch,
    rotation,
    basis,
    inv_metric_diag,
    inv_metric_cross,
    thickness,
    wind_first,
    wind_second,
):
    levels = thickness.shape[0]
    tile_rows = thickness.shape[1]
    tile_cols = thickness.shape[2]
    tx_count = lax.axis_size("tx")
    ty_count = lax.axis_size("ty")
    owners = slot_patch.shape[2]
    capacity = slot_patch.shape[3]
    patch_count = tile_rows * tile_cols // TPATCH
    row_width = 3 * levels * TPATCH
    tx_index = lax.axis_index("tx")
    ty_index = lax.axis_index("ty")
    partial_terms = jnp.einsum(
        "clsk,stpk->stclp", increments, remap_weights[0, 0], preferred_element_type=jnp.float32
    )
    entries = partial_terms.shape[0] * partial_terms.shape[1]
    partial_terms = partial_terms.reshape(entries, row_width)
    offsets = dest_offset.reshape(entries)
    onehot = (offsets[:, None] == jnp.arange(owners, dtype=jnp.int32)[None, :]).astype(jnp.int32)
    earlier = jnp.cumsum(onehot, axis=0) - onehot
    slot_index = jnp.sum(earlier * onehot, axis=1)
    position = offsets * capacity + slot_index
    outgoing = (
        jnp.zeros((owners * capacity, row_width), jnp.float32)
        .at[position]
        .set(partial_terms)
        .reshape(owners, capacity, row_width)
    )
    pieces = [outgoing[0]]
    for offset in range(1, owners):
        pieces.append(from_behind(outgoing[offset], "ty", offset))
    received = jnp.stack(pieces)
    patches = (
        jnp.zeros((patch_count, row_width), jnp.float32)
        .at[slot_patch.reshape(-1)]
        .add(received.reshape(-1, row_width))
    )
    blocks_per_row = tile_cols // TPATCH
    tiles = (
        patches.reshape(tile_rows, blocks_per_row, 3, levels, TPATCH)
        .transpose(2, 3, 0, 1, 4)
        .reshape(3, levels, tile_rows, tile_cols)
    )
    cov_first = wind_first + basis[0] * tiles[0] + basis[1] * tiles[1]
    cov_second = wind_second + basis[2] * tiles[0] + basis[3] * tiles[1]
    depth = thickness + tiles[2]
    total_rows = tile_rows * ty_count
    global_rows = ty_index * tile_rows + jnp.arange(tile_rows, dtype=jnp.int32)
    below_codes, above_codes = rotation_codes(global_rows, total_rows, rotation)
    cos_below, sin_below = quarter_turn(below_codes)
    cos_above, sin_above = quarter_turn(above_codes)
    col_iota = jnp.arange(tile_cols, dtype=jnp.int32)
    wall_left = jnp.where((tx_index == 0) & (col_iota == 0), 0.0, 1.0).astype(jnp.float32)
    wall_right = jnp.where(
        (tx_index == tx_count - 1) & (col_iota == tile_cols - 1), 0.0, 1.0
    ).astype(jnp.float32)
    for iteration in range(STEPS):
        con_first = inv_metric_diag[0] * cov_first + inv_metric_cross * cov_second
        con_second = inv_metric_cross * cov_first + inv_metric_diag[1] * cov_second
        row_ext = padded(jnp.stack([depth, con_first, con_second]), (("ty", 2),), 1, True)
        col_ext = padded(jnp.stack([depth, con_first]), (("tx", 3),), 1, False)
        lower = row_ext[:, :, :-2]
        upper = row_ext[:, :, 2:]
        second_below = sin_below * lower[1] + cos_below * lower[2]
        second_above = sin_above * upper[1] + cos_above * upper[2]
        depth, cov_first, cov_second = advance(
            depth,
            cov_first,
            cov_second,
            con_first,
            con_second,
            lower[0],
            second_below,
            upper[0],
            second_above,
            col_ext[0, :, :, :-2],
            col_ext[1, :, :, :-2],
            col_ext[0, :, :, 2:],
            col_ext[1, :, :, 2:],
            wall_left,
            wall_right,
        )
    return (depth, cov_first, cov_second)


def solution(mesh):
    in_specs = (
        P(None, None, "tx", "ty"),
        P("tx", "ty", None, None, None, None),
        P("tx", "ty", None, None),
        P("tx", "ty", None, None),
        P(),
        P(None, "ty", "tx"),
        P(None, "ty", "tx"),
        P("ty", "tx"),
        P(None, "ty", "tx"),
        P(None, "ty", "tx"),
        P(None, "ty", "tx"),
    )
    out_specs = (P(None, "ty", "tx"), P(None, "ty", "tx"), P(None, "ty", "tx"))
    return jax.shard_map(body, mesh=mesh, in_specs=in_specs, out_specs=out_specs, check_vma=False)
```

profile of v0, /device:TPU:1, one launch (start us, length us, event | category | flops | bytes accessed | tf_op | source)
XLA Modules:
  0.0 248.1 jit_solution(305705327196378859)
XLA Ops:
  4.4 10.7 %fusion.4 = f32[144,2,3,8,128]{4,3,2,1,0:T(8,128)} fusion(bf16[1,1,144,2,128,256]{5,4,3,2,1,0:T(8,128)(2,1)} %param.12, bf16[3,8,144,256,1]{3,2,1,0,4:T(8,128)(2,1)S(1)} %bitcast.408), kind=kOutput, calls=%fused_computation.7 | convolution fusion | flops 452984832 | bytes 24182784 | tf_op jit(solution)/shard_map/clsk,stpk->stclp/dot_general | solution.py:110
  15.1 4.8 %reshape.214 = f32[288,3072]{1,0:T(8,128)} reshape(f32[144,2,3,8,128]{4,3,2,1,0:T(8,128)} %fusion.4) | data formatting | bytes 7077888 | tf_op jit(solution)/shard_map/reshape | solution.py:114
  19.9 6.7 %scatter_custom_fusion = f32[432,3072]{1,0:T(8,128)} fusion(s32[288]{0:T(512)S(1)} %fusion.94, f32[288,3072]{1,0:T(8,128)} %reshape.214, f32[]{:T(128)} %constant.20.clone.1), kind=kCustom, calls=%fused_computation.5 | custom fusion | bytes 5308928 | tf_op jit(solution)/shard_map/scatter | solution.py:123
  26.6 4.9 %slice_bitcast_fusion = (f32[1,108,3072]{2,1,0:T(8,128)S(1)}, f32[108,3072]{1,0:T(8,128)}, f32[108,3072]{1,0:T(8,128)}, f32[108,3072]{1,0:T(8,128)S(1)}) fusion(f32[432,3072]{1,0:T(8,128)} %scatter_custom_fusion), kind=kLoop, calls=%fused_computation.9 | loop fusion | bytes 10616832 | tf_op jit(solution)/shard_map/slice | solution.py:126
  31.5 2.1 collective-permute-start.1
  33.6 2.2 collective-permute-start.2
  38.1 27.7 %collective-permute-done.1 = f32[108,3072]{1,0:T(8,128)} collective-permute-done((f32[108,3072]{1,0:T(8,128)}, f32[108,3072]{1,0:T(8,128)}, u32[]{:S(2)}, u32[]{:S(2)}) %collective-permute-start.1) | collective-permute-done | bytes 1327136 | tf_op jit(solution)/shard_map/ppermute | solution.py:17
  65.9 90.1 %collective-permute-done.2 = f32[108,3072]{1,0:T(8,128)} collective-permute-done((f32[108,3072]{1,0:T(8,128)}, f32[108,3072]{1,0:T(8,128)}, u32[]{:S(2)}, u32[]{:S(2)}) %collective-permute-start.2) | collective-permute-done | bytes 1327136 | tf_op jit(solution)/shard_map/ppermute | solution.py:17
  156.0 5.2 %pad_maximum_fusion = f32[4,108,3072]{2,1,0:T(8,128)} fusion(f32[1,108,3072]{2,1,0:T(8,128)} %bitcast.11, f32[1,108,3072]{2,1,0:T(8,128)} %bitcast.10, f32[1,108,3072]{2,1,0:T(8,128)} %bitcast.9, f32[1,108,3072]{2,1,0:T(8,128)S(1)} %get-tuple-element.17), kind=kLoop, calls=%fused_computation.4 | loop fusion | flops 3981312 | bytes 10616832 | tf_op jit(solution)/shard_map/stack | solution.py:129
  161.2 4.4 %reshape.222 = f32[432,3072]{1,0:T(8,128)} reshape(f32[4,108,3072]{2,1,0:T(8,128)} %pad_maximum_fusion) | data formatting | bytes 10616832 | tf_op jit(solution)/shard_map/reshape | solution.py:133
  165.7 9.8 %scatter_custom_fusion.1 = f32[144,3072]{1,0:T(8,128)S(1)} fusion(s32[432]{0:T(512)S(1)} %bitcast.429, f32[432,3072]{1,0:T(8,128)} %reshape.222, f32[]{:T(128)} %constant.20.clone.1), kind=kCustom, calls=%fused_computation.10 | custom fusion | flops 1327104 | bytes 1769984 | tf_op jit(solution)/shard_map/scatter-add | solution.py:133
  183.0 2.9 %collective-permute-start.3 = (f32[2,8,48,1]{3,2,1,0:T(8,128)S(1)}, f32[2,8,48,1]{3,2,1,0:T(8,128)S(1)}, u32[]{:S(2)}, u32[]{:S(2)}) collective-permute-start(f32[2,8,48,1]{3,2,1,0:T(8,128)S(1)} %get-tuple-element.40), channel_id=1, source_target_pairs={{8,0},{16,8},{24,16},{9,1},{17,9},{25,17},{10,2},{18,10},{26,18},{... | collective-permute-start | bytes 9224 | tf_op jit(solution)/shard_map/ppermute | solution.py:30
  185.9 3.3 %collective-permute-start.4 = (f32[2,8,48,1]{3,2,1,0:T(8,128)S(1)}, f32[2,8,48,1]{3,2,1,0:T(8,128)S(1)}, u32[]{:S(2)}, u32[]{:S(2)}) collective-permute-start(f32[2,8,48,1]{3,2,1,0:T(8,128)S(1)} %get-tuple-element.41), channel_id=1, source_target_pairs={{0,8},{8,16},{16,24},{1,9},{9,17},{17,25},{2,10},{10,18},{18,26},{... | collective-permute-start | bytes 9224 | tf_op jit(solution)/shard_map/ppermute | solution.py:28
  189.2 3.3 %collective-permute-done.3 = f32[2,8,48,1]{3,2,1,0:T(8,128)S(1)} collective-permute-done((f32[2,8,48,1]{3,2,1,0:T(8,128)S(1)}, f32[2,8,48,1]{3,2,1,0:T(8,128)S(1)}, u32[]{:S(2)}, u32[]{:S(2)}) %collective-permute-start.3) | collective-permute-done | bytes 3104 | tf_op jit(solution)/shard_map/ppermute | solution.py:30
  196.2 4.1 %collective-permute-start.9 = (f32[3,8,1,384]{3,2,1,0:T(1,128)S(1)}, f32[3,8,1,384]{3,2,1,0:T(1,128)S(1)}, u32[]{:S(2)}, u32[]{:S(2)}) collective-permute-start(f32[3,8,1,384]{3,2,1,0:T(1,128)S(1)} %get-tuple-element.25), channel_id=1, source_target_pairs={{1,0},{2,1},{3,2},{4,3},{5,4},{6,5},{7,6},{0,7},{9,8},{10,9},{11,1... | collective-permute-start | bytes 110600 | tf_op jit(solution)/shard_map/ppermute | solution.py:30
  200.5 1.9 collective-permute-start.7
  202.4 4.9 %collective-permute-start.8 = (f32[2,8,48,1]{3,2,1,0:T(8,128)S(1)}, f32[2,8,48,1]{3,2,1,0:T(8,128)S(1)}, u32[]{:S(2)}, u32[]{:S(2)}) collective-permute-start(f32[2,8,48,1]{3,2,1,0:T(8,128)S(1)} %get-tuple-element.39), channel_id=1, source_target_pairs={{0,8},{8,16},{16,24},{1,9},{9,17},{17,25},{2,10},{10,18},{18,26},{... | collective-permute-start | bytes 9224 | tf_op jit(solution)/shard_map/ppermute | solution.py:28
  207.4 3.5 %collective-permute-done.7 = f32[2,8,48,1]{3,2,1,0:T(8,128)S(1)} collective-permute-done((f32[2,8,48,1]{3,2,1,0:T(8,128)S(1)}, f32[2,8,48,1]{3,2,1,0:T(8,128)S(1)}, u32[]{:S(2)}, u32[]{:S(2)}) %collective-permute-start.7) | collective-permute-done | bytes 3104 | tf_op jit(solution)/shard_map/ppermute | solution.py:30
  218.1 4.9 %collective-permute-start.12 = (f32[2,8,48,1]{3,2,1,0:T(8,128)S(1)}, f32[2,8,48,1]{3,2,1,0:T(8,128)S(1)}, u32[]{:S(2)}, u32[]{:S(2)}) collective-permute-start(f32[2,8,48,1]{3,2,1,0:T(8,128)S(1)} %get-tuple-element.37), channel_id=1, source_target_pairs={{0,8},{8,16},{16,24},{1,9},{9,17},{17,25},{2,10},{10,18},{18,26},{... | collective-permute-start | bytes 9224 | tf_op jit(solution)/shard_map/ppermute | solution.py:28
  223.1 3.5 %collective-permute-done.11 = f32[2,8,48,1]{3,2,1,0:T(8,128)S(1)} collective-permute-done((f32[2,8,48,1]{3,2,1,0:T(8,128)S(1)}, f32[2,8,48,1]{3,2,1,0:T(8,128)S(1)}, u32[]{:S(2)}, u32[]{:S(2)}) %collective-permute-start.11) | collective-permute-done | bytes 3104 | tf_op jit(solution)/shard_map/ppermute | solution.py:30
  230.2 2.5 %collective-permute-start.17 = (f32[3,8,1,384]{3,2,1,0:T(1,128)S(1)}, f32[3,8,1,384]{3,2,1,0:T(1,128)S(1)}, u32[]{:S(2)}, u32[]{:S(2)}) collective-permute-start(f32[3,8,1,384]{3,2,1,0:T(1,128)S(1)} %get-tuple-element.21), channel_id=1, source_target_pairs={{1,0},{2,1},{3,2},{4,3},{5,4},{6,5},{7,6},{0,7},{9,8},{10,9},{11,1... | collective-permute-start | bytes 110600 | tf_op jit(solution)/shard_map/ppermute | solution.py:30
  234.8 4.7 %collective-permute-start.16 = (f32[2,8,48,1]{3,2,1,0:T(8,128)S(1)}, f32[2,8,48,1]{3,2,1,0:T(8,128)S(1)}, u32[]{:S(2)}, u32[]{:S(2)}) collective-permute-start(f32[2,8,48,1]{3,2,1,0:T(8,128)S(1)} %get-tuple-element.35), channel_id=1, source_target_pairs={{0,8},{8,16},{16,24},{1,9},{9,17},{17,25},{2,10},{10,18},{18,26},{... | collective-permute-start | bytes 9224 | tf_op jit(solution)/shard_map/ppermute | solution.py:28
  239.5 3.5 %collective-permute-done.15 = f32[2,8,48,1]{3,2,1,0:T(8,128)S(1)} collective-permute-done((f32[2,8,48,1]{3,2,1,0:T(8,128)S(1)}, f32[2,8,48,1]{3,2,1,0:T(8,128)S(1)}, u32[]{:S(2)}, u32[]{:S(2)}) %collective-permute-start.15) | collective-permute-done | bytes 3104 | tf_op jit(solution)/shard_map/ppermute | solution.py:30
  245.6 2.4 multiply_subtract_fusion.2
  (102 shorter events, 32.6 us)
Async XLA Ops:
  26.6 10.5 %copy-start.12 = (s32[1,1,4,108]{3,2,1,0:T(4,128)S(1)}, s32[1,1,4,108]{3,2,1,0:T(4,128)}, u32[]{:S(2)}) copy-start(s32[1,1,4,108]{3,2,1,0:T(4,128)} %param.14) | copy-start | bytes 5188
  26.6 10.6 %copy-start.13 = (s32[2,4]{1,0:T(2,128)S(1)}, s32[2,4]{1,0:T(2,128)}, u32[]{:S(2)}) copy-start(s32[2,4]{1,0:T(2,128)} %param.15) | copy-start | bytes 100
  26.6 10.8 %copy-start.6 = (f32[4,48,384]{2,1,0:T(8,128)S(1)}, f32[4,48,384]{2,1,0:T(8,128)}, u32[]{:S(2)}) copy-start(f32[4,48,384]{2,1,0:T(8,128)} %param.16) | copy-start | bytes 884740
  26.6 10.8 %copy-start.11 = (f32[2,48,384]{2,1,0:T(8,128)S(1)}, f32[2,48,384]{2,1,0:T(8,128)}, u32[]{:S(2)}) copy-start(f32[2,48,384]{2,1,0:T(8,128)} %param.17) | copy-start | bytes 442372
  31.5 34.4 %collective-permute-start.1 = (f32[108,3072]{1,0:T(8,128)}, f32[108,3072]{1,0:T(8,128)}, u32[]{:S(2)}, u32[]{:S(2)}) collective-permute-start(f32[108,3072]{1,0:T(8,128)} %get-tuple-element.19), channel_id=1, source_target_pairs={{0,2},{1,3},{2,4},{3,5},{4,6},{5,7},{6,0},{7,1},{8,10},{9,11},{10,... | collective-permute-start | bytes 3981320 | tf_op jit(solution)/shard_map/ppermute | solution.py:17
  33.6 122.4 %collective-permute-start.2 = (f32[108,3072]{1,0:T(8,128)}, f32[108,3072]{1,0:T(8,128)}, u32[]{:S(2)}, u32[]{:S(2)}) collective-permute-start(f32[108,3072]{1,0:T(8,128)} %get-tuple-element.18), channel_id=1, source_target_pairs={{0,3},{1,4},{2,5},{3,6},{4,7},{5,0},{6,1},{7,2},{8,11},{9,12},{10,... | collective-permute-start | bytes 3981320 | tf_op jit(solution)/shard_map/ppermute | solution.py:17
  35.9 120.2 %collective-permute-start = (f32[108,3072]{1,0:T(8,128)S(1)}, f32[108,3072]{1,0:T(8,128)}, u32[]{:S(2)}, u32[]{:S(2)}) collective-permute-start(f32[108,3072]{1,0:T(8,128)S(1)} %get-tuple-element.20), channel_id=1, source_target_pairs={{0,1},{1,2},{2,3},{3,4},{4,5},{5,6},{6,7},{7,0},{8,9},{9,10},{10,1... | collective-permute-start | bytes 3981320 | tf_op jit(solution)/shard_map/ppermute | solution.py:17
  181.5 12.2 %collective-permute-start.5 = (f32[3,8,1,384]{3,2,1,0:T(1,128)S(1)}, f32[3,8,1,384]{3,2,1,0:T(1,128)S(1)}, u32[]{:S(2)}, u32[]{:S(2)}) collective-permute-start(f32[3,8,1,384]{3,2,1,0:T(1,128)S(1)} %get-tuple-element.27), channel_id=1, source_target_pairs={{1,0},{2,1},{3,2},{4,3},{5,4},{6,5},{7,6},{0,7},{9,8},{10,9},{11,1... | collective-permute-start | bytes 110600 | tf_op jit(solution)/shard_map/ppermute | solution.py:30
  181.5 12.2 %collective-permute-start.6 = (f32[3,8,1,384]{3,2,1,0:T(1,128)S(1)}, f32[3,8,1,384]{3,2,1,0:T(1,128)S(1)}, u32[]{:S(2)}, u32[]{:S(2)}) collective-permute-start(f32[3,8,1,384]{3,2,1,0:T(1,128)S(1)} %get-tuple-element.28), channel_id=1, source_target_pairs={{0,1},{1,2},{2,3},{3,4},{4,5},{5,6},{6,7},{7,0},{8,9},{9,10},{10,1... | collective-permute-start | bytes 110600 | tf_op jit(solution)/shard_map/ppermute | solution.py:28
  183.0 9.5 %collective-permute-start.3 = (f32[2,8,48,1]{3,2,1,0:T(8,128)S(1)}, f32[2,8,48,1]{3,2,1,0:T(8,128)S(1)}, u32[]{:S(2)}, u32[]{:S(2)}) collective-permute-start(f32[2,8,48,1]{3,2,1,0:T(8,128)S(1)} %get-tuple-element.40), channel_id=1, source_target_pairs={{8,0},{16,8},{24,16},{9,1},{17,9},{25,17},{10,2},{18,10},{26,18},{... | collective-permute-start | bytes 9224 | tf_op jit(solution)/shard_map/ppermute | solution.py:30
  185.9 7.8 %collective-permute-start.4 = (f32[2,8,48,1]{3,2,1,0:T(8,128)S(1)}, f32[2,8,48,1]{3,2,1,0:T(8,128)S(1)}, u32[]{:S(2)}, u32[]{:S(2)}) collective-permute-start(f32[2,8,48,1]{3,2,1,0:T(8,128)S(1)} %get-tuple-element.41), channel_id=1, source_target_pairs={{0,8},{8,16},{16,24},{1,9},{9,17},{17,25},{2,10},{10,18},{18,26},{... | collective-permute-start | bytes 9224 | tf_op jit(solution)/shard_map/ppermute | solution.py:28
  196.1 16.0 %collective-permute-start.10 = (f32[3,8,1,384]{3,2,1,0:T(1,128)S(1)}, f32[3,8,1,384]{3,2,1,0:T(1,128)S(1)}, u32[]{:S(2)}, u32[]{:S(2)}) collective-permute-start(f32[3,8,1,384]{3,2,1,0:T(1,128)S(1)} %get-tuple-element.26), channel_id=1, source_target_pairs={{0,1},{1,2},{2,3},{3,4},{4,5},{5,6},{6,7},{7,0},{8,9},{9,10},{10,1... | collective-permute-start | bytes 110600 | tf_op jit(solution)/shard_map/ppermute | solution.py:28
  196.2 15.9 %collective-permute-start.9 = (f32[3,8,1,384]{3,2,1,0:T(1,128)S(1)}, f32[3,8,1,384]{3,2,1,0:T(1,128)S(1)}, u32[]{:S(2)}, u32[]{:S(2)}) collective-permute-start(f32[3,8,1,384]{3,2,1,0:T(1,128)S(1)} %get-tuple-element.25), channel_id=1, source_target_pairs={{1,0},{2,1},{3,2},{4,3},{5,4},{6,5},{7,6},{0,7},{9,8},{10,9},{11,1... | collective-permute-start | bytes 110600 | tf_op jit(solution)/shard_map/ppermute | solution.py:30
  200.5 10.4 %collective-permute-start.7 = (f32[2,8,48,1]{3,2,1,0:T(8,128)S(1)}, f32[2,8,48,1]{3,2,1,0:T(8,128)S(1)}, u32[]{:S(2)}, u32[]{:S(2)}) collective-permute-start(f32[2,8,48,1]{3,2,1,0:T(8,128)S(1)} %get-tuple-element.38), channel_id=1, source_target_pairs={{8,0},{16,8},{24,16},{9,1},{17,9},{25,17},{10,2},{18,10},{26,18},{... | collective-permute-start | bytes 9224 | tf_op jit(solution)/shard_map/ppermute | solution.py:30
  202.4 9.7 %collective-permute-start.8 = (f32[2,8,48,1]{3,2,1,0:T(8,128)S(1)}, f32[2,8,48,1]{3,2,1,0:T(8,128)S(1)}, u32[]{:S(2)}, u32[]{:S(2)}) collective-permute-start(f32[2,8,48,1]{3,2,1,0:T(8,128)S(1)} %get-tuple-element.39), channel_id=1, source_target_pairs={{0,8},{8,16},{16,24},{1,9},{9,17},{17,25},{2,10},{10,18},{18,26},{... | collective-permute-start | bytes 9224 | tf_op jit(solution)/shard_map/ppermute | solution.py:28
  214.5 13.3 %collective-permute-start.13 = (f32[3,8,1,384]{3,2,1,0:T(1,128)S(1)}, f32[3,8,1,384]{3,2,1,0:T(1,128)S(1)}, u32[]{:S(2)}, u32[]{:S(2)}) collective-permute-start(f32[3,8,1,384]{3,2,1,0:T(1,128)S(1)} %get-tuple-element.23), channel_id=1, source_target_pairs={{1,0},{2,1},{3,2},{4,3},{5,4},{6,5},{7,6},{0,7},{9,8},{10,9},{11,1... | collective-permute-start | bytes 110600 | tf_op jit(solution)/shard_map/ppermute | solution.py:30
  214.6 13.2 %collective-permute-start.14 = (f32[3,8,1,384]{3,2,1,0:T(1,128)S(1)}, f32[3,8,1,384]{3,2,1,0:T(1,128)S(1)}, u32[]{:S(2)}, u32[]{:S(2)}) collective-permute-start(f32[3,8,1,384]{3,2,1,0:T(1,128)S(1)} %get-tuple-element.24), channel_id=1, source_target_pairs={{0,1},{1,2},{2,3},{3,4},{4,5},{5,6},{6,7},{7,0},{8,9},{9,10},{10,1... | collective-permute-start | bytes 110600 | tf_op jit(solution)/shard_map/ppermute | solution.py:28
  216.2 10.4 %collective-permute-start.11 = (f32[2,8,48,1]{3,2,1,0:T(8,128)S(1)}, f32[2,8,48,1]{3,2,1,0:T(8,128)S(1)}, u32[]{:S(2)}, u32[]{:S(2)}) collective-permute-start(f32[2,8,48,1]{3,2,1,0:T(8,128)S(1)} %get-tuple-element.36), channel_id=1, source_target_pairs={{8,0},{16,8},{24,16},{9,1},{17,9},{25,17},{10,2},{18,10},{26,18},{... | collective-permute-start | bytes 9224 | tf_op jit(solution)/shard_map/ppermute | solution.py:30
  218.1 9.7 %collective-permute-start.12 = (f32[2,8,48,1]{3,2,1,0:T(8,128)S(1)}, f32[2,8,48,1]{3,2,1,0:T(8,128)S(1)}, u32[]{:S(2)}, u32[]{:S(2)}) collective-permute-start(f32[2,8,48,1]{3,2,1,0:T(8,128)S(1)} %get-tuple-element.37), channel_id=1, source_target_pairs={{0,8},{8,16},{16,24},{1,9},{9,17},{17,25},{2,10},{10,18},{18,26},{... | collective-permute-start | bytes 9224 | tf_op jit(solution)/shard_map/ppermute | solution.py:28
  230.2 14.0 %collective-permute-start.17 = (f32[3,8,1,384]{3,2,1,0:T(1,128)S(1)}, f32[3,8,1,384]{3,2,1,0:T(1,128)S(1)}, u32[]{:S(2)}, u32[]{:S(2)}) collective-permute-start(f32[3,8,1,384]{3,2,1,0:T(1,128)S(1)} %get-tuple-element.21), channel_id=1, source_target_pairs={{1,0},{2,1},{3,2},{4,3},{5,4},{6,5},{7,6},{0,7},{9,8},{10,9},{11,1... | collective-permute-start | bytes 110600 | tf_op jit(solution)/shard_map/ppermute | solution.py:30
  232.7 11.5 %collective-permute-start.18 = (f32[3,8,1,384]{3,2,1,0:T(1,128)S(1)}, f32[3,8,1,384]{3,2,1,0:T(1,128)S(1)}, u32[]{:S(2)}, u32[]{:S(2)}) collective-permute-start(f32[3,8,1,384]{3,2,1,0:T(1,128)S(1)} %get-tuple-element.22), channel_id=1, source_target_pairs={{0,1},{1,2},{2,3},{3,4},{4,5},{5,6},{6,7},{7,0},{8,9},{9,10},{10,1... | collective-permute-start | bytes 110600 | tf_op jit(solution)/shard_map/ppermute | solution.py:28
  232.9 10.1 %collective-permute-start.15 = (f32[2,8,48,1]{3,2,1,0:T(8,128)S(1)}, f32[2,8,48,1]{3,2,1,0:T(8,128)S(1)}, u32[]{:S(2)}, u32[]{:S(2)}) collective-permute-start(f32[2,8,48,1]{3,2,1,0:T(8,128)S(1)} %get-tuple-element.34), channel_id=1, source_target_pairs={{8,0},{16,8},{24,16},{9,1},{17,9},{25,17},{10,2},{18,10},{26,18},{... | collective-permute-start | bytes 9224 | tf_op jit(solution)/shard_map/ppermute | solution.py:30
  234.8 9.4 %collective-permute-start.16 = (f32[2,8,48,1]{3,2,1,0:T(8,128)S(1)}, f32[2,8,48,1]{3,2,1,0:T(8,128)S(1)}, u32[]{:S(2)}, u32[]{:S(2)}) collective-permute-start(f32[2,8,48,1]{3,2,1,0:T(8,128)S(1)} %get-tuple-element.35), channel_id=1, source_target_pairs={{0,8},{8,16},{16,24},{1,9},{9,17},{17,25},{2,10},{10,18},{18,26},{... | collective-permute-start | bytes 9224 | tf_op jit(solution)/shard_map/ppermute | solution.py:28
  244.2 3.9 %copy-start.1 = (bf16[3,8,144,256]{3,2,1,0:T(8,128)(2,1)S(1)}, bf16[3,8,144,256]{3,2,1,0:T(8,128)(2,1)}, u32[]{:S(2)}) copy-start(bf16[3,8,144,256]{3,2,1,0:T(8,128)(2,1)} %param.11) | copy-start | bytes 5308420
  (9 other events, 20.4 us)
where the time goes:
time: 249 us; the launch traced here: 248 us
  waiting for transfers between devices  136 us (55%)
  starting transfers between devices  41.9 us (17%)
  other arithmetic  31.9 us (13%)
  local copies, waits for them, and re-layouts  26 us (10%)
  matrix products  10.7 us (4%)
    ppermute x3, waiting for transfers between devices, from_behind(): lax.ppermute(array, axis, [(i, (i + by) % size) for i in range(size)])  118 us
    ppermute x8, starting transfers between devices, padded(): lax.ppermute(tail, axis, [(i, (i + 1) % count) for i in range(ends)])  20.8 us
    ppermute x8, starting transfers between devices, padded(): lax.ppermute(head, axis, [((i + 1) % count, i) for i in range(ends)])  15.5 us
    ppermute x8, waiting for transfers between devices, padded(): lax.ppermute(head, axis, [((i + 1) % count, i) for i in range(ends)])  13.8 us
    dot_general x1, matrix products, body(): jnp.einsum('clsk,stpk->stclp', increments, remap_weights[0, 0], preferred...  10.7 us
    scatter-add x1, other arithmetic, body(): patches = jnp.zeros((patch_count, row_width), jnp.float32).at[slot_patch....  9.81 us
    sub x4, other arithmetic, advance(): depth - COURANT * (flux_right - flux_left + (flux_above - flux_below))  7.7 us
    scatter x1, local copies, waits for them, and re-layouts, body(): outgoing = jnp.zeros((owners * capacity, row_width), jnp.float32).at[posi...  6.67 us
  transfers between devices with their start and end apart: 19, of which 10 were waited for; matrix products, arithmetic and copies ran while one was open for 1% of the time, Pallas kernels for 0%

commit v1 on v0

v1 whole, which is shorter than its diff:
```python
import functools

import jax
import jax.numpy as jnp
from jax import lax
from jax.experimental import pallas as pl
from jax.experimental.pallas import tpu as pltpu
from jax.sharding import PartitionSpec as P

PANELS = 4
STEPS = 4
TPATCH = 128
HALO = 4
SUB = 8
FIELDS = 3
COURANT = 0.15
GRADIENT = 0.3
CHUNKS = (4, 4)
GROUP = 16
VMEM = 61 * 2**20

ROWS_BY_ROWS = (((1,), (1,)), ((), ()))


def params(limit=VMEM):
    return pltpu.CompilerParams(vmem_limit_bytes=limit)


def in_vmem(count):
    return [pl.BlockSpec(memory_space=pltpu.VMEM)] * count


def in_smem(count):
    return [pl.BlockSpec(memory_space=pltpu.SMEM)] * count


def in_hbm(count):
    return [pl.BlockSpec(memory_space=pl.ANY)] * count


def terms_kernel(bounds, group, offsets, increments, weights, *refs):
    parts = len(bounds) - 1
    fields, levels, rows, width = increments.shape
    count = fields * levels
    pieces, tops = weights.shape[1] // TPATCH, offsets.shape[3]
    outs = refs[: -9]
    owners = len(outs) // parts
    capacity = outs[0].shape[0] // (fields * (bounds[1] - bounds[0]))
    held, source, left, right, slots, used, source_sem, held_sem, out_sem = refs[-9:]
    groups = rows // group

    first = pltpu.make_async_copy(increments, source, source_sem)
    first.start()

    def fetch(g):
        piece = pl.ds(g * group, group)
        return pltpu.make_async_copy(weights.at[piece], held.at[piece], held_sem.at[g])

    @pl.loop(0, groups)
    def _(g):
        fetch(g).start()

    for o in range(owners):
        used[o] = 0
    slots[...] = jnp.zeros_like(slots)
    first.wait()
    half = width // 2
    for l in range(levels):
        for c in range(fields):
            at = pl.ds((l * fields + c) * rows, rows)
            left[at, :] = source[c, l, :, :half].astype(jnp.float32)
            right[at, :] = source[c, l, :, half:].astype(jnp.float32)

    @pl.loop(0, groups)
    def _(g):
        fetch(g).wait()
        for j in range(group):
            s = g * group + j
            at = pl.ds(s, count, stride=rows)
            block = jnp.concatenate([left[at, :], right[at, :]], axis=1).astype(jnp.bfloat16)
            term = lax.dot_general(block, held[s], ROWS_BY_ROWS, preferred_element_type=jnp.float32)
            for t in range(tops):
                o = offsets[0, 0, s, t]
                k = used[o]
                used[o] = k + 1
                slots[pl.ds(o * (count * capacity) + k, count, stride=capacity), :] = term[
                    :, t * TPATCH : (t + 1) * TPATCH
                ]

    copies = []
    for o in range(owners):
        for j in range(parts):
            size = fields * (bounds[j + 1] - bounds[j]) * capacity
            start = (o * count + fields * bounds[j]) * capacity
            copy = pltpu.make_async_copy(
                slots.at[pl.ds(start, size)], outs[o * parts + j], out_sem.at[o * parts + j]
            )
            copy.start()
            copies.append(copy)
    for copy in copies:
        copy.wait()


def terms(bounds, owners, capacity, offsets, increments, weights):
    parts = len(bounds) - 1
    fields, levels, rows, width = increments.shape
    count = fields * levels
    group = max(g for g in range(1, GROUP + 1) if rows % g == 0)
    out = pl.pallas_call(
        functools.partial(terms_kernel, bounds, group),
        in_specs=in_smem(1) + in_hbm(2),
        out_specs=in_hbm(owners * parts),
        out_shape=[
            jax.ShapeDtypeStruct((fields * (bounds[j + 1] - bounds[j]) * capacity, TPATCH), jnp.float32)
            for _ in range(owners)
            for j in range(parts)
        ],
        scratch_shapes=[
            pltpu.VMEM(weights.shape, jnp.bfloat16),
            pltpu.VMEM(increments.shape, jnp.bfloat16),
            pltpu.VMEM((count * rows, width // 2), jnp.float32),
            pltpu.VMEM((count * rows, width // 2), jnp.float32),
            pltpu.VMEM((owners * count * capacity, TPATCH), jnp.float32),
            pltpu.SMEM((owners,), jnp.int32),
            pltpu.SemaphoreType.DMA,
            pltpu.SemaphoreType.DMA((rows // group,)),
            pltpu.SemaphoreType.DMA((owners * parts,)),
        ],
        compiler_params=params(),
        name="terms",
    )(offsets, increments, weights)
    return [out[o * parts : (o + 1) * parts] for o in range(owners)]


def add_slots(total, slots, places, which, count, patches):
    capacity = slots.shape[0] // count

    def one(k, carry):
        at = pl.ds(places[which, k], count, stride=patches)
        total[at, :] = total[at, :] + slots[pl.ds(k, count, stride=capacity), :]
        return carry

    lax.fori_loop(0, capacity, one, 0, unroll=4)


def gather_kernel(which, whole, count, patches, places, *refs):
    total = refs[-1]
    if whole:
        total[...] = refs[0][...]
        for i in range(1, whole):
            total[...] += refs[i][...]
    else:
        total[...] = jnp.zeros_like(total)
    for row, slots in zip(which, refs[whole:-1]):
        add_slots(total, slots, places, row, count, patches)


def gathered(places, wholes, slot_arrays, which, count, patches):
    return pl.pallas_call(
        functools.partial(gather_kernel, which, len(wholes), count, patches),
        in_specs=in_smem(1) + in_vmem(len(wholes) + len(slot_arrays)),
        out_specs=in_vmem(1)[0],
        out_shape=jax.ShapeDtypeStruct((count * patches, TPATCH), jnp.float32),
        compiler_params=params(24 * 2**20),
        name="gather_patches",
    )(places, *wholes, *slot_arrays)


def fields_kernel(levels, patches, odd, places, last, across, direct, own, basis, thickness, wind_first, wind_second, *refs):
    depth, cov_first, cov_second, low_rows, high_rows, low_cols, high_cols, total = refs
    rows, cols = depth.shape[1:]
    blocks = cols // TPATCH
    count = FIELDS * levels
    total[...] = last[...]

    @pl.when(odd[0] == 1)
    def _():
        total[...] += across[...]
        add_slots(total, direct, places, 2, count, patches)

    add_slots(total, own, places, 0, count, patches)
    lane = lax.broadcasted_iota(jnp.int32, (rows, TPATCH), 1)
    low, high = jnp.zeros((rows, TPATCH), jnp.float32), jnp.zeros((rows, TPATCH), jnp.float32)
    for l in range(levels):
        for block in range(blocks):
            at = slice(block * TPATCH, (block + 1) * TPATCH)
            east, north, thick = (
                total[(l * FIELDS + c) * patches + block * rows : (l * FIELDS + c) * patches + (block + 1) * rows, :]
                for c in range(FIELDS)
            )
            values = (
                thickness[l, :, at] + thick,
                wind_first[l, :, at] + basis[0, :, at] * east + basis[1, :, at] * north,
                wind_second[l, :, at] + basis[2, :, at] * east + basis[3, :, at] * north,
            )
            for f, (ref, value) in enumerate(zip((depth, cov_first, cov_second), values)):
                ref[l, :, at] = value
                i = f * levels + l
                low_rows[i * HALO : (i + 1) * HALO, at] = value[:HALO]
                high_rows[i * HALO : (i + 1) * HALO, at] = value[rows - HALO :]
                here = (lane >= i * HALO) & (lane < (i + 1) * HALO)
                if block == 0:
                    low = jnp.where(here, pltpu.roll(value, i * HALO, 1), low)
                if block == blocks - 1:
                    high = jnp.where(here, pltpu.roll(value, (i + 1) * HALO, 1), high)
    low_cols[...] = low
    high_cols[...] = high


def first_fields(levels, patches, odd, places, last, across, direct, own, basis, thickness, wind_first, wind_second):
    rows, cols = thickness.shape[1:]
    count = FIELDS * levels
    whole = jax.ShapeDtypeStruct((levels, rows, cols), jnp.float32)
    ends = jax.ShapeDtypeStruct((count * HALO, cols), jnp.float32)
    sides = jax.ShapeDtypeStruct((rows, TPATCH), jnp.float32)
    return pl.pallas_call(
        functools.partial(fields_kernel, levels, patches),
        in_specs=in_smem(2) + in_vmem(8),
        out_specs=in_vmem(7),
        out_shape=[whole, whole, whole, ends, ends, sides, sides],
        scratch_shapes=[pltpu.VMEM((count * patches, TPATCH), jnp.float32)],
        compiler_params=params(32 * 2**20),
        name="first_fields",
    )(odd, places, last, across, direct, own, basis, thickness, wind_first, wind_second)


def steps_kernel(levels, metric, turns, wall, from_below, from_above, from_left, from_right, *refs):
    parts, outs = refs[:FIELDS], refs[-FIELDS:]
    rows, cols = parts[0].shape[1:]
    count = FIELDS * levels
    ext_rows, ext_cols = rows + SUB, cols + TPATCH

    def side(own, at):
        lanes = slice(at * TPATCH, (at + 1) * TPATCH)
        ends = [ref[count * HALO : (count + 1) * HALO, lanes] for ref in (from_above, from_below)]
        return jnp.concatenate([own[...]] + ends, axis=0)

    left, right = side(from_left, 0), side(from_right, 1)
    lane = lax.broadcasted_iota(jnp.int32, (ext_rows, TPATCH), 1)

    for l in range(levels):
        values = []
        for f in range(FIELDS):
            i = f * levels + l
            at = slice(i * HALO, (i + 1) * HALO)
            ends = jnp.concatenate([from_above[at, :], from_below[at, :]], axis=0)
            rim = jnp.where(
                lane < HALO,
                pltpu.roll(right, (TPATCH - i * HALO) % TPATCH, 1),
                jnp.where(lane >= TPATCH - HALO, pltpu.roll(left, (TPATCH - (i + 1) * HALO) % TPATCH, 1), 0.0),
            )
            values.append(
                jnp.concatenate([jnp.concatenate([parts[f][l], ends], axis=0), rim], axis=1)
            )
        depth, cov_first, cov_second = values
        cos_below, sin_below, cos_above, sin_above = (
            jnp.concatenate([turns[i]] * (ext_cols // TPATCH), axis=1) for i in range(4)
        )
        for _ in range(STEPS):
            con_first = metric[0] * cov_first + metric[2] * cov_second
            con_second = metric[2] * cov_first + metric[1] * cov_second
            before, after = functools.partial(pltpu.roll, shift=1), lambda v, axis: pltpu.roll(v, v.shape[axis] - 1, axis)
            depth_below, depth_above = before(depth, axis=0), after(depth, 0)
            second_below = sin_below * before(con_first, axis=0) + cos_below * before(con_second, axis=0)
            second_above = sin_above * after(con_first, 0) + cos_above * after(con_second, 0)
            face_below = 0.5 * (con_second + second_below)
            flux_below = jnp.maximum(face_below, 0.0) * depth_below + jnp.minimum(face_below, 0.0) * depth
            face_above = 0.5 * (con_second + second_above)
            flux_above = jnp.maximum(face_above, 0.0) * depth + jnp.minimum(face_above, 0.0) * depth_above
            depth_left, depth_right = before(depth, axis=1), after(depth, 1)
            face_left = 0.5 * (con_first + before(con_first, axis=1)) * wall[0:1, :]
            flux_left = jnp.maximum(face_left, 0.0) * depth_left + jnp.minimum(face_left, 0.0) * depth
            flux_right = after(flux_left, 1)
            depth = depth - COURANT * ((flux_right - flux_left) + (flux_above - flux_below))
            cov_first = cov_first - GRADIENT * 0.5 * (depth_right - depth_left)
            cov_second = cov_second - GRADIENT * 0.5 * (depth_above - depth_below)
        for ref, value in zip(outs, (depth, cov_first, cov_second)):
            ref[l] = value[:rows, :cols]


def steps(levels, metric, turns, wall, halos, parts):
    rows, cols = parts[0].shape[1:]
    return pl.pallas_call(
        functools.partial(steps_kernel, levels),
        in_specs=in_vmem(7 + FIELDS),
        out_specs=in_vmem(FIELDS),
        out_shape=[jax.ShapeDtypeStruct((levels, rows, cols), jnp.float32)] * FIELDS,
        compiler_params=params(32 * 2**20),
        name="steps",
    )(metric, turns, wall, *halos, *parts)


def quarter_turn(code):
    cosine = (code == 0).astype(jnp.float32) - (code == 2).astype(jnp.float32)
    sine_value = (code == 1).astype(jnp.float32) - (code == 3).astype(jnp.float32)
    return (cosine, sine_value)


def turn_factors(first_row, rows, total_rows, rotation):
    index = jnp.arange(rows + SUB, dtype=jnp.int32)
    index = jnp.where(index < rows + HALO, index, index - rows - SUB)
    row = (first_row + index) % total_rows
    panel_rows = total_rows // PANELS
    matches = jnp.arange(PANELS, dtype=jnp.int32)[None, :] == (row // panel_rows)[:, None]
    lower = jnp.sum(jnp.where(matches, rotation[0][None, :], 0), axis=1)
    upper = jnp.sum(jnp.where(matches, rotation[1][None, :], 0), axis=1)
    below = jnp.where(row % panel_rows == 0, lower, 0)
    above = jnp.where(row % panel_rows == panel_rows - 1, upper, 0)
    factors = jnp.stack(quarter_turn(below) + quarter_turn(above))
    return jnp.broadcast_to(factors[:, :, None], factors.shape + (TPATCH,))


def shift(array, axis, by, closed):
    size = lax.axis_size(axis)
    pairs = [(i, (i + by) % size) for i in range(size) if closed or 0 <= i + by < size]
    return lax.ppermute(array, axis, pairs)


def rimmed(array):
    rows, cols = array.shape[1:]
    below = shift(array[:, rows - HALO :], "ty", 1, True)
    above = shift(array[:, :HALO], "ty", -1, True)
    array = jnp.concatenate([array, above, below], axis=1)
    left = shift(array[:, :, cols - HALO :], "tx", 1, False)
    right = shift(array[:, :, :HALO], "tx", -1, False)
    gap = jnp.zeros(array.shape[:2] + (TPATCH - 2 * HALO,), array.dtype)
    return jnp.concatenate([array, right, gap, left], axis=2)


def body(
    increments,
    remap_weights,
    dest_offset,
    slot_patch,
    rotation,
    basis,
    inv_metric_diag,
    inv_metric_cross,
    thickness,
    wind_first,
    wind_second,
):
    levels, rows, cols = thickness.shape
    tx_count, ty_count = lax.axis_size("tx"), lax.axis_size("ty")
    tx_index, ty_index = lax.axis_index("tx"), lax.axis_index("ty")
    owners, capacity = slot_patch.shape[2:]
    blocks = cols // TPATCH
    patches = rows * blocks
    bounds = [0]
    while bounds[-1] < levels:
        bounds.append(min(levels, bounds[-1] + CHUNKS[len(bounds) - 1]))
    parts = len(bounds) - 1

    evens, odds = range(0, ty_count, 2), range(1, ty_count, 2)
    swap = [(b, b + 1) for b in evens] + [(b, b - 1) for b in odds]
    on_even = [(b, (b + 2) % ty_count) for b in evens]
    on_odd = [(b, (b + 2) % ty_count) for b in odds]
    send = lambda array, pairs: lax.ppermute(array, "ty", pairs)

    places = slot_patch[0, 0]
    places = (places % blocks) * rows + places // blocks
    places_next = shift(places, "ty", -1, True)
    places_second = shift(places, "ty", -2, True)
    odd = (ty_index % 2).reshape(1)

    metric = rimmed(jnp.concatenate([inv_metric_diag, inv_metric_cross[None]], axis=0))
    turns = turn_factors(ty_index * rows, rows, rows * ty_count, rotation)
    column = jnp.arange(cols + TPATCH, dtype=jnp.int32)
    column = tx_index * cols + jnp.where(column < cols + TPATCH // 2, column, column - cols - TPATCH)
    wall = jnp.where((column == 0) | (column == cols * tx_count), 0.0, 1.0).astype(jnp.float32)
    wall = jnp.broadcast_to(wall[None, :], (SUB, cols + TPATCH))

    slots = terms(
        bounds, owners, capacity, dest_offset, increments,
        remap_weights.reshape(increments.shape[2], -1, remap_weights.shape[-1]),
    )
    results = []
    for j in range(parts):
        size = bounds[j + 1] - bounds[j]
        count = FIELDS * size
        third = send(slots[3][j], on_even + on_odd)
        direct = send(slots[2][j], on_odd)
        paired = gathered(places_next, [], [third, slots[1][j]], (3, 1), count, patches)
        across = send(paired, swap)
        joined = gathered(places_second, [across], [slots[2][j]], (2,), count, patches)
        last = send(joined, on_even)
        *fields, low_rows, high_rows, low_cols, high_cols = first_fields(
            size, patches, odd, places, last, across, direct, slots[0][j], basis,
            *(a[bounds[j] : bounds[j + 1]] for a in (thickness, wind_first, wind_second)),
        )
        from_left = shift(high_cols, "tx", 1, False)
        from_right = shift(low_cols, "tx", -1, False)

        def with_corners(ends, at):
            corners = [a[at : at + HALO] for a in (from_left, from_right)]
            corners.append(jnp.zeros((HALO, cols - 2 * TPATCH), jnp.float32))
            return jnp.concatenate([ends, jnp.concatenate(corners, axis=1)], axis=0)

        from_below = shift(with_corners(high_rows, rows - HALO), "ty", 1, True)
        from_above = shift(with_corners(low_rows, 0), "ty", -1, True)
        results.append(
            steps(size, metric, turns, wall, (from_below, from_above, from_left, from_right), fields)
        )
    return tuple(jnp.concatenate(field, axis=0) for field in zip(*results))


def solution(mesh):
    in_specs = (
        P(None, None, "tx", "ty"),
        P("tx", "ty", None, None, None, None),
        P("tx", "ty", None, None),
        P("tx", "ty", None, None),
        P(),
        P(None, "ty", "tx"),
        P(None, "ty", "tx"),
        P("ty", "tx"),
        P(None, "ty", "tx"),
        P(None, "ty", "tx"),
        P(None, "ty", "tx"),
    )
    out_specs = (P(None, "ty", "tx"), P(None, "ty", "tx"), P(None, "ty", "tx"))
    return jax.shard_map(body, mesh=mesh, in_specs=in_specs, out_specs=out_specs, check_vma=False)
```

time: 249 us -> 152 us (0.61)
  waiting for transfers between devices: 136 us -> 40.9 us
  Pallas kernels: 0 us -> 37.5 us
  other arithmetic: 31.9 us -> 6.75 us
  local copies, waits for them, and re-layouts: 26 us -> 12.3 us
  starting transfers between devices: 41.9 us -> 52.8 us
  matrix products: 10.7 us -> 0 us
    ppermute x19 -> x22, waiting for transfers between devices: 136 us -> 40.9 us  [the longest x14 27.5 us: shift(): return lax.ppermute(array, axis, pairs)]
    pallas_call x0 -> x9, Pallas kernels: none -> 37.5 us  [the longest x1 13.1 us: terms(): pl.pallas_call(functools.partial(terms_kernel, bounds, group), in_specs=i...]
    ppermute x19 -> x22, starting transfers between devices: 41.9 us -> 52.8 us  [the longest x14 41 us: shift(): return lax.ppermute(array, axis, pairs)]
    dot_general x1 -> x0, matrix products: 10.7 us -> none  [body(): jnp.einsum('clsk,stpk->stclp', increments, remap_weights[0, 0], preferred...]
    scatter-add x1 -> x0, other arithmetic: 9.81 us -> none  [body(): patches = jnp.zeros((patch_count, row_width), jnp.float32).at[slot_patch....]
    reshape x3 -> x0, local copies, waits for them, and re-layouts: 9.32 us -> none  [the longest x1 4.8 us: body(): partial_terms = partial_terms.reshape(entries, row_width)]
    another operation x12 -> x1, other arithmetic: 9.9 us -> 0.69 us  [turn_factors(): factors = jnp.stack(quarter_turn(below) + quarter_turn(above))]
    sub x6 -> x1, other arithmetic: 9.16 us -> 0.62 us  [quarter_turn(): cosine = (code == 0).astype(jnp.float32) - (code == 2).astype(jnp.float32)]
  transfers between devices with their start and end apart: 19 -> 22, of which waited for: 10 -> 4; matrix products, arithmetic and copies ran while one was open for 1% -> 5% of each run, Pallas kernels for 0% -> 13%
where the time goes in v1:
time: 152 us; the launch traced here: 151 us
  starting transfers between devices  52.8 us (35%)
  waiting for transfers between devices  40.9 us (27%)
  Pallas kernels  37.5 us (25%)
  local copies, waits for them, and re-layouts  12.3 us (8%)
  other arithmetic  6.75 us (4%)
    ppermute x14, starting transfers between devices, shift(): return lax.ppermute(array, axis, pairs)  41 us
    ppermute x14, waiting for transfers between devices, shift(): return lax.ppermute(array, axis, pairs)  27.5 us
    ppermute x8, waiting for transfers between devices, body(): send = lambda array, pairs: lax.ppermute(array, 'ty', pairs)  13.4 us
    pallas_call x1, Pallas kernels, terms(): pl.pallas_call(functools.partial(terms_kernel, bounds, group), in_specs=i...  13.1 us
    ppermute x8, starting transfers between devices, body(): send = lambda array, pairs: lax.ppermute(array, 'ty', pairs)  11.8 us
    pallas_call x4, Pallas kernels, gathered(): pl.pallas_call(functools.partial(gather_kernel, which, len(wholes), count...  10.3 us
    pallas_call x2, Pallas kernels, steps(): pl.pallas_call(functools.partial(steps_kernel, levels), in_specs=in_vmem(...  9.1 us
    unnamed x25, local copies, waits for them, and re-layouts  8.99 us
  transfers between devices with their start and end apart: 22, of which 4 were waited for; matrix products, arithmetic and copies ran while one was open for 5% of the time, Pallas kernels for 13%

profile of v1, /device:TPU:1, one launch (start us, length us, event | category | flops | bytes accessed | tf_op | source)
XLA Modules:
  0.0 151.2 jit_solution(8987668013669853577)
XLA Ops:
  2.2 13.1 %terms.1 = (f32[1296,128]{1,0:T(8,128)}, f32[1296,128]{1,0:T(8,128)}, f32[1296,128]{1,0:T(8,128)}, f32[1296,128]{1,0:T(8,128)}, f32[1296,128]{1,0:T(8,128)}, /*i...) custom-call(s32[1,1,144,2]{3,2,1,0:T(8,128)} %copy.15.offsets, bf16[3,8,144,256]{3,2,1,0:T(8,128)(2,1)} %increments.1, ...), custom_call_target="tpu_custom_call" | custom-call | tf_op jit(solution)/shard_map/terms/pallas_call | solution.py:109
  15.3 2.2 %collective-permute-start.14 = (f32[1296,128]{1,0:T(8,128)}, f32[1296,128]{1,0:T(8,128)S(1)}, u32[]{:S(2)}, u32[]{:S(2)}) collective-permute-start(f32[1296,128]{1,0:T(8,128)} %get-tuple-element.43), channel_id=1, source_target_pairs={{0,2},{2,4},{4,6},{6,0},{1,3},{3,5},{5,7},{7,1},{8,10},{10,12},{12... | collective-permute-start | bytes 1990664 | tf_op jit(solution)/shard_map/ppermute | solution.py:358
  18.7 2.9 %collective-permute-start.5 = (s32[4,108]{1,0:T(4,128)S(1)}, s32[4,108]{1,0:T(4,128)S(1)}, u32[]{:S(2)}, u32[]{:S(2)}) collective-permute-start(s32[4,108]{1,0:T(4,128)S(1)} %fusion.5.places), channel_id=1, source_target_pairs={{0,7},{1,0},{2,1},{3,2},{4,3},{5,4},{6,5},{7,6},{8,15},{9,8},{10,9... | collective-permute-start | bytes 5192 | tf_op jit(solution)/shard_map/ppermute | solution.py:316
  21.7 23.9 %collective-permute-done.5.places = s32[4,108]{1,0:T(4,128)S(1)} collective-permute-done((s32[4,108]{1,0:T(4,128)S(1)}, s32[4,108]{1,0:T(4,128)S(1)}, u32[]{:S(2)}, u32[]{:S(2)}) %collective-permute-start.5) | collective-permute-done | bytes 1760 | tf_op jit(solution)/shard_map/ppermute | solution.py:316
  46.6 2.3 %gather_patches.6 = f32[1728,128]{1,0:T(8,128)S(1)} custom-call(s32[4,108]{1,0:T(4,128)S(1)} %collective-permute-done.5.places, f32[1296,128]{1,0:T(8,128)S(1)} %collective-permute-done.14.refs_0_, f32[1296,128]{1,0:T(8,128)S(1)} %copy-done.3), custom_call_target="tpu_custom_call" | custom-call | tf_op jit(solution)/shard_map/gather_patches/pallas_call | solution.py:159
  50.1 3.2 %gather_patches.4 = f32[1728,128]{1,0:T(8,128)} custom-call(s32[4,108]{1,0:T(4,128)S(1)} %collective-permute-done.5.places, f32[1296,128]{1,0:T(8,128)S(1)} %collective-permute-done.6.refs_0_, f32[1296,128]{1,0:T(8,128)S(1)} %copy-done.2), custom_call_target="tpu_custom_call" | custom-call | tf_op jit(solution)/shard_map/gather_patches/pallas_call | solution.py:159
  54.8 3.4 %collective-permute-start.4 = (s32[4,108]{1,0:T(4,128)S(1)}, s32[4,108]{1,0:T(4,128)S(1)}, u32[]{:S(2)}, u32[]{:S(2)}) collective-permute-start(s32[4,108]{1,0:T(4,128)S(1)} %fusion.5.places), channel_id=1, source_target_pairs={{0,6},{1,7},{2,0},{3,1},{4,2},{5,3},{6,4},{7,5},{8,14},{9,15},{10,... | collective-permute-start | bytes 5192 | tf_op jit(solution)/shard_map/ppermute | solution.py:316
  63.6 5.3 %collective-permute-start = (f32[3,4,384]{2,1,0:T(4,128)}, f32[3,4,384]{2,1,0:T(4,128)}, u32[]{:S(2)}, u32[]{:S(2)}) collective-permute-start(f32[3,4,384]{2,1,0:T(4,128)} %get-tuple-element.69), channel_id=1, source_target_pairs={{0,7},{1,0},{2,1},{3,2},{4,3},{5,4},{6,5},{7,6},{8,15},{9,8},{10,9... | collective-permute-start | bytes 55304 | tf_op jit(solution)/shard_map/ppermute | solution.py:316
  70.0 2.4 %gather_patches.7 = f32[1728,128]{1,0:T(8,128)} custom-call(s32[4,108]{1,0:T(4,128)S(1)} %collective-permute-done.4.places, f32[1728,128]{1,0:T(8,128)S(1)} %collective-permute-done.15.refs_0_.across, f32[1296,128]{1,0:T(8,128)S(1)} %copy-done.5), custom_call_target="tpu_custom_call" | custom-call | tf_op jit(solution)/shard_map/gather_patches/pallas_call | solution.py:159
  74.3 13.4 %collective-permute-done.7.refs_0_.across = f32[1728,128]{1,0:T(8,128)S(1)} collective-permute-done((f32[1728,128]{1,0:T(8,128)}, f32[1728,128]{1,0:T(8,128)S(1)}, u32[]{:S(2)}, u32[]{:S(2)}) %collective-permute-start.7) | collective-permute-done | bytes 884768 | tf_op jit(solution)/shard_map/ppermute | solution.py:358
  88.8 2.4 %gather_patches.5 = f32[1728,128]{1,0:T(8,128)} custom-call(s32[4,108]{1,0:T(4,128)S(1)} %collective-permute-done.4.places, f32[1728,128]{1,0:T(8,128)S(1)} %collective-permute-done.7.refs_0_.across, f32[1296,128]{1,0:T(8,128)S(1)} %copy-done.4), custom_call_target="tpu_custom_call" | custom-call | tf_op jit(solution)/shard_map/gather_patches/pallas_call | solution.py:159
  98.3 2.5 %first_fields.3 = (f32[4,48,384]{2,1,0:T(8,128)S(1)}, f32[4,48,384]{2,1,0:T(8,128)S(1)}, f32[4,48,384]{2,1,0:T(8,128)S(1)}, f32[48,384]{1,0:T(8,128)S(1)}, f32[4...) custom-call(s32[1]{0:T(128)} %bitcast.5.odd, s32[4,108]{1,0:T(4,128)S(1)} %fusion.5.places, ...), custom_call_target="tpu_custom_call" | custom-call | tf_op jit(solution)/shard_map/first_fields/pallas_call | solution.py:216
  100.8 5.4 %collective-permute-start.18 = (f32[48,128]{1,0:T(8,128)S(1)}, f32[48,128]{1,0:T(8,128)S(1)}, u32[]{:S(2)}, u32[]{:S(2)}) collective-permute-start(f32[48,128]{1,0:T(8,128)S(1)} %get-tuple-element.48), channel_id=1, source_target_pairs={{0,8},{8,16},{16,24},{1,9},{9,17},{17,25},{2,10},{10,18},{18,26},{... | collective-permute-start | bytes 73736 | tf_op jit(solution)/shard_map/ppermute | solution.py:316
  107.2 1.9 %collective-permute-start.2 = (f32[3,56,4]{2,1,0:T(8,128)S(1)}, f32[3,56,4]{2,1,0:T(8,128)S(1)}, u32[]{:S(2)}, u32[]{:S(2)}) collective-permute-start(f32[3,56,4]{2,1,0:T(8,128)S(1)} %get-tuple-element.67), channel_id=1, source_target_pairs={{8,0},{16,8},{24,16},{9,1},{17,9},{25,17},{10,2},{18,10},{26,18},{... | collective-permute-start | bytes 8072 | tf_op jit(solution)/shard_map/ppermute | solution.py:316
  109.2 3.6 %collective-permute-start.3 = (f32[3,56,4]{2,1,0:T(8,128)S(1)}, f32[3,56,4]{2,1,0:T(8,128)S(1)}, u32[]{:S(2)}, u32[]{:S(2)}) collective-permute-start(f32[3,56,4]{2,1,0:T(8,128)S(1)} %get-tuple-element.68), channel_id=1, source_target_pairs={{0,8},{8,16},{16,24},{1,9},{9,17},{17,25},{2,10},{10,18},{18,26},{... | collective-permute-start | bytes 8072 | tf_op jit(solution)/shard_map/ppermute | solution.py:316
  112.8 1.9 %collective-permute-start.19 = (f32[48,128]{1,0:T(8,128)S(1)}, f32[48,128]{1,0:T(8,128)S(1)}, u32[]{:S(2)}, u32[]{:S(2)}) collective-permute-start(f32[48,128]{1,0:T(8,128)S(1)} %get-tuple-element.49), channel_id=1, source_target_pairs={{8,0},{16,8},{24,16},{9,1},{17,9},{25,17},{10,2},{18,10},{26,18},{... | collective-permute-start | bytes 73736 | tf_op jit(solution)/shard_map/ppermute | solution.py:316
  115.9 2.5 %first_fields.2 = (f32[4,48,384]{2,1,0:T(8,128)S(1)}, f32[4,48,384]{2,1,0:T(8,128)S(1)}, f32[4,48,384]{2,1,0:T(8,128)S(1)}, f32[48,384]{1,0:T(8,128)S(1)}, f32[4...) custom-call(s32[1]{0:T(128)} %bitcast.5.odd, s32[4,108]{1,0:T(4,128)S(1)} %fusion.5.places, ...), custom_call_target="tpu_custom_call" | custom-call | tf_op jit(solution)/shard_map/first_fields/pallas_call | solution.py:216
  118.4 5.6 %collective-permute-start.10 = (f32[48,128]{1,0:T(8,128)S(1)}, f32[48,128]{1,0:T(8,128)S(1)}, u32[]{:S(2)}, u32[]{:S(2)}) collective-permute-start(f32[48,128]{1,0:T(8,128)S(1)} %get-tuple-element.36), channel_id=1, source_target_pairs={{0,8},{8,16},{16,24},{1,9},{9,17},{17,25},{2,10},{10,18},{18,26},{... | collective-permute-start | bytes 73736 | tf_op jit(solution)/shard_map/ppermute | solution.py:316
  124.0 1.9 %collective-permute-start.11 = (f32[48,128]{1,0:T(8,128)S(1)}, f32[48,128]{1,0:T(8,128)S(1)}, u32[]{:S(2)}, u32[]{:S(2)}) collective-permute-start(f32[48,128]{1,0:T(8,128)S(1)} %get-tuple-element.37), channel_id=1, source_target_pairs={{8,0},{16,8},{24,16},{9,1},{17,9},{25,17},{10,2},{18,10},{26,18},{... | collective-permute-start | bytes 73736 | tf_op jit(solution)/shard_map/ppermute | solution.py:316
  126.0 3.2 %collective-permute-done.11.from_right = f32[48,128]{1,0:T(8,128)S(1)} collective-permute-done((f32[48,128]{1,0:T(8,128)S(1)}, f32[48,128]{1,0:T(8,128)S(1)}, u32[]{:S(2)}, u32[]{:S(2)}) %collective-permute-start.11) | collective-permute-done | bytes 24608 | tf_op jit(solution)/shard_map/ppermute | solution.py:316
  129.2 4.4 %collective-permute-start.12 = (f32[52,384]{1,0:T(8,128)S(1)}, f32[52,384]{1,0:T(8,128)S(1)}, u32[]{:S(2)}, u32[]{:S(2)}) collective-permute-start(f32[52,384]{1,0:T(8,128)S(1)} %get-tuple-element.82), channel_id=1, source_target_pairs={{0,1},{1,2},{2,3},{3,4},{4,5},{5,6},{6,7},{7,0},{8,9},{9,10},{10,1... | collective-permute-start | bytes 239624 | tf_op jit(solution)/shard_map/ppermute | solution.py:316
  135.1 2.7 %collective-permute-start.21 = (f32[52,384]{1,0:T(8,128)S(1)}, f32[52,384]{1,0:T(8,128)S(1)}, u32[]{:S(2)}, u32[]{:S(2)}) collective-permute-start(f32[52,384]{1,0:T(8,128)S(1)} %get-tuple-element.81), channel_id=1, source_target_pairs={{0,7},{1,0},{2,1},{3,2},{4,3},{5,4},{6,5},{7,6},{8,15},{9,8},{10,9... | collective-permute-start | bytes 239624 | tf_op jit(solution)/shard_map/ppermute | solution.py:316
  139.5 4.6 %steps.2 = (f32[4,48,384]{2,1,0:T(8,128)S(1)}, f32[4,48,384]{2,1,0:T(8,128)S(1)}, f32[4,48,384]{2,1,0:T(8,128)S(1)}) custom-call(f32[3,56,512]{2,1,0:T(8,128)S(1)} %pad_maximum_fusion.3.metric, f32[4,56,128]{2,1,0:T(8,128)S(1)} %broadcast_in_dim.60.turns, f32[8,512]{1,0:T(8,128)S(1)} %broadcast_in_dim.63.wall, ...), custom_call_target="tpu_custom_call" | custom-call | tf_op jit(solution)/shard_map/steps/pallas_call | solution.py:283
  144.0 4.6 %steps.3 = (f32[4,48,384]{2,1,0:T(8,128)S(1)}, f32[4,48,384]{2,1,0:T(8,128)S(1)}, f32[4,48,384]{2,1,0:T(8,128)S(1)}) custom-call(f32[3,56,512]{2,1,0:T(8,128)S(1)} %pad_maximum_fusion.3.metric, f32[4,56,128]{2,1,0:T(8,128)S(1)} %broadcast_in_dim.60.turns, f32[8,512]{1,0:T(8,128)S(1)} %broadcast_in_dim.63.wall, ...), custom_call_target="tpu_custom_call" | custom-call | tf_op jit(solution)/shard_map/steps/pallas_call | solution.py:283
  (79 shorter events, 31.1 us)
Async XLA Ops:
  0.7 62.3 %copy-start.9 = (f32[48,384]{1,0:T(8,128)S(1)}, f32[48,384]{1,0:T(8,128)}, u32[]{:S(2)}) copy-start(f32[48,384]{1,0:T(8,128)} %param.18) | copy-start | bytes 221188
  0.7 95.6 %copy-start = (f32[4,48,384]{2,1,0:T(8,128)S(1)}, f32[4,48,384]{2,1,0:T(8,128)}, u32[]{:S(2)}) copy-start(f32[4,48,384]{2,1,0:T(8,128)} %basis.3) | copy-start | bytes 884740
  15.3 30.3 %collective-permute-start.14 = (f32[1296,128]{1,0:T(8,128)}, f32[1296,128]{1,0:T(8,128)S(1)}, u32[]{:S(2)}, u32[]{:S(2)}) collective-permute-start(f32[1296,128]{1,0:T(8,128)} %get-tuple-element.43), channel_id=1, source_target_pairs={{0,2},{2,4},{4,6},{6,0},{1,3},{3,5},{5,7},{7,1},{8,10},{10,12},{12... | collective-permute-start | bytes 1990664 | tf_op jit(solution)/shard_map/ppermute | solution.py:358
  17.4 31.6 %collective-permute-start.6 = (f32[1296,128]{1,0:T(8,128)}, f32[1296,128]{1,0:T(8,128)S(1)}, u32[]{:S(2)}, u32[]{:S(2)}) collective-permute-start(f32[1296,128]{1,0:T(8,128)} %get-tuple-element.31), channel_id=1, source_target_pairs={{0,2},{2,4},{4,6},{6,0},{1,3},{3,5},{5,7},{7,1},{8,10},{10,12},{12... | collective-permute-start | bytes 1990664 | tf_op jit(solution)/shard_map/ppermute | solution.py:358
  18.7 26.8 %collective-permute-start.5 = (s32[4,108]{1,0:T(4,128)S(1)}, s32[4,108]{1,0:T(4,128)S(1)}, u32[]{:S(2)}, u32[]{:S(2)}) collective-permute-start(s32[4,108]{1,0:T(4,128)S(1)} %fusion.5.places), channel_id=1, source_target_pairs={{0,7},{1,0},{2,1},{3,2},{4,3},{5,4},{6,5},{7,6},{8,15},{9,8},{10,9... | collective-permute-start | bytes 5192 | tf_op jit(solution)/shard_map/ppermute | solution.py:316
  48.9 19.9 %collective-permute-start.15 = (f32[1728,128]{1,0:T(8,128)S(1)}, f32[1728,128]{1,0:T(8,128)S(1)}, u32[]{:S(2)}, u32[]{:S(2)}) collective-permute-start(f32[1728,128]{1,0:T(8,128)S(1)} %gather_patches.6), channel_id=1, source_target_pairs={{0,1},{2,3},{4,5},{6,7},{1,0},{3,2},{5,4},{7,6},{8,9},{10,11},{12,... | collective-permute-start | bytes 2654216 | tf_op jit(solution)/shard_map/ppermute | solution.py:358
  53.3 34.3 %collective-permute-start.7 = (f32[1728,128]{1,0:T(8,128)}, f32[1728,128]{1,0:T(8,128)S(1)}, u32[]{:S(2)}, u32[]{:S(2)}) collective-permute-start(f32[1728,128]{1,0:T(8,128)} %gather_patches.4), channel_id=1, source_target_pairs={{0,1},{2,3},{4,5},{6,7},{1,0},{3,2},{5,4},{7,6},{8,9},{10,11},{12,... | collective-permute-start | bytes 2654216 | tf_op jit(solution)/shard_map/ppermute | solution.py:358
  54.8 8.8 %collective-permute-start.4 = (s32[4,108]{1,0:T(4,128)S(1)}, s32[4,108]{1,0:T(4,128)S(1)}, u32[]{:S(2)}, u32[]{:S(2)}) collective-permute-start(s32[4,108]{1,0:T(4,128)S(1)} %fusion.5.places), channel_id=1, source_target_pairs={{0,6},{1,7},{2,0},{3,1},{4,2},{5,3},{6,4},{7,5},{8,14},{9,15},{10,... | collective-permute-start | bytes 5192 | tf_op jit(solution)/shard_map/ppermute | solution.py:316
  58.2 36.9 %collective-permute-start.17 = (f32[1296,128]{1,0:T(8,128)}, f32[1296,128]{1,0:T(8,128)}, u32[]{:S(2)}, u32[]{:S(2)}) collective-permute-start(f32[1296,128]{1,0:T(8,128)} %get-tuple-element.45.refs_1_), channel_id=1, source_target_pairs={{1,3},{3,5},{5,7},{7,1},{9,11},{11,13},{13,15},{15,9},{17,19},{19,... | collective-permute-start | bytes 1990664 | tf_op jit(solution)/shard_map/ppermute | solution.py:358
  59.7 53.2 %collective-permute-start.9 = (f32[1296,128]{1,0:T(8,128)}, f32[1296,128]{1,0:T(8,128)}, u32[]{:S(2)}, u32[]{:S(2)}) collective-permute-start(f32[1296,128]{1,0:T(8,128)} %get-tuple-element.33.refs_1_), channel_id=1, source_target_pairs={{1,3},{3,5},{5,7},{7,1},{9,11},{11,13},{13,15},{15,9},{17,19},{19,... | collective-permute-start | bytes 1990664 | tf_op jit(solution)/shard_map/ppermute | solution.py:358
  63.6 42.6 %collective-permute-start = (f32[3,4,384]{2,1,0:T(4,128)}, f32[3,4,384]{2,1,0:T(4,128)}, u32[]{:S(2)}, u32[]{:S(2)}) collective-permute-start(f32[3,4,384]{2,1,0:T(4,128)} %get-tuple-element.69), channel_id=1, source_target_pairs={{0,7},{1,0},{2,1},{3,2},{4,3},{5,4},{6,5},{7,6},{8,15},{9,8},{10,9... | collective-permute-start | bytes 55304 | tf_op jit(solution)/shard_map/ppermute | solution.py:316
  72.4 23.9 %collective-permute-start.16 = (f32[1728,128]{1,0:T(8,128)}, f32[1728,128]{1,0:T(8,128)}, u32[]{:S(2)}, u32[]{:S(2)}) collective-permute-start(f32[1728,128]{1,0:T(8,128)} %gather_patches.7), channel_id=1, source_target_pairs={{0,2},{2,4},{4,6},{6,0},{8,10},{10,12},{12,14},{14,8},{16,18},{18,... | collective-permute-start | bytes 2654216 | tf_op jit(solution)/shard_map/ppermute | solution.py:358
  91.1 23.6 %collective-permute-start.8 = (f32[1728,128]{1,0:T(8,128)}, f32[1728,128]{1,0:T(8,128)}, u32[]{:S(2)}, u32[]{:S(2)}) collective-permute-start(f32[1728,128]{1,0:T(8,128)} %gather_patches.5), channel_id=1, source_target_pairs={{0,2},{2,4},{4,6},{6,0},{8,10},{10,12},{12,14},{14,8},{16,18},{18,... | collective-permute-start | bytes 2654216 | tf_op jit(solution)/shard_map/ppermute | solution.py:358
  95.1 11.1 %collective-permute-start.1 = (f32[3,4,384]{2,1,0:T(4,128)}, f32[3,4,384]{2,1,0:T(4,128)}, u32[]{:S(2)}, u32[]{:S(2)}) collective-permute-start(f32[3,4,384]{2,1,0:T(4,128)} %get-tuple-element.70), channel_id=1, source_target_pairs={{0,1},{1,2},{2,3},{3,4},{4,5},{5,6},{6,7},{7,0},{8,9},{9,10},{10,1... | collective-permute-start | bytes 55304 | tf_op jit(solution)/shard_map/ppermute | solution.py:316
  100.8 23.2 %collective-permute-start.18 = (f32[48,128]{1,0:T(8,128)S(1)}, f32[48,128]{1,0:T(8,128)S(1)}, u32[]{:S(2)}, u32[]{:S(2)}) collective-permute-start(f32[48,128]{1,0:T(8,128)S(1)} %get-tuple-element.48), channel_id=1, source_target_pairs={{0,8},{8,16},{16,24},{1,9},{9,17},{17,25},{2,10},{10,18},{18,26},{... | collective-permute-start | bytes 73736 | tf_op jit(solution)/shard_map/ppermute | solution.py:316
  107.2 27.8 %collective-permute-start.2 = (f32[3,56,4]{2,1,0:T(8,128)S(1)}, f32[3,56,4]{2,1,0:T(8,128)S(1)}, u32[]{:S(2)}, u32[]{:S(2)}) collective-permute-start(f32[3,56,4]{2,1,0:T(8,128)S(1)} %get-tuple-element.67), channel_id=1, source_target_pairs={{8,0},{16,8},{24,16},{9,1},{17,9},{25,17},{10,2},{18,10},{26,18},{... | collective-permute-start | bytes 8072 | tf_op jit(solution)/shard_map/ppermute | solution.py:316
  109.2 28.6 %collective-permute-start.3 = (f32[3,56,4]{2,1,0:T(8,128)S(1)}, f32[3,56,4]{2,1,0:T(8,128)S(1)}, u32[]{:S(2)}, u32[]{:S(2)}) collective-permute-start(f32[3,56,4]{2,1,0:T(8,128)S(1)} %get-tuple-element.68), channel_id=1, source_target_pairs={{0,8},{8,16},{16,24},{1,9},{9,17},{17,25},{2,10},{10,18},{18,26},{... | collective-permute-start | bytes 8072 | tf_op jit(solution)/shard_map/ppermute | solution.py:316
  112.8 13.1 %collective-permute-start.19 = (f32[48,128]{1,0:T(8,128)S(1)}, f32[48,128]{1,0:T(8,128)S(1)}, u32[]{:S(2)}, u32[]{:S(2)}) collective-permute-start(f32[48,128]{1,0:T(8,128)S(1)} %get-tuple-element.49), channel_id=1, source_target_pairs={{8,0},{16,8},{24,16},{9,1},{17,9},{25,17},{10,2},{18,10},{26,18},{... | collective-permute-start | bytes 73736 | tf_op jit(solution)/shard_map/ppermute | solution.py:316
  118.4 7.6 %collective-permute-start.10 = (f32[48,128]{1,0:T(8,128)S(1)}, f32[48,128]{1,0:T(8,128)S(1)}, u32[]{:S(2)}, u32[]{:S(2)}) collective-permute-start(f32[48,128]{1,0:T(8,128)S(1)} %get-tuple-element.36), channel_id=1, source_target_pairs={{0,8},{8,16},{16,24},{1,9},{9,17},{17,25},{2,10},{10,18},{18,26},{... | collective-permute-start | bytes 73736 | tf_op jit(solution)/shard_map/ppermute | solution.py:316
  124.0 5.1 %collective-permute-start.11 = (f32[48,128]{1,0:T(8,128)S(1)}, f32[48,128]{1,0:T(8,128)S(1)}, u32[]{:S(2)}, u32[]{:S(2)}) collective-permute-start(f32[48,128]{1,0:T(8,128)S(1)} %get-tuple-element.37), channel_id=1, source_target_pairs={{8,0},{16,8},{24,16},{9,1},{17,9},{25,17},{10,2},{18,10},{26,18},{... | collective-permute-start | bytes 73736 | tf_op jit(solution)/shard_map/ppermute | solution.py:316
  129.2 9.7 %collective-permute-start.12 = (f32[52,384]{1,0:T(8,128)S(1)}, f32[52,384]{1,0:T(8,128)S(1)}, u32[]{:S(2)}, u32[]{:S(2)}) collective-permute-start(f32[52,384]{1,0:T(8,128)S(1)} %get-tuple-element.82), channel_id=1, source_target_pairs={{0,1},{1,2},{2,3},{3,4},{4,5},{5,6},{6,7},{7,0},{8,9},{9,10},{10,1... | collective-permute-start | bytes 239624 | tf_op jit(solution)/shard_map/ppermute | solution.py:316
  133.6 5.8 %collective-permute-start.13 = (f32[52,384]{1,0:T(8,128)S(1)}, f32[52,384]{1,0:T(8,128)S(1)}, u32[]{:S(2)}, u32[]{:S(2)}) collective-permute-start(f32[52,384]{1,0:T(8,128)S(1)} %get-tuple-element.79), channel_id=1, source_target_pairs={{0,7},{1,0},{2,1},{3,2},{4,3},{5,4},{6,5},{7,6},{8,15},{9,8},{10,9... | collective-permute-start | bytes 239624 | tf_op jit(solution)/shard_map/ppermute | solution.py:316
  133.6 10.4 %collective-permute-start.20 = (f32[52,384]{1,0:T(8,128)S(1)}, f32[52,384]{1,0:T(8,128)S(1)}, u32[]{:S(2)}, u32[]{:S(2)}) collective-permute-start(f32[52,384]{1,0:T(8,128)S(1)} %get-tuple-element.80), channel_id=1, source_target_pairs={{0,1},{1,2},{2,3},{3,4},{4,5},{5,6},{6,7},{7,0},{8,9},{9,10},{10,1... | collective-permute-start | bytes 239624 | tf_op jit(solution)/shard_map/ppermute | solution.py:316
  135.1 9.0 %collective-permute-start.21 = (f32[52,384]{1,0:T(8,128)S(1)}, f32[52,384]{1,0:T(8,128)S(1)}, u32[]{:S(2)}, u32[]{:S(2)}) collective-permute-start(f32[52,384]{1,0:T(8,128)S(1)} %get-tuple-element.81), channel_id=1, source_target_pairs={{0,7},{1,0},{2,1},{3,2},{4,3},{5,4},{6,5},{7,6},{8,15},{9,8},{10,9... | collective-permute-start | bytes 239624 | tf_op jit(solution)/shard_map/ppermute | solution.py:316
  (10 other events, 148.5 us)

commit v2 on v1

v2 whole, which is shorter than its diff:
```python
import functools

import jax
import jax.numpy as jnp
from jax import lax
from jax.experimental import pallas as pl
from jax.experimental.pallas import tpu as pltpu
from jax.sharding import PartitionSpec as P

PANELS = 4
STEPS = 4
TPATCH = 128
HALO = 4
SUB = 8
FIELDS = 3
COURANT = 0.15
GRADIENT = 0.3
CHUNKS = (2, 2, 2, 2)
PAIRS = ((0,), (1,), (2,), (3,))
GROUPS = ((0, 1, 2, 3),)
ORDER = "P0 P1 P2 J0 P3 J1 J2 S0 F0 J3 S1 F1 S2 F2 S3 F3 H0"
GROUP = 16
VMEM = 61 * 2**20

ROWS_BY_ROWS = (((1,), (1,)), ((), ()))


def params(limit=VMEM):
    return pltpu.CompilerParams(vmem_limit_bytes=limit)


def in_vmem(count):
    return [pl.BlockSpec(memory_space=pltpu.VMEM)] * count


def in_smem(count):
    return [pl.BlockSpec(memory_space=pltpu.SMEM)] * count


def in_hbm(count):
    return [pl.BlockSpec(memory_space=pl.ANY)] * count


def spread(source, left, right):
    fields, levels, rows, width = source.shape
    half = width // 2
    for l in range(levels):
        for c in range(fields):
            at = pl.ds((l * fields + c) * rows, rows)
            left[at, :] = source[c, l, :, :half].astype(jnp.float32)
            right[at, :] = source[c, l, :, half:].astype(jnp.float32)


def row_block(left, right, s, count):
    at = pl.ds(s, count, stride=left.shape[0] // count)
    return jnp.concatenate([left[at, :], right[at, :]], axis=1).astype(jnp.bfloat16)


def write_out(cuts, fields, capacity, slots, outs, sems):
    count, copies = fields * cuts[0][-1], []
    starts = [(o * count + fields * first) * capacity for o, cut in enumerate(cuts) for first in cut[:-1]]
    for i, (start, out) in enumerate(zip(starts, outs)):
        copies.append(pltpu.make_async_copy(slots.at[pl.ds(start, out.shape[0])], out, sems.at[i]))
        copies[-1].start()
    for copy in copies:
        copy.wait()


def terms_kernel(cuts, group, capacity, offsets, increments, weights, *refs):
    fields, levels, rows, _ = increments.shape
    count, tops = fields * levels, offsets.shape[0]
    outs = refs[:-9]
    held, source, left, right, slots, used, source_sem, held_sem, out_sem = refs[-9:]
    groups = rows // group
    first = pltpu.make_async_copy(increments, source, source_sem)
    first.start()

    def fetch(g):
        piece = pl.ds(g * group, group)
        return pltpu.make_async_copy(weights.at[piece], held.at[piece], held_sem.at[g])

    @pl.loop(0, groups)
    def _(g):
        fetch(g).start()

    for o in range(len(cuts)):
        used[o] = 0
    slots[...] = jnp.zeros_like(slots)
    first.wait()
    spread(source, left, right)

    @pl.loop(0, groups)
    def _(g):
        fetch(g).wait()
        for j in range(group):
            s = g * group + j
            block = row_block(left, right, s, count)
            term = lax.dot_general(block, held[s], ROWS_BY_ROWS, preferred_element_type=jnp.float32)
            for t in range(tops):
                o = offsets[t, s]
                k = used[o]
                used[o] = k + 1
                at = pl.ds(o * (count * capacity) + k, count, stride=capacity)
                slots[at, :] = term[:, t * TPATCH : (t + 1) * TPATCH]

    write_out(cuts, fields, capacity, slots, outs, out_sem)


def terms(cuts, capacity, offsets, increments, weights):
    fields, levels, rows, width = increments.shape
    tops, wide = offsets.shape[0], weights.shape[-1]
    count = fields * levels
    group = max(g for g in range(1, GROUP + 1) if rows % g == 0)
    sizes = [last - first for cut in cuts for first, last in zip(cut[:-1], cut[1:])]
    weights = weights.reshape(rows, tops * TPATCH, wide)
    out = pl.pallas_call(
        functools.partial(terms_kernel, cuts, group, capacity),
        in_specs=in_smem(1) + in_hbm(2),
        out_specs=in_hbm(len(sizes)),
        out_shape=[jax.ShapeDtypeStruct((fields * size * capacity, TPATCH), jnp.float32) for size in sizes],
        scratch_shapes=[
            pltpu.VMEM(weights.shape, jnp.bfloat16),
            pltpu.VMEM(increments.shape, jnp.bfloat16),
            pltpu.VMEM((count * rows, width // 2), jnp.float32),
            pltpu.VMEM((count * rows, width // 2), jnp.float32),
            pltpu.VMEM((len(cuts) * count * capacity, TPATCH), jnp.float32),
            pltpu.SMEM((len(cuts),), jnp.int32),
            pltpu.SemaphoreType.DMA,
            pltpu.SemaphoreType.DMA((rows // group,)),
            pltpu.SemaphoreType.DMA((len(sizes),)),
        ],
        compiler_params=params(),
        cost_estimate=pl.CostEstimate(flops=0, bytes_accessed=rows * tops * TPATCH * wide * 2, transcendentals=0),
        name="terms",
    )(offsets, increments, weights)
    given = []
    for cut in cuts:
        given.append(out[: len(cut) - 1])
        out = out[len(cut) - 1 :]
    return given


def sum_kernel(which, parity, patches, odd, places, *refs):
    slot_arrays, refs = refs[: len(which)], refs[len(which) :]
    wholes, outs, partial = [], refs[:-1], refs[-1]
    if parity is not None:
        wholes, outs = outs[:1], outs[1:]
    count = sum(out.shape[0] for out in outs) // patches
    capacity = slot_arrays[0].shape[0] // count
    totals = [partial.at[i] for i in range(len(slot_arrays))]
    for held in totals:
        held[...] = jnp.zeros_like(held)

    def one(k, carry):
        for row, slots, held in zip(which, slot_arrays, totals):
            at = pl.ds(places[row, k], count, stride=patches)
            held[at, :] = held[at, :] + slots[pl.ds(k, count, stride=capacity), :]
        return carry

    lax.fori_loop(0, capacity, one, 0, unroll=4)
    start = 0
    for out in outs:
        at = pl.ds(start, out.shape[0])
        total = totals[0][at, :]
        for more in totals[1:]:
            total = total + more[at, :]
        out[...] = total
        start += out.shape[0]
        if wholes:

            @pl.when(odd[0] == parity)
            def _():
                out[...] += wholes[0][at, :]


def patch_sums(odd, places, slot_arrays, which, patches, counts, whole=None, parity=None):
    wholes = [] if whole is None else [whole]
    return pl.pallas_call(
        functools.partial(sum_kernel, which, parity, patches),
        in_specs=in_smem(2) + in_vmem(len(wholes) + len(slot_arrays)),
        out_specs=in_vmem(len(counts)),
        out_shape=[jax.ShapeDtypeStruct((count * patches, TPATCH), jnp.float32) for count in counts],
        scratch_shapes=[pltpu.VMEM((len(slot_arrays), sum(counts) * patches, TPATCH), jnp.float32)],
        compiler_params=params(24 * 2**20),
        name="patch_sums",
    )(odd, places, *slot_arrays, *wholes)


def fields_kernel(first, settled, last, basis, thickness, wind_first, wind_second, *refs):
    depth, cov_first, cov_second, low_rows, high_rows, low_cols, high_cols = refs[-7:]
    rows, cols = depth.shape[1:]
    blocks = cols // TPATCH
    patches = rows * blocks
    lane = lax.broadcasted_iota(jnp.int32, (rows, TPATCH), 1)

    @pl.when(pl.program_id(0) == 0)
    def _():
        if first:
            low_cols[...] = refs[0][...]
            high_cols[...] = refs[1][...]
        else:
            low, high = (jnp.zeros((rows, TPATCH), jnp.float32) for _ in range(2))
            for f in range(FIELDS):
                lanes = TPATCH - (FIELDS - f) * HALO
                here = (lane >= lanes) & (lane < lanes + HALO)
                tile = refs[1][...] if f == FIELDS - 1 else refs[0][f]
                low = jnp.where(here, pltpu.roll(tile[:, :TPATCH], lanes, 1), low)
                high = jnp.where(here, pltpu.roll(tile[:, cols - TPATCH :], (lanes + HALO) % TPATCH, 1), high)
            low_cols[...] = low
            high_cols[...] = high

    for block in range(blocks):
        at = slice(block * TPATCH, (block + 1) * TPATCH)
        pieces = [slice(c * patches + block * rows, c * patches + (block + 1) * rows) for c in range(FIELDS)]
        east, north, thick = (settled[piece, :] + last[piece, :] for piece in pieces)
        values = (
            thickness[0, :, at] + thick,
            wind_first[0, :, at] + basis[0, :, at] * east + basis[1, :, at] * north,
            wind_second[0, :, at] + basis[2, :, at] * east + basis[3, :, at] * north,
        )
        for f, (ref, value) in enumerate(zip((depth, cov_first, cov_second), values)):
            ref[0, :, at] = value
            low_rows[0, f, :, at] = value[:HALO]
            high_rows[0, f, :, at] = value[rows - HALO :]
            lanes = ((first + pl.program_id(0)) * FIELDS + f) * HALO
            here = (lane >= lanes) & (lane < lanes + HALO)
            if block == 0:
                low_cols[...] = jnp.where(here, pltpu.roll(value, lanes, 1), low_cols[...])
            if block == blocks - 1:
                high_cols[...] = jnp.where(here, pltpu.roll(value, lanes + HALO, 1), high_cols[...])


def first_fields(begin, first, levels, total, patches, settled, last, basis, thickness, wind_first, wind_second, metric, sides, so_far):
    rows, cols = thickness.shape[1:]
    fixed = lambda shape: pl.BlockSpec(shape, lambda l: (0,) * len(shape))
    of_level = lambda start: pl.BlockSpec((1, rows, cols), lambda l: (start + l, 0, 0))
    of_ends = pl.BlockSpec((1, FIELDS, HALO, cols), lambda l: (first - begin + l, 0, 0, 0))
    of_patches = pl.BlockSpec((FIELDS * patches, TPATCH), lambda l: (l, 0))
    shapes = [(total, rows, cols)] * 3 + [(total + 2, FIELDS, HALO, cols)] * 2 + [(rows, TPATCH)] * 2
    beside = sides if so_far else metric
    out = pl.pallas_call(
        functools.partial(fields_kernel, first - begin),
        grid=(levels,),
        in_specs=[of_patches, of_patches, fixed(basis.shape)]
        + [of_level(first)] * 3
        + [fixed(array.shape) for array in beside]
        + in_hbm(len(so_far)),
        out_specs=[of_level(first - begin)] * 3 + [of_ends] * 2 + [fixed((rows, TPATCH))] * 2,
        out_shape=[jax.ShapeDtypeStruct(shape, jnp.float32) for shape in shapes],
        input_output_aliases={8 + i: i for i in range(len(so_far))},
        compiler_params=params(32 * 2**20),
        name="first_fields",
    )(settled, last, basis, thickness, wind_first, wind_second, *beside, *so_far)
    return out[:5], out[5:]


def with_rim(core, entry, lanes, from_below, from_above, left, right):
    ends = jnp.concatenate([from_above[entry], from_below[entry]], axis=0)
    lane = lax.broadcasted_iota(jnp.int32, left.shape, 1)
    rim = jnp.where(
        lane < HALO,
        pltpu.roll(right, (TPATCH - lanes) % TPATCH, 1),
        jnp.where(lane >= TPATCH - HALO, pltpu.roll(left, TPATCH - HALO - lanes, 1), 0.0),
    )
    return jnp.concatenate([jnp.concatenate([core, ends], axis=0), rim], axis=1)


def columns(own, from_below, from_above, side):
    entry = (from_below.shape[0] - 1, side)
    return jnp.concatenate(
        [own[...], from_above[*entry, :, :TPATCH], from_below[*entry, :, :TPATCH]], axis=0
    )


def steps_kernel(diag, cross, turns, wall, *refs):
    metric_halos, halos = refs[:4], refs[4:8]
    parts, outs, rimmed = refs[8 : 8 + FIELDS], refs[-FIELDS - 1 : -1], refs[-1]
    rows, cols = parts[0].shape[1:]
    ext_cols = cols + TPATCH
    l = pl.program_id(0)

    @pl.when(l == 0)
    def _():
        below, above, *own = metric_halos
        left, right = (columns(own[side], below, above, side) for side in range(2))
        for f in range(FIELDS):
            tile = cross[...] if f == FIELDS - 1 else diag[f]
            entry, lanes = (below.shape[0] - 2, f), TPATCH - (FIELDS - f) * HALO
            rimmed[f] = with_rim(tile, entry, lanes, below, above, left, right)

    below, above, *own = halos
    left, right = (columns(own[side], below, above, side) for side in range(2))
    depth, cov_first, cov_second = (
        with_rim(parts[f][0], (l, f), (l * FIELDS + f) * HALO, below, above, left, right) for f in range(FIELDS)
    )
    cos_below, sin_below, cos_above, sin_above = (
        jnp.concatenate([turns[i]] * (ext_cols // TPATCH), axis=1) for i in range(4)
    )
    before = lambda v, axis: pltpu.roll(v, 1, axis)
    after = lambda v, axis: pltpu.roll(v, v.shape[axis] - 1, axis)
    for _ in range(STEPS):
        con_first = rimmed[0] * cov_first + rimmed[2] * cov_second
        con_second = rimmed[2] * cov_first + rimmed[1] * cov_second
        depth_below, depth_above = before(depth, 0), after(depth, 0)
        second_below = sin_below * before(con_first, 0) + cos_below * before(con_second, 0)
        second_above = sin_above * after(con_first, 0) + cos_above * after(con_second, 0)
        face_below = 0.5 * (con_second + second_below)
        flux_below = jnp.maximum(face_below, 0.0) * depth_below + jnp.minimum(face_below, 0.0) * depth
        face_above = 0.5 * (con_second + second_above)
        flux_above = jnp.maximum(face_above, 0.0) * depth + jnp.minimum(face_above, 0.0) * depth_above
        depth_left, depth_right = before(depth, 1), after(depth, 1)
        face_left = 0.5 * (con_first + before(con_first, 1)) * wall[0:1, :]
        flux_left = jnp.maximum(face_left, 0.0) * depth_left + jnp.minimum(face_left, 0.0) * depth
        flux_right = after(flux_left, 1)
        depth = depth - COURANT * ((flux_right - flux_left) + (flux_above - flux_below))
        cov_first = cov_first - GRADIENT * 0.5 * (depth_right - depth_left)
        cov_second = cov_second - GRADIENT * 0.5 * (depth_above - depth_below)
    for ref, value in zip(outs, (depth, cov_first, cov_second)):
        ref[0] = value[:rows, :cols]


def steps(first, levels, total, diag, cross, turns, wall, metric_halos, halos, parts, so_far):
    rows, cols = parts[0].shape[1:]
    fixed = lambda array: pl.BlockSpec(array.shape, lambda l: (0,) * array.ndim)
    of_level = lambda start: pl.BlockSpec((1, rows, cols), lambda l: (start + l, 0, 0))
    given = (diag, cross, turns, wall, *metric_halos, *halos)
    return pl.pallas_call(
        steps_kernel,
        grid=(levels,),
        in_specs=[fixed(array) for array in given] + [of_level(0)] * FIELDS + in_hbm(len(so_far)),
        out_specs=[of_level(first)] * FIELDS,
        out_shape=[jax.ShapeDtypeStruct((total, rows, cols), jnp.float32)] * FIELDS,
        input_output_aliases={len(given) + FIELDS + i: i for i in range(len(so_far))},
        scratch_shapes=[pltpu.VMEM((FIELDS, rows + SUB, cols + TPATCH), jnp.float32)],
        compiler_params=params(32 * 2**20),
        cost_estimate=pl.CostEstimate(flops=0, bytes_accessed=levels * 4 * 2**20, transcendentals=0),
        name="steps",
    )(*given, *parts, *so_far)


def quarter_turn(code):
    cosine = (code == 0).astype(jnp.float32) - (code == 2).astype(jnp.float32)
    sine_value = (code == 1).astype(jnp.float32) - (code == 3).astype(jnp.float32)
    return (cosine, sine_value)


def turn_factors(first_row, rows, total_rows, rotation):
    index = jnp.arange(rows + SUB, dtype=jnp.int32)
    index = jnp.where(index < rows + HALO, index, index - rows - SUB)
    row = (first_row + index) % total_rows
    panel_rows = total_rows // PANELS
    matches = jnp.arange(PANELS, dtype=jnp.int32)[None, :] == (row // panel_rows)[:, None]
    lower = jnp.sum(jnp.where(matches, rotation[0][None, :], 0), axis=1)
    upper = jnp.sum(jnp.where(matches, rotation[1][None, :], 0), axis=1)
    below = jnp.where(row % panel_rows == 0, lower, 0)
    above = jnp.where(row % panel_rows == panel_rows - 1, upper, 0)
    factors = jnp.stack(quarter_turn(below) + quarter_turn(above))
    return jnp.broadcast_to(factors[:, :, None], factors.shape + (TPATCH,))


def shift(array, axis, by, closed):
    size = lax.axis_size(axis)
    pairs = [(i, (i + by) % size) for i in range(size) if closed or 0 <= i + by < size]
    return lax.ppermute(array, axis, pairs)


def together(*arrays):
    return lax.optimization_barrier(arrays)


def body(
    increments,
    remap_weights,
    dest_offset,
    slot_patch,
    rotation,
    basis,
    inv_metric_diag,
    inv_metric_cross,
    thickness,
    wind_first,
    wind_second,
):
    levels, rows, cols = thickness.shape
    tx_count, ty_count = lax.axis_size("tx"), lax.axis_size("ty")
    tx_index, ty_index = lax.axis_index("tx"), lax.axis_index("ty")
    owners, capacity = slot_patch.shape[2:]
    blocks = cols // TPATCH
    patches = rows * blocks
    bounds = [0]
    while bounds[-1] < levels:
        bounds.append(min(levels, bounds[-1] + CHUNKS[len(bounds) - 1]))
    parts = len(bounds) - 1

    evens, odds = range(0, ty_count, 2), range(1, ty_count, 2)
    swap = [(b, b + 1) for b in evens] + [(b, b - 1) for b in odds]
    send = lambda array, pairs: lax.ppermute(array, "ty", pairs)

    to_next = [(b, (b + 2) % ty_count) for b in range(ty_count)]
    places_of = [slot_patch[0, 0]] + [shift(slot_patch[0, 0], "ty", -by, True) for by in (1, 2)]
    odd = (ty_index % 2).reshape(1)

    offsets = dest_offset[0, 0].T
    counts = [FIELDS * (last - first) for first, last in zip(bounds[:-1], bounds[1:])]
    wide = [bounds[pair[0]] for pair in PAIRS] + [levels]
    cuts = [bounds, wide] + [bounds] * (owners - 3) + [wide]
    own, first, second, far = terms(cuts, capacity, offsets, increments, remap_weights)
    *far, places_of[1], places_of[2] = together(*far, places_of[1], places_of[2])
    places, places_next, places_second = ((p % blocks) * rows + p // blocks for p in places_of)
    turns = turn_factors(ty_index * rows, rows, rows * ty_count, rotation)
    column = jnp.arange(cols + TPATCH, dtype=jnp.int32)
    column = tx_index * cols + jnp.where(column < cols + TPATCH // 2, column, column - cols - TPATCH)
    wall = jnp.where((column == 0) | (column == cols * tx_count), 0.0, 1.0).astype(jnp.float32)
    wall = jnp.broadcast_to(wall[None, :], (SUB, cols + TPATCH))

    thirds = [send(slots, to_next) for slots in far]
    token, payload = odd, None
    across, last, settled, found, edges, pending = {}, {}, {}, {}, {}, []
    for step in ORDER.split():
        kind, n = step[0], int(step[1:])
        if kind == "P":
            chunks = PAIRS[n]
            paired = patch_sums(token, places_next, [thirds[n], first[n]], (3, 1), patches, [counts[j] for j in chunks])
            token, *paired = together(token, *paired)
            for j, part in zip(chunks, paired):
                across[j] = send(part, swap)
            if n == 0:
                token, turns, wall = together(token, turns, wall)
        elif kind == "J":
            (joined,) = patch_sums(token, places_second, [second[n]], (2,), patches, [counts[n]], across[n], 0)
            token, joined = together(token, joined)
            last[n] = send(joined, to_next)
        elif kind == "S":
            (settled[n],) = patch_sums(token, places, [own[n]], (0,), patches, [counts[n]], across[n], 1)
            token, settled[n] = together(token, settled[n])
        elif kind == "F":
            (g,) = (i for i, group in enumerate(GROUPS) if n in group)
            begin, total = bounds[GROUPS[g][0]], bounds[GROUPS[g][-1] + 1] - bounds[GROUPS[g][0]]
            token, ready = together(token, settled[n])
            found[g], edges[g] = first_fields(
                begin, bounds[n], bounds[n + 1] - bounds[n], total, patches, ready, last[n], basis, thickness,
                wind_first, wind_second, (inv_metric_diag, inv_metric_cross), edges.get(g), found.get(g, []),
            )
            token, *edges[g] = together(token, *edges[g])
        else:
            begin, total = bounds[GROUPS[n][0]], bounds[GROUPS[n][-1] + 1] - bounds[GROUPS[n][0]]
            *fields, low_rows, high_rows = found[n]
            low_cols, high_cols = edges[n]
            from_left = shift(high_cols, "tx", 1, False)
            from_right = shift(low_cols, "tx", -1, False)

            def ends(entries, at):
                metric = jnp.concatenate([inv_metric_diag, inv_metric_cross[None]], axis=0)[:, at : at + HALO]
                corners = jnp.stack([side[at : at + HALO] for side in (from_left, from_right)])
                corners = jnp.pad(corners, ((0, FIELDS - 2), (0, 0), (0, cols - TPATCH)))
                return entries.at[total].set(metric).at[total + 1].set(corners)

            payload = (ends(high_rows, rows - HALO), ends(low_rows, 0))
            halos = (shift(payload[0], "ty", 1, True), shift(payload[1], "ty", -1, True), from_left, from_right)
            token, *halos = together(token, *halos)
            pending.append((begin, total, halos, fields))

    results, metric_halos = [], pending[0][2]
    for n, (begin, total, halos, fields) in enumerate(pending):
        results = steps(
            begin, total, levels, inv_metric_diag, inv_metric_cross, turns, wall, metric_halos, halos, fields, results
        )
    return tuple(results)


def solution(mesh):
    in_specs = (
        P(None, None, "tx", "ty"),
        P("tx", "ty", None, None, None, None),
        P("tx", "ty", None, None),
        P("tx", "ty", None, None),
        P(),
        P(None, "ty", "tx"),
        P(None, "ty", "tx"),
        P("ty", "tx"),
        P(None, "ty", "tx"),
        P(None, "ty", "tx"),
        P(None, "ty", "tx"),
    )
    out_specs = (P(None, "ty", "tx"), P(None, "ty", "tx"), P(None, "ty", "tx"))
    return jax.shard_map(body, mesh=mesh, in_specs=in_specs, out_specs=out_specs, check_vma=False)
```

time: 152 us -> 119 us (0.78)
  starting transfers between devices: 52.8 us -> 18.7 us
  other arithmetic: 6.75 us -> 0.25 us
  waiting for transfers between devices: 40.9 us -> 47 us
  Pallas kernels: 37.5 us -> 41.3 us
  local copies, waits for them, and re-layouts: 12.3 us -> 10.6 us
    ppermute x14 -> x6, starting transfers between devices: 41 us -> 15.2 us  [shift(): return lax.ppermute(array, axis, pairs)]
    ppermute x8 -> x12, waiting for transfers between devices: 13.4 us -> 36.6 us  [body(): send = lambda array, pairs: lax.ppermute(array, 'ty', pairs)]
    ppermute x14 -> x6, waiting for transfers between devices: 27.5 us -> 10.4 us  [shift(): return lax.ppermute(array, axis, pairs)]
    ppermute x8 -> x12, starting transfers between devices: 11.8 us -> 3.5 us  [body(): send = lambda array, pairs: lax.ppermute(array, 'ty', pairs)]
    pallas_call x9 -> x18, Pallas kernels: 37.5 us -> 41.3 us  [the longest x12 18.3 us: patch_sums(): pl.pallas_call(functools.partial(sum_kernel, which, parity, patches), in_...]
    concatenate x5 -> x0, other arithmetic: 3.67 us -> none  [the longest x3 2.57 us: body(): return tuple((jnp.concatenate(field, axis=0) for field in zip(*results)))]
    slice x6 -> x0, local copies, waits for them, and re-layouts: 3.14 us -> none  [the longest x2 3.12 us: body(): a[bounds[j]:bounds[j + 1]]]
    slice x2 -> x0, other arithmetic: 1.63 us -> none  [the longest x1 1.01 us: rimmed(): right = shift(array[:, :, :HALO], 'tx', -1, False)]
  transfers between devices with their start and end apart: 22 -> 18, of which waited for: 4 -> 10; matrix products, arithmetic and copies ran while one was open for 5% -> 1% of each run, Pallas kernels for 13% -> 26%
where the time goes in v2:
time: 119 us
  waiting for transfers between devices  47 us (39%)
  Pallas kernels  41.3 us (35%)
  starting transfers between devices  18.7 us (16%)
  local copies, waits for them, and re-layouts  10.6 us (9%)
    ppermute x12, waiting for transfers between devices, body(): send = lambda array, pairs: lax.ppermute(array, 'ty', pairs)  36.6 us
    pallas_call x12, Pallas kernels, patch_sums(): pl.pallas_call(functools.partial(sum_kernel, which, parity, patches), in_...  18.3 us
    ppermute x6, starting transfers between devices, shift(): return lax.ppermute(array, axis, pairs)  15.2 us
    pallas_call x1, Pallas kernels, terms(): pl.pallas_call(functools.partial(terms_kernel, cuts, group, capacity), in...  11.9 us
    ppermute x6, waiting for transfers between devices, shift(): return lax.ppermute(array, axis, pairs)  10.4 us
    pallas_call x1, Pallas kernels, steps(): pl.pallas_call(steps_kernel, grid=(levels,), in_specs=[fixed(array) for a...  9.79 us
    unnamed x38, local copies, waits for them, and re-layouts  9.77 us
    ppermute x12, starting transfers between devices, body(): send = lambda array, pairs: lax.ppermute(array, 'ty', pairs)  3.5 us
  transfers between devices with their start and end apart: 18, of which 10 were waited for; matrix products, arithmetic and copies ran while one was open for 1% of the time, Pallas kernels for 26%

profile of v2, /device:TPU:1, one launch (start us, length us, event | category | flops | bytes accessed | tf_op | source)
XLA Modules:
  0.0 118.9 jit_solution(3309022654907290915)
XLA Ops:
  0.7 4.2 %collective-permute-start.1 = (s32[4,108]{1,0:T(4,128)}, s32[4,108]{1,0:T(4,128)S(1)}, u32[]{:S(2)}, u32[]{:S(2)}) collective-permute-start(s32[4,108]{1,0:T(4,128)} %bitcast.50), channel_id=1, source_target_pairs={{0,6},{1,7},{2,0},{3,1},{4,2},{5,3},{6,4},{7,5},{8,14},{9,15},{10,... | collective-permute-start | bytes 5192 | tf_op jit(solution)/shard_map/ppermute | solution.py:364
  6.9 11.9 %terms.1 = (f32[648,128]{1,0:T(8,128)}, f32[648,128]{1,0:T(8,128)}, f32[648,128]{1,0:T(8,128)}, f32[648,128]{1,0:T(8,128)}, f32[648,128]{1,0:T(8,128)}, /*index=...) custom-call(s32[2,144]{1,0:T(2,128)} %bitcast.52, ...), custom_call_target="tpu_custom_call" | custom-call | bytes 18874368 | tf_op jit(solution)/shard_map/terms/pallas_call | solution.py:116
  18.9 1.4 %collective-permute-start.2 = (f32[648,128]{1,0:T(8,128)}, f32[648,128]{1,0:T(8,128)S(1)}, u32[]{:S(2)}, u32[]{:S(2)}) collective-permute-start(f32[648,128]{1,0:T(8,128)} %get-tuple-element.148), channel_id=1, source_target_pairs={{0,2},{1,3},{2,4},{3,5},{4,6},{5,7},{6,0},{7,1},{8,10},{9,11},{10,... | collective-permute-start | bytes 995336 | tf_op jit(solution)/shard_map/ppermute | solution.py:397
  20.4 8.5 %collective-permute-done.2.refs_0_ = f32[648,128]{1,0:T(8,128)S(1)} collective-permute-done((f32[648,128]{1,0:T(8,128)}, f32[648,128]{1,0:T(8,128)S(1)}, u32[]{:S(2)}, u32[]{:S(2)}) %collective-permute-start.2) | collective-permute-done | bytes 331808 | tf_op jit(solution)/shard_map/ppermute | solution.py:397
  29.9 2.0 %patch_sums.12 = f32[864,128]{1,0:T(8,128)S(1)} custom-call(s32[1]{0:T(128)} %bitcast.odd, s32[4,108]{1,0:T(4,128)S(1)} %fusion.9.places, f32[648,128]{1,0:T(8,128)S(1)} %collective-permute-done.2.refs_0_, f32[648,128]{1,0:T(8,128)S(1)} %copy-done.17), custom_call_target="tpu_custom_call" | custom-call | tf_op jit(solution)/shard_map/patch_sums/pallas_call | solution.py:178
  32.5 3.6 %collective-permute-done.3.refs_0_ = f32[648,128]{1,0:T(8,128)S(1)} collective-permute-done((f32[648,128]{1,0:T(8,128)}, f32[648,128]{1,0:T(8,128)S(1)}, u32[]{:S(2)}, u32[]{:S(2)}) %collective-permute-start.3) | collective-permute-done | bytes 331808 | tf_op jit(solution)/shard_map/ppermute | solution.py:397
  37.1 2.0 %patch_sums.13 = f32[864,128]{1,0:T(8,128)S(1)} custom-call(s32[1]{0:T(128)} %bitcast.odd, s32[4,108]{1,0:T(4,128)S(1)} %fusion.9.places, f32[648,128]{1,0:T(8,128)S(1)} %collective-permute-done.3.refs_0_, f32[648,128]{1,0:T(8,128)S(1)} %copy-done.16), custom_call_target="tpu_custom_call" | custom-call | tf_op jit(solution)/shard_map/patch_sums/pallas_call | solution.py:178
  39.5 3.7 %collective-permute-done.4.refs_0_ = f32[648,128]{1,0:T(8,128)S(1)} collective-permute-done((f32[648,128]{1,0:T(8,128)}, f32[648,128]{1,0:T(8,128)S(1)}, u32[]{:S(2)}, u32[]{:S(2)}) %collective-permute-start.4) | collective-permute-done | bytes 331808 | tf_op jit(solution)/shard_map/ppermute | solution.py:397
  44.2 2.0 %patch_sums.14 = f32[864,128]{1,0:T(8,128)S(1)} custom-call(s32[1]{0:T(128)} %bitcast.odd, s32[4,108]{1,0:T(4,128)S(1)} %fusion.9.places, f32[648,128]{1,0:T(8,128)S(1)} %collective-permute-done.4.refs_0_, f32[648,128]{1,0:T(8,128)S(1)} %copy-done.15), custom_call_target="tpu_custom_call" | custom-call | tf_op jit(solution)/shard_map/patch_sums/pallas_call | solution.py:178
  47.6 1.4 %patch_sums.15 = f32[864,128]{1,0:T(8,128)S(1)} custom-call(s32[1]{0:T(128)} %bitcast.odd, s32[4,108]{1,0:T(4,128)S(1)} %fusion.8.places, f32[648,128]{1,0:T(8,128)S(1)} %copy-done.14, f32[864,128]{1,0:T(8,128)S(1)} %collective-permute-done.5.refs_1_), custom_call_target="tpu_custom_call" | custom-call | tf_op jit(solution)/shard_map/patch_sums/pallas_call | solution.py:178
  51.3 2.0 %patch_sums.16 = f32[864,128]{1,0:T(8,128)S(1)} custom-call(s32[1]{0:T(128)} %bitcast.odd, s32[4,108]{1,0:T(4,128)S(1)} %fusion.9.places, f32[648,128]{1,0:T(8,128)S(1)} %collective-permute-done.6.refs_0_, f32[648,128]{1,0:T(8,128)S(1)} %copy-done.13), custom_call_target="tpu_custom_call" | custom-call | tf_op jit(solution)/shard_map/patch_sums/pallas_call | solution.py:178
  54.7 1.3 %patch_sums.17 = f32[864,128]{1,0:T(8,128)S(1)} custom-call(s32[1]{0:T(128)} %bitcast.odd, s32[4,108]{1,0:T(4,128)S(1)} %fusion.8.places, f32[648,128]{1,0:T(8,128)S(1)} %copy-done.12, f32[864,128]{1,0:T(8,128)S(1)} %collective-permute-done.7.refs_1_), custom_call_target="tpu_custom_call" | custom-call | tf_op jit(solution)/shard_map/patch_sums/pallas_call | solution.py:178
  56.1 4.7 %collective-permute-done.8.refs_1_ = f32[864,128]{1,0:T(8,128)S(1)} collective-permute-done((f32[864,128]{1,0:T(8,128)S(1)}, f32[864,128]{1,0:T(8,128)S(1)}, u32[]{:S(2)}, u32[]{:S(2)}) %collective-permute-start.8) | collective-permute-done | bytes 442400 | tf_op jit(solution)/shard_map/ppermute | solution.py:397
  61.8 1.3 %patch_sums.18 = f32[864,128]{1,0:T(8,128)S(1)} custom-call(s32[1]{0:T(128)} %bitcast.odd, s32[4,108]{1,0:T(4,128)S(1)} %fusion.8.places, f32[648,128]{1,0:T(8,128)S(1)} %copy-done.11, f32[864,128]{1,0:T(8,128)S(1)} %collective-permute-done.8.refs_1_), custom_call_target="tpu_custom_call" | custom-call | tf_op jit(solution)/shard_map/patch_sums/pallas_call | solution.py:178
  65.9 4.4 %collective-permute-done.10.refs_1_ = f32[864,128]{1,0:T(8,128)S(1)} collective-permute-done((f32[864,128]{1,0:T(8,128)S(1)}, f32[864,128]{1,0:T(8,128)S(1)}, u32[]{:S(2)}, u32[]{:S(2)}) %collective-permute-start.10) | collective-permute-done | bytes 442400 | tf_op jit(solution)/shard_map/ppermute | solution.py:397
  71.3 1.3 %patch_sums.20 = f32[864,128]{1,0:T(8,128)S(1)} custom-call(s32[1]{0:T(128)} %bitcast.odd, s32[4,108]{1,0:T(4,128)S(1)} %fusion.8.places, f32[648,128]{1,0:T(8,128)S(1)} %copy-done.9, f32[864,128]{1,0:T(8,128)S(1)} %collective-permute-done.10.refs_1_), custom_call_target="tpu_custom_call" | custom-call | tf_op jit(solution)/shard_map/patch_sums/pallas_call | solution.py:178
  76.5 2.4 %collective-permute-done.12.last = f32[864,128]{1,0:T(8,128)S(1)} collective-permute-done((f32[864,128]{1,0:T(8,128)S(1)}, f32[864,128]{1,0:T(8,128)S(1)}, u32[]{:S(2)}, u32[]{:S(2)}) %collective-permute-start.12) | collective-permute-done | bytes 442400 | tf_op jit(solution)/shard_map/ppermute | solution.py:397
  80.5 7.9 %collective-permute-done.13.last = f32[864,128]{1,0:T(8,128)S(1)} collective-permute-done((f32[864,128]{1,0:T(8,128)S(1)}, f32[864,128]{1,0:T(8,128)S(1)}, u32[]{:S(2)}, u32[]{:S(2)}) %collective-permute-start.13) | collective-permute-done | bytes 442400 | tf_op jit(solution)/shard_map/ppermute | solution.py:397
  88.7 6.4 %collective-permute-start.14 = (f32[48,128]{1,0:T(8,128)S(1)}, f32[48,128]{1,0:T(8,128)S(1)}, u32[]{:S(2)}, u32[]{:S(2)}) collective-permute-start(f32[48,128]{1,0:T(8,128)S(1)} %get-tuple-element.224), channel_id=1, source_target_pairs={{0,8},{8,16},{16,24},{1,9},{9,17},{17,25},{2,10},{10,18},{18,26},{... | collective-permute-start | bytes 73736 | tf_op jit(solution)/shard_map/ppermute | solution.py:364
  95.1 1.9 %collective-permute-start.15 = (f32[48,128]{1,0:T(8,128)S(1)}, f32[48,128]{1,0:T(8,128)S(1)}, u32[]{:S(2)}, u32[]{:S(2)}) collective-permute-start(f32[48,128]{1,0:T(8,128)S(1)} %get-tuple-element.225), channel_id=1, source_target_pairs={{8,0},{16,8},{24,16},{9,1},{17,9},{25,17},{10,2},{18,10},{26,18},{... | collective-permute-start | bytes 73736 | tf_op jit(solution)/shard_map/ppermute | solution.py:364
  97.1 3.2 %collective-permute-done.15.refs_3_.refs_7_ = f32[48,128]{1,0:T(8,128)S(1)} collective-permute-done((f32[48,128]{1,0:T(8,128)S(1)}, f32[48,128]{1,0:T(8,128)S(1)}, u32[]{:S(2)}, u32[]{:S(2)}) %collective-permute-start.15) | collective-permute-done | bytes 24608 | tf_op jit(solution)/shard_map/ppermute | solution.py:364
  100.4 1.5 %collective-permute-start.16 = (f32[10,3,4,384]{3,2,1,0:T(4,128)S(1)}, f32[10,3,4,384]{3,2,1,0:T(4,128)S(1)}, u32[]{:S(2)}, u32[]{:S(2)}) collective-permute-start(f32[10,3,4,384]{3,2,1,0:T(4,128)S(1)} %fusion.5), channel_id=1, source_target_pairs={{0,1},{1,2},{2,3},{3,4},{4,5},{5,6},{6,7},{7,0},{8,9},{9,10},{10,1... | collective-permute-start | bytes 552968 | tf_op jit(solution)/shard_map/ppermute | solution.py:364
  101.9 7.2 %collective-permute-done.17.refs_1_.refs_5_ = f32[10,3,4,384]{3,2,1,0:T(4,128)S(1)} collective-permute-done((f32[10,3,4,384]{3,2,1,0:T(4,128)S(1)}, f32[10,3,4,384]{3,2,1,0:T(4,128)S(1)}, u32[]{:S(2)}, u32[]{:S(2)}) %collective-permute-start.17) | collective-permute-done | bytes 184352 | tf_op jit(solution)/shard_map/ppermute | solution.py:364
  109.1 9.8 %steps.1 = (f32[8,48,384]{2,1,0:T(8,128)}, f32[8,48,384]{2,1,0:T(8,128)}, f32[8,48,384]{2,1,0:T(8,128)}) custom-call(f32[2,48,384]{2,1,0:T(8,128)S(1)} %copy-done.4, f32[48,384]{1,0:T(8,128)S(1)} %copy-done.5, f32[4,56,128]{2,1,0:T(8,128)S(1)} %broadcast_in_dim.56.turns, f32[8,512]{1,0:T(8,128)S(1)} %broadcast_in_dim.59.wall, ...), custom_call_target="tpu_custom_call" | custom-call | bytes 33554432 | tf_op jit(solution)/shard_map/steps/pallas_call | solution.py:327
  (84 shorter events, 21.8 us)
Async XLA Ops:
  0.6 64.8 %copy-start.2 = (f32[8,48,384]{2,1,0:T(8,128)S(1)}, f32[8,48,384]{2,1,0:T(8,128)}, u32[]{:S(2)}) copy-start(f32[8,48,384]{2,1,0:T(8,128)} %wind_second.7) | copy-start | bytes 1769476
  0.7 64.8 %copy-start.1 = (f32[8,48,384]{2,1,0:T(8,128)S(1)}, f32[8,48,384]{2,1,0:T(8,128)}, u32[]{:S(2)}) copy-start(f32[8,48,384]{2,1,0:T(8,128)} %wind_first.7) | copy-start | bytes 1769476
  0.7 64.8 %copy-start = (f32[8,48,384]{2,1,0:T(8,128)S(1)}, f32[8,48,384]{2,1,0:T(8,128)}, u32[]{:S(2)}) copy-start(f32[8,48,384]{2,1,0:T(8,128)} %thickness.7) | copy-start | bytes 1769476
  0.7 64.8 %copy-start.3 = (f32[4,48,384]{2,1,0:T(8,128)S(1)}, f32[4,48,384]{2,1,0:T(8,128)}, u32[]{:S(2)}) copy-start(f32[4,48,384]{2,1,0:T(8,128)} %basis.7) | copy-start | bytes 884740
  0.7 64.8 %copy-start.5 = (f32[48,384]{1,0:T(8,128)S(1)}, f32[48,384]{1,0:T(8,128)}, u32[]{:S(2)}) copy-start(f32[48,384]{1,0:T(8,128)} %cross.1) | copy-start | bytes 221188
  0.7 64.8 %copy-start.4 = (f32[2,48,384]{2,1,0:T(8,128)S(1)}, f32[2,48,384]{2,1,0:T(8,128)}, u32[]{:S(2)}) copy-start(f32[2,48,384]{2,1,0:T(8,128)} %diag.1) | copy-start | bytes 442372
  0.7 18.1 %collective-permute-start.1 = (s32[4,108]{1,0:T(4,128)}, s32[4,108]{1,0:T(4,128)S(1)}, u32[]{:S(2)}, u32[]{:S(2)}) collective-permute-start(s32[4,108]{1,0:T(4,128)} %bitcast.50), channel_id=1, source_target_pairs={{0,6},{1,7},{2,0},{3,1},{4,2},{5,3},{6,4},{7,5},{8,14},{9,15},{10,... | collective-permute-start | bytes 5192 | tf_op jit(solution)/shard_map/ppermute | solution.py:364
  4.9 14.0 %collective-permute-start = (s32[4,108]{1,0:T(4,128)}, s32[4,108]{1,0:T(4,128)S(1)}, u32[]{:S(2)}, u32[]{:S(2)}) collective-permute-start(s32[4,108]{1,0:T(4,128)} %bitcast.51), channel_id=1, source_target_pairs={{0,7},{1,0},{2,1},{3,2},{4,3},{5,4},{6,5},{7,6},{8,15},{9,8},{10,9... | collective-permute-start | bytes 5192 | tf_op jit(solution)/shard_map/ppermute | solution.py:364
  18.9 10.1 %collective-permute-start.2 = (f32[648,128]{1,0:T(8,128)}, f32[648,128]{1,0:T(8,128)S(1)}, u32[]{:S(2)}, u32[]{:S(2)}) collective-permute-start(f32[648,128]{1,0:T(8,128)} %get-tuple-element.148), channel_id=1, source_target_pairs={{0,2},{1,3},{2,4},{3,5},{4,6},{5,7},{6,0},{7,1},{8,10},{9,11},{10,... | collective-permute-start | bytes 995336 | tf_op jit(solution)/shard_map/ppermute | solution.py:397
  20.3 15.8 %collective-permute-start.3 = (f32[648,128]{1,0:T(8,128)}, f32[648,128]{1,0:T(8,128)S(1)}, u32[]{:S(2)}, u32[]{:S(2)}) collective-permute-start(f32[648,128]{1,0:T(8,128)} %get-tuple-element.154), channel_id=1, source_target_pairs={{0,2},{1,3},{2,4},{3,5},{4,6},{5,7},{6,0},{7,1},{8,10},{9,11},{10,... | collective-permute-start | bytes 995336 | tf_op jit(solution)/shard_map/ppermute | solution.py:397
  20.3 22.9 %collective-permute-start.4 = (f32[648,128]{1,0:T(8,128)}, f32[648,128]{1,0:T(8,128)S(1)}, u32[]{:S(2)}, u32[]{:S(2)}) collective-permute-start(f32[648,128]{1,0:T(8,128)} %get-tuple-element.157), channel_id=1, source_target_pairs={{0,2},{1,3},{2,4},{3,5},{4,6},{5,7},{6,0},{7,1},{8,10},{9,11},{10,... | collective-permute-start | bytes 995336 | tf_op jit(solution)/shard_map/ppermute | solution.py:397
  31.9 14.7 %collective-permute-start.5 = (f32[864,128]{1,0:T(8,128)S(1)}, f32[864,128]{1,0:T(8,128)S(1)}, u32[]{:S(2)}, u32[]{:S(2)}) collective-permute-start(f32[864,128]{1,0:T(8,128)S(1)} %patch_sums.12), channel_id=1, source_target_pairs={{0,1},{2,3},{4,5},{6,7},{1,0},{3,2},{5,4},{7,6},{8,9},{10,11},{12,... | collective-permute-start | bytes 1327112 | tf_op jit(solution)/shard_map/ppermute | solution.py:397
  32.4 17.9 %collective-permute-start.6 = (f32[648,128]{1,0:T(8,128)}, f32[648,128]{1,0:T(8,128)S(1)}, u32[]{:S(2)}, u32[]{:S(2)}) collective-permute-start(f32[648,128]{1,0:T(8,128)} %get-tuple-element.164), channel_id=1, source_target_pairs={{0,2},{1,3},{2,4},{3,5},{4,6},{5,7},{6,0},{7,1},{8,10},{9,11},{10,... | collective-permute-start | bytes 995336 | tf_op jit(solution)/shard_map/ppermute | solution.py:397
  39.0 14.7 %collective-permute-start.7 = (f32[864,128]{1,0:T(8,128)S(1)}, f32[864,128]{1,0:T(8,128)S(1)}, u32[]{:S(2)}, u32[]{:S(2)}) collective-permute-start(f32[864,128]{1,0:T(8,128)S(1)} %patch_sums.13), channel_id=1, source_target_pairs={{0,1},{2,3},{4,5},{6,7},{1,0},{3,2},{5,4},{7,6},{8,9},{10,11},{12,... | collective-permute-start | bytes 1327112 | tf_op jit(solution)/shard_map/ppermute | solution.py:397
  46.1 14.7 %collective-permute-start.8 = (f32[864,128]{1,0:T(8,128)S(1)}, f32[864,128]{1,0:T(8,128)S(1)}, u32[]{:S(2)}, u32[]{:S(2)}) collective-permute-start(f32[864,128]{1,0:T(8,128)S(1)} %patch_sums.14), channel_id=1, source_target_pairs={{0,1},{2,3},{4,5},{6,7},{1,0},{3,2},{5,4},{7,6},{8,9},{10,11},{12,... | collective-permute-start | bytes 1327112 | tf_op jit(solution)/shard_map/ppermute | solution.py:397
  48.9 16.5 %collective-permute-start.9 = (f32[864,128]{1,0:T(8,128)S(1)}, f32[864,128]{1,0:T(8,128)S(1)}, u32[]{:S(2)}, u32[]{:S(2)}) collective-permute-start(f32[864,128]{1,0:T(8,128)S(1)} %patch_sums.15), channel_id=1, source_target_pairs={{0,2},{1,3},{2,4},{3,5},{4,6},{5,7},{6,0},{7,1},{8,10},{9,11},{10,... | collective-permute-start | bytes 1327112 | tf_op jit(solution)/shard_map/ppermute | solution.py:397
  53.2 17.1 %collective-permute-start.10 = (f32[864,128]{1,0:T(8,128)S(1)}, f32[864,128]{1,0:T(8,128)S(1)}, u32[]{:S(2)}, u32[]{:S(2)}) collective-permute-start(f32[864,128]{1,0:T(8,128)S(1)} %patch_sums.16), channel_id=1, source_target_pairs={{0,1},{2,3},{4,5},{6,7},{1,0},{3,2},{5,4},{7,6},{8,9},{10,11},{12,... | collective-permute-start | bytes 1327112 | tf_op jit(solution)/shard_map/ppermute | solution.py:397
  56.0 18.9 %collective-permute-start.11 = (f32[864,128]{1,0:T(8,128)S(1)}, f32[864,128]{1,0:T(8,128)S(1)}, u32[]{:S(2)}, u32[]{:S(2)}) collective-permute-start(f32[864,128]{1,0:T(8,128)S(1)} %patch_sums.17), channel_id=1, source_target_pairs={{0,2},{1,3},{2,4},{3,5},{4,6},{5,7},{6,0},{7,1},{8,10},{9,11},{10,... | collective-permute-start | bytes 1327112 | tf_op jit(solution)/shard_map/ppermute | solution.py:397
  65.4 13.5 %collective-permute-start.12 = (f32[864,128]{1,0:T(8,128)S(1)}, f32[864,128]{1,0:T(8,128)S(1)}, u32[]{:S(2)}, u32[]{:S(2)}) collective-permute-start(f32[864,128]{1,0:T(8,128)S(1)} %patch_sums.18), channel_id=1, source_target_pairs={{0,2},{1,3},{2,4},{3,5},{4,6},{5,7},{6,0},{7,1},{8,10},{9,11},{10,... | collective-permute-start | bytes 1327112 | tf_op jit(solution)/shard_map/ppermute | solution.py:397
  72.6 15.8 %collective-permute-start.13 = (f32[864,128]{1,0:T(8,128)S(1)}, f32[864,128]{1,0:T(8,128)S(1)}, u32[]{:S(2)}, u32[]{:S(2)}) collective-permute-start(f32[864,128]{1,0:T(8,128)S(1)} %patch_sums.20), channel_id=1, source_target_pairs={{0,2},{1,3},{2,4},{3,5},{4,6},{5,7},{6,0},{7,1},{8,10},{9,11},{10,... | collective-permute-start | bytes 1327112 | tf_op jit(solution)/shard_map/ppermute | solution.py:397
  88.7 8.4 %collective-permute-start.14 = (f32[48,128]{1,0:T(8,128)S(1)}, f32[48,128]{1,0:T(8,128)S(1)}, u32[]{:S(2)}, u32[]{:S(2)}) collective-permute-start(f32[48,128]{1,0:T(8,128)S(1)} %get-tuple-element.224), channel_id=1, source_target_pairs={{0,8},{8,16},{16,24},{1,9},{9,17},{17,25},{2,10},{10,18},{18,26},{... | collective-permute-start | bytes 73736 | tf_op jit(solution)/shard_map/ppermute | solution.py:364
  95.1 5.1 %collective-permute-start.15 = (f32[48,128]{1,0:T(8,128)S(1)}, f32[48,128]{1,0:T(8,128)S(1)}, u32[]{:S(2)}, u32[]{:S(2)}) collective-permute-start(f32[48,128]{1,0:T(8,128)S(1)} %get-tuple-element.225), channel_id=1, source_target_pairs={{8,0},{16,8},{24,16},{9,1},{17,9},{25,17},{10,2},{18,10},{26,18},{... | collective-permute-start | bytes 73736 | tf_op jit(solution)/shard_map/ppermute | solution.py:364
  100.3 8.8 %collective-permute-start.17 = (f32[10,3,4,384]{3,2,1,0:T(4,128)S(1)}, f32[10,3,4,384]{3,2,1,0:T(4,128)S(1)}, u32[]{:S(2)}, u32[]{:S(2)}) collective-permute-start(f32[10,3,4,384]{3,2,1,0:T(4,128)S(1)} %fusion.1), channel_id=1, source_target_pairs={{0,7},{1,0},{2,1},{3,2},{4,3},{5,4},{6,5},{7,6},{8,15},{9,8},{10,9... | collective-permute-start | bytes 552968 | tf_op jit(solution)/shard_map/ppermute | solution.py:364
  100.4 8.7 %collective-permute-start.16 = (f32[10,3,4,384]{3,2,1,0:T(4,128)S(1)}, f32[10,3,4,384]{3,2,1,0:T(4,128)S(1)}, u32[]{:S(2)}, u32[]{:S(2)}) collective-permute-start(f32[10,3,4,384]{3,2,1,0:T(4,128)S(1)} %fusion.5), channel_id=1, source_target_pairs={{0,1},{1,2},{2,3},{3,4},{4,5},{5,6},{6,7},{7,0},{8,9},{9,10},{10,1... | collective-permute-start | bytes 552968 | tf_op jit(solution)/shard_map/ppermute | solution.py:364
  (13 other events, 182.0 us)

commit v3 on v2

--- a/solution.py
+++ b/solution.py
@@ -15,10 +15,15 @@
 FIELDS = 3
 COURANT = 0.15
 GRADIENT = 0.3
+GRADIENT_HALF = GRADIENT * 0.5
 CHUNKS = (2, 2, 2, 2)
 PAIRS = ((0,), (1,), (2,), (3,))
-GROUPS = ((0, 1, 2, 3),)
-ORDER = "P0 P1 P2 J0 P3 J1 J2 S0 F0 J3 S1 F1 S2 F2 S3 F3 H0"
+GROUPS = ((0, 1), (2, 3))
+LATE = ()
+EARLY = ((0, 2),)
+ORDER = (
+    "P0", "P1", "P2", "J0", "P3", "J1", "S0", "S1", "J2", "F0", "J3", "S2", "S3", "F1", "F2", "H0", "F3", "H1",
+)
 GROUP = 16
 VMEM = 61 * 2**20
 
@@ -220,8 +225,8 @@
         )
         for f, (ref, value) in enumerate(zip((depth, cov_first, cov_second), values)):
             ref[0, :, at] = value
-            low_rows[0, f, :, at] = value[:HALO]
-            high_rows[0, f, :, at] = value[rows - HALO :]
+            low_rows[f, :, at] = value[:HALO]
+            high_rows[f, :, at] = value[rows - HALO :]
             lanes = ((first + pl.program_id(0)) * FIELDS + f) * HALO
             here = (lane >= lanes) & (lane < lanes + HALO)
             if block == 0:
@@ -230,132 +235,186 @@
                 high_cols[...] = jnp.where(here, pltpu.roll(value, lanes + HALO, 1), high_cols[...])
 
 
-def first_fields(begin, first, levels, total, patches, settled, last, basis, thickness, wind_first, wind_second, metric, sides, so_far):
-    rows, cols = thickness.shape[1:]
+def first_fields(place, levels, patches, settled, last, basis, thickness, wind_first, wind_second, metric, sides, fields, ends, later):
+    first, begin, total, extra = place
+    every, rows, cols = thickness.shape
     fixed = lambda shape: pl.BlockSpec(shape, lambda l: (0,) * len(shape))
-    of_level = lambda start: pl.BlockSpec((1, rows, cols), lambda l: (start + l, 0, 0))
-    of_ends = pl.BlockSpec((1, FIELDS, HALO, cols), lambda l: (first - begin + l, 0, 0, 0))
+    of_level = pl.BlockSpec((1, rows, cols), lambda l: (first + l, 0, 0))
+    of_ends = pl.BlockSpec((FIELDS, HALO, cols), lambda l: (first - begin + l, 0, 0))
     of_patches = pl.BlockSpec((FIELDS * patches, TPATCH), lambda l: (l, 0))
-    shapes = [(total, rows, cols)] * 3 + [(total + 2, FIELDS, HALO, cols)] * 2 + [(rows, TPATCH)] * 2
-    beside = sides if so_far else metric
+    shapes = [(every, rows, cols)] * 3 + [(total * FIELDS + extra, HALO, cols)] * 2 + [(rows, TPATCH)] * 2
+    beside = sides if ends else metric
+    given = [*fields, *ends]
+    aliases = {8 + i: i for i in range(len(fields))}
+    aliases.update({8 + len(fields) + i: FIELDS + i for i in range(len(ends))})
     out = pl.pallas_call(
         functools.partial(fields_kernel, first - begin),
         grid=(levels,),
         in_specs=[of_patches, of_patches, fixed(basis.shape)]
-        + [of_level(first)] * 3
+        + [of_level] * 3
         + [fixed(array.shape) for array in beside]
-        + in_hbm(len(so_far)),
-        out_specs=[of_level(first - begin)] * 3 + [of_ends] * 2 + [fixed((rows, TPATCH))] * 2,
+        + in_hbm(len(given) + len(later)),
+        out_specs=[of_level] * 3 + [of_ends] * 2 + [fixed((rows, TPATCH))] * 2,
         out_shape=[jax.ShapeDtypeStruct(shape, jnp.float32) for shape in shapes],
-        input_output_aliases={8 + i: i for i in range(len(so_far))},
+        input_output_aliases=aliases,
         compiler_params=params(32 * 2**20),
         name="first_fields",
-    )(settled, last, basis, thickness, wind_first, wind_second, *beside, *so_far)
-    return out[:5], out[5:]
-
-
-def with_rim(core, entry, lanes, from_below, from_above, left, right):
-    ends = jnp.concatenate([from_above[entry], from_below[entry]], axis=0)
+    )(settled, last, basis, thickness, wind_first, wind_second, *beside, *given, *later)
+    return out[:3], out[3:5], out[5:]
+
+
+def entries_kernel(diag, cross, left, right, *refs):
+    outs, i, count = refs[-2:], pl.program_id(0), pl.num_programs(0)
+    rows, cols = cross.shape
+    for out, at in zip(outs, (0, rows - HALO)):
+        for f in range(FIELDS):
+
+            @pl.when((i == f) & (i < count - 1))
+            def _():
+                out[0] = cross[at : at + HALO, :] if f == FIELDS - 1 else diag[f, at : at + HALO, :]
+
+        @pl.when(i == count - 1)
+        def _():
+            out[...] = jnp.zeros_like(out)
+            out[0, :, :TPATCH] = left[at : at + HALO, :]
+            out[0, :, TPATCH : 2 * TPATCH] = right[at : at + HALO, :]
+
+
+def last_entries(extra, ends, diag, cross, sides, later):
+    whole, cols = ends[0].shape[0], ends[0].shape[-1]
+    entry = pl.BlockSpec((1, HALO, cols), lambda i: (whole - extra + i, 0, 0))
+    fixed = lambda array: pl.BlockSpec(array.shape, lambda i: (0,) * array.ndim)
+    given = (diag, cross, *sides)
+    return pl.pallas_call(
+        entries_kernel,
+        grid=(extra,),
+        in_specs=[fixed(array) for array in given] + in_hbm(len(ends) + len(later)),
+        out_specs=[entry] * 2,
+        out_shape=[jax.ShapeDtypeStruct(end.shape, jnp.float32) for end in ends],
+        input_output_aliases={len(given) + i: i for i in range(len(ends))},
+        compiler_params=params(16 * 2**20),
+        name="last_entries",
+    )(*given, *ends, *later)
+
+
+def rim_tile(lanes, left, right):
     lane = lax.broadcasted_iota(jnp.int32, left.shape, 1)
-    rim = jnp.where(
+    return jnp.where(
         lane < HALO,
         pltpu.roll(right, (TPATCH - lanes) % TPATCH, 1),
         jnp.where(lane >= TPATCH - HALO, pltpu.roll(left, TPATCH - HALO - lanes, 1), 0.0),
     )
-    return jnp.concatenate([jnp.concatenate([core, ends], axis=0), rim], axis=1)
-
-
-def columns(own, from_below, from_above, side):
-    entry = (from_below.shape[0] - 1, side)
-    return jnp.concatenate(
-        [own[...], from_above[*entry, :, :TPATCH], from_below[*entry, :, :TPATCH]], axis=0
-    )
-
-
-def steps_kernel(diag, cross, turns, wall, *refs):
-    metric_halos, halos = refs[:4], refs[4:8]
-    parts, outs, rimmed = refs[8 : 8 + FIELDS], refs[-FIELDS - 1 : -1], refs[-1]
+
+
+def upwind(face, behind, ahead):
+    return face * jnp.where(face > 0.0, behind, ahead)
+
+
+def steps_kernel(skipped, total_rows, spot, rotation, diag, cross, *refs):
+    metric_halos, halos, parts = refs[:4], refs[4:8], refs[8 : 8 + FIELDS]
+    outs, done, rimmed, wall = refs[-FIELDS - 3 : -3], refs[-3], refs[-2], refs[-1]
+    done[...] = jnp.zeros_like(done)
     rows, cols = parts[0].shape[1:]
-    ext_cols = cols + TPATCH
-    l = pl.program_id(0)
-
-    @pl.when(l == 0)
+    ext_rows, ext_cols = rows + SUB, cols + TPATCH
+    panel_rows = total_rows // PANELS
+    l = skipped + pl.program_id(0)
+
+    def columns(below, above, *sides):
+        last = below.shape[0] - 1
+        corners = lambda n: [end[last, :, n * TPATCH : (n + 1) * TPATCH] for end in (above, below)]
+        return [jnp.concatenate([side[...]] + corners(n), axis=0) for n, side in enumerate(sides)]
+
+    def with_rim(core, above, below, lanes, sides):
+        return jnp.concatenate([jnp.concatenate([core, above, below], axis=0), rim_tile(lanes, *sides)], axis=1)
+
+    @pl.when(pl.program_id(0) == 0)
     def _():
-        below, above, *own = metric_halos
-        left, right = (columns(own[side], below, above, side) for side in range(2))
+        below, above = metric_halos[:2]
+        sides, entry = columns(*metric_halos), below.shape[0] - 1 - FIELDS
         for f in range(FIELDS):
-            tile = cross[...] if f == FIELDS - 1 else diag[f]
-            entry, lanes = (below.shape[0] - 2, f), TPATCH - (FIELDS - f) * HALO
-            rimmed[f] = with_rim(tile, entry, lanes, below, above, left, right)
-
-    below, above, *own = halos
-    left, right = (columns(own[side], below, above, side) for side in range(2))
+            core = cross[...] if f == FIELDS - 1 else diag[f]
+            lanes = TPATCH - (FIELDS - f) * HALO
+            rimmed[f] = with_rim(core, above[entry + f], below[entry + f], lanes, sides) * (COURANT * 0.5)
+        column = lax.broadcasted_iota(jnp.int32, wall.shape, 1)
+        walled = ((spot[2] == 0) & (column == 0)) | ((spot[2] == spot[3] - 1) & (column == cols))
+        wall[...] = jnp.where(walled, 0.0, 1.0)
+
+    turns = []
+    for edge in (0, rows):
+        upper = lax.rem(spot[1] * rows + edge, total_rows)
+        lower = lax.rem(upper + total_rows - 1, total_rows)
+        joint = lax.rem(upper, panel_rows) == 0
+        codes = [rotation[0, upper // panel_rows], rotation[1, lower // panel_rows]]
+        turns.append([factor for code in codes for factor in quarter_turn(jnp.where(joint, code, 0))])
+
+    sides = columns(*halos)
     depth, cov_first, cov_second = (
-        with_rim(parts[f][0], (l, f), (l * FIELDS + f) * HALO, below, above, left, right) for f in range(FIELDS)
-    )
-    cos_below, sin_below, cos_above, sin_above = (
-        jnp.concatenate([turns[i]] * (ext_cols // TPATCH), axis=1) for i in range(4)
+        with_rim(
+            parts[f][0], halos[1][l * FIELDS + f], halos[0][l * FIELDS + f], (l * FIELDS + f) * HALO, sides
+        )
+        for f in range(FIELDS)
     )
     before = lambda v, axis: pltpu.roll(v, 1, axis)
     after = lambda v, axis: pltpu.roll(v, v.shape[axis] - 1, axis)
+    piece = lambda v, start: v[start : start + SUB]
+    joints = ((0, rows, 0), (rows, rows - SUB, 1)), ((rows - SUB, rows, 1), (rows, 0, 0))
+    depth = depth * GRADIENT_HALF
     for _ in range(STEPS):
         con_first = rimmed[0] * cov_first + rimmed[2] * cov_second
         con_second = rimmed[2] * cov_first + rimmed[1] * cov_second
         depth_below, depth_above = before(depth, 0), after(depth, 0)
-        second_below = sin_below * before(con_first, 0) + cos_below * before(con_second, 0)
-        second_above = sin_above * after(con_first, 0) + cos_above * after(con_second, 0)
-        face_below = 0.5 * (con_second + second_below)
-        flux_below = jnp.maximum(face_below, 0.0) * depth_below + jnp.minimum(face_below, 0.0) * depth
-        face_above = 0.5 * (con_second + second_above)
-        flux_above = jnp.maximum(face_above, 0.0) * depth + jnp.minimum(face_above, 0.0) * depth_above
+        second_below = before(con_second, 0)
+        second_above = after(con_second, 0)
+        row = lax.broadcasted_iota(jnp.int32, (SUB, ext_cols), 0)
+        below, above = [], []
+        for at, source, joint in joints[0]:
+            turned = turns[joint][0] * piece(second_below, at) + turns[joint][1] * before(piece(con_first, source), 0)
+            below.append(jnp.where(row == 0, turned, piece(second_below, at)))
+        second_below = jnp.concatenate([below[0], second_below[SUB:rows], below[1]], axis=0)
+        flux_below = upwind(con_second + second_below, depth_below, depth)
+        for at, source, joint in joints[1]:
+            turned = turns[joint][2] * piece(second_above, at) + turns[joint][3] * after(piece(con_first, source), 0)
+            second = jnp.where(row == SUB - 1, turned, piece(second_above, at))
+            above.append(upwind(piece(con_second, at) + second, piece(depth, at), piece(depth_above, at)))
+        flux_above = jnp.concatenate([after(flux_below, 0)[: rows - SUB]] + above, axis=0)
         depth_left, depth_right = before(depth, 1), after(depth, 1)
-        face_left = 0.5 * (con_first + before(con_first, 1)) * wall[0:1, :]
-        flux_left = jnp.maximum(face_left, 0.0) * depth_left + jnp.minimum(face_left, 0.0) * depth
+        flux_left = upwind((con_first + before(con_first, 1)) * wall[0:1, :], depth_left, depth)
         flux_right = after(flux_left, 1)
-        depth = depth - COURANT * ((flux_right - flux_left) + (flux_above - flux_below))
-        cov_first = cov_first - GRADIENT * 0.5 * (depth_right - depth_left)
-        cov_second = cov_second - GRADIENT * 0.5 * (depth_above - depth_below)
-    for ref, value in zip(outs, (depth, cov_first, cov_second)):
+        cov_first = cov_first - (depth_right - depth_left)
+        cov_second = cov_second - (depth_above - depth_below)
+        depth = depth - ((flux_right - flux_left) + (flux_above - flux_below))
+    for ref, value in zip(outs, (depth * (1.0 / GRADIENT_HALF), cov_first, cov_second)):
         ref[0] = value[:rows, :cols]
 
 
-def steps(first, levels, total, diag, cross, turns, wall, metric_halos, halos, parts, so_far):
-    rows, cols = parts[0].shape[1:]
+def steps(first, count, skipped, total_rows, spot, rotation, diag, cross, metric_halos, halos, parts, so_far):
+    levels, rows, cols = parts[0].shape
+    assert total_rows // PANELS % rows == 0
     fixed = lambda array: pl.BlockSpec(array.shape, lambda l: (0,) * array.ndim)
-    of_level = lambda start: pl.BlockSpec((1, rows, cols), lambda l: (start + l, 0, 0))
-    given = (diag, cross, turns, wall, *metric_halos, *halos)
+    of_level = pl.BlockSpec((1, rows, cols), lambda l: (first + l, 0, 0))
+    given = (diag, cross, *metric_halos, *halos)
+    before = 2 + len(given) + len(parts)
     return pl.pallas_call(
-        steps_kernel,
-        grid=(levels,),
-        in_specs=[fixed(array) for array in given] + [of_level(0)] * FIELDS + in_hbm(len(so_far)),
-        out_specs=[of_level(first)] * FIELDS,
-        out_shape=[jax.ShapeDtypeStruct((total, rows, cols), jnp.float32)] * FIELDS,
-        input_output_aliases={len(given) + FIELDS + i: i for i in range(len(so_far))},
-        scratch_shapes=[pltpu.VMEM((FIELDS, rows + SUB, cols + TPATCH), jnp.float32)],
+        functools.partial(steps_kernel, skipped, total_rows),
+        grid=(count,),
+        in_specs=in_smem(2) + [fixed(array) for array in given] + [of_level] * FIELDS + in_hbm(len(so_far)),
+        out_specs=[of_level] * FIELDS + [pl.BlockSpec((SUB, TPATCH), lambda l: (0, 0))],
+        out_shape=[jax.ShapeDtypeStruct((levels, rows, cols), jnp.float32)] * FIELDS
+        + [jax.ShapeDtypeStruct((SUB, TPATCH), jnp.float32)],
+        input_output_aliases={before + i: i for i in range(len(so_far))},
+        scratch_shapes=[
+            pltpu.VMEM((FIELDS, rows + SUB, cols + TPATCH), jnp.float32),
+            pltpu.VMEM((SUB, cols + TPATCH), jnp.float32),
+        ],
         compiler_params=params(32 * 2**20),
-        cost_estimate=pl.CostEstimate(flops=0, bytes_accessed=levels * 4 * 2**20, transcendentals=0),
         name="steps",
-    )(*given, *parts, *so_far)
+    )(spot, rotation, *given, *parts, *so_far)
 
 
 def quarter_turn(code):
     cosine = (code == 0).astype(jnp.float32) - (code == 2).astype(jnp.float32)
     sine_value = (code == 1).astype(jnp.float32) - (code == 3).astype(jnp.float32)
     return (cosine, sine_value)
-
-
-def turn_factors(first_row, rows, total_rows, rotation):
-    index = jnp.arange(rows + SUB, dtype=jnp.int32)
-    index = jnp.where(index < rows + HALO, index, index - rows - SUB)
-    row = (first_row + index) % total_rows
-    panel_rows = total_rows // PANELS
-    matches = jnp.arange(PANELS, dtype=jnp.int32)[None, :] == (row // panel_rows)[:, None]
-    lower = jnp.sum(jnp.where(matches, rotation[0][None, :], 0), axis=1)
-    upper = jnp.sum(jnp.where(matches, rotation[1][None, :], 0), axis=1)
-    below = jnp.where(row % panel_rows == 0, lower, 0)
-    above = jnp.where(row % panel_rows == panel_rows - 1, upper, 0)
-    factors = jnp.stack(quarter_turn(below) + quarter_turn(above))
-    return jnp.broadcast_to(factors[:, :, None], factors.shape + (TPATCH,))
 
 
 def shift(array, axis, by, closed):
@@ -397,26 +456,28 @@
     send = lambda array, pairs: lax.ppermute(array, "ty", pairs)
 
     to_next = [(b, (b + 2) % ty_count) for b in range(ty_count)]
-    places_of = [slot_patch[0, 0]] + [shift(slot_patch[0, 0], "ty", -by, True) for by in (1, 2)]
-    odd = (ty_index % 2).reshape(1)
-
-    offsets = dest_offset[0, 0].T
+    places = slot_patch.reshape(owners, capacity)
+    places = (places % blocks) * rows + places // blocks
+    ahead = [shift(slot_patch.reshape(owners, capacity), "ty", -by, True) for by in (1, 2)]
+    spot = jnp.stack([ty_index % 2, ty_index, tx_index, jnp.int32(tx_count)])
+
+    offsets = dest_offset.transpose(0, 1, 3, 2).reshape(-1, dest_offset.shape[2])
     counts = [FIELDS * (last - first) for first, last in zip(bounds[:-1], bounds[1:])]
     wide = [bounds[pair[0]] for pair in PAIRS] + [levels]
     cuts = [bounds, wide] + [bounds] * (owners - 3) + [wide]
     own, first, second, far = terms(cuts, capacity, offsets, increments, remap_weights)
-    *far, places_of[1], places_of[2] = together(*far, places_of[1], places_of[2])
-    places, places_next, places_second = ((p % blocks) * rows + p // blocks for p in places_of)
-    turns = turn_factors(ty_index * rows, rows, rows * ty_count, rotation)
-    column = jnp.arange(cols + TPATCH, dtype=jnp.int32)
-    column = tx_index * cols + jnp.where(column < cols + TPATCH // 2, column, column - cols - TPATCH)
-    wall = jnp.where((column == 0) | (column == cols * tx_count), 0.0, 1.0).astype(jnp.float32)
-    wall = jnp.broadcast_to(wall[None, :], (SUB, cols + TPATCH))
-
+    *far, ahead[0], ahead[1] = together(*far, *ahead)
+    places_next, places_second = ((p % blocks) * rows + p // blocks for p in ahead)
     thirds = [send(slots, to_next) for slots in far]
-    token, payload = odd, None
-    across, last, settled, found, edges, pending = {}, {}, {}, {}, {}, []
-    for step in ORDER.split():
+    metric = (inv_metric_diag, inv_metric_cross)
+    token, results, finished = spot, [], []
+
+    def steps_on(n, first, count, results):
+        skipped = first - bounds[GROUPS[n][0]]
+        return steps(first, count, skipped, rows * ty_count, spot, rotation, *metric, halos[0], halos[n], fields, results)
+
+    across, last, settled, ends, sides, fields, halos = {}, {}, {}, {}, {}, [], []
+    for step in ORDER:
         kind, n = step[0], int(step[1:])
         if kind == "P":
             chunks = PAIRS[n]
@@ -424,8 +485,6 @@
             token, *paired = together(token, *paired)
             for j, part in zip(chunks, paired):
                 across[j] = send(part, swap)
-            if n == 0:
-                token, turns, wall = together(token, turns, wall)
         elif kind == "J":
             (joined,) = patch_sums(token, places_second, [second[n]], (2,), patches, [counts[n]], across[n], 0)
             token, joined = together(token, joined)
@@ -435,36 +494,30 @@
             token, settled[n] = together(token, settled[n])
         elif kind == "F":
             (g,) = (i for i, group in enumerate(GROUPS) if n in group)
-            begin, total = bounds[GROUPS[g][0]], bounds[GROUPS[g][-1] + 1] - bounds[GROUPS[g][0]]
+            begin = bounds[GROUPS[g][0]]
+            place = (bounds[n], begin, bounds[GROUPS[g][-1] + 1] - begin, 1 if g else 1 + FIELDS)
             token, ready = together(token, settled[n])
-            found[g], edges[g] = first_fields(
-                begin, bounds[n], bounds[n + 1] - bounds[n], total, patches, ready, last[n], basis, thickness,
-                wind_first, wind_second, (inv_metric_diag, inv_metric_cross), edges.get(g), found.get(g, []),
+            fields, ends[g], sides[g] = first_fields(
+                place, bounds[n + 1] - bounds[n], patches, ready, last[n], basis, thickness, wind_first, wind_second,
+                metric, sides.get(g), fields, ends.get(g, []),
+                halos[0] if g and n in LATE else [],
             )
-            token, *edges[g] = together(token, *edges[g])
+            token, *sides[g] = together(token, *sides[g])
         else:
-            begin, total = bounds[GROUPS[n][0]], bounds[GROUPS[n][-1] + 1] - bounds[GROUPS[n][0]]
-            *fields, low_rows, high_rows = found[n]
-            low_cols, high_cols = edges[n]
-            from_left = shift(high_cols, "tx", 1, False)
-            from_right = shift(low_cols, "tx", -1, False)
-
-            def ends(entries, at):
-                metric = jnp.concatenate([inv_metric_diag, inv_metric_cross[None]], axis=0)[:, at : at + HALO]
-                corners = jnp.stack([side[at : at + HALO] for side in (from_left, from_right)])
-                corners = jnp.pad(corners, ((0, FIELDS - 2), (0, 0), (0, cols - TPATCH)))
-                return entries.at[total].set(metric).at[total + 1].set(corners)
-
-            payload = (ends(high_rows, rows - HALO), ends(low_rows, 0))
-            halos = (shift(payload[0], "ty", 1, True), shift(payload[1], "ty", -1, True), from_left, from_right)
-            token, *halos = together(token, *halos)
-            pending.append((begin, total, halos, fields))
-
-    results, metric_halos = [], pending[0][2]
-    for n, (begin, total, halos, fields) in enumerate(pending):
-        results = steps(
-            begin, total, levels, inv_metric_diag, inv_metric_cross, turns, wall, metric_halos, halos, fields, results
-        )
+            low_cols, high_cols = sides[n]
+            beside = [shift(high_cols, "tx", 1, False), shift(low_cols, "tx", -1, False)]
+
+            if n == len(GROUPS) - 1:
+                for first, count in EARLY:
+                    *results, finished = steps_on(0, first, count, results)
+                    finished = [finished]
+            high_rows, low_rows = reversed(last_entries(1 if n else 1 + FIELDS, ends[n], *metric, beside, finished))
+            halos.append([shift(high_rows, "ty", 1, True), shift(low_rows, "ty", -1, True), *beside])
+
+    done = EARLY[-1][0] + EARLY[-1][1] if EARLY else 0
+    for n, group in enumerate(GROUPS):
+        first, end = max(done, bounds[group[0]]), bounds[group[-1] + 1]
+        *results, _ = steps_on(n, first, end - first, results)
     return tuple(results)
 
 

time: 119 us -> 115 us (0.966)
  waiting for transfers between devices: 47 us -> 27.5 us
  starting transfers between devices: 18.7 us -> 30.9 us
  Pallas kernels: 41.3 us -> 44.7 us
    ppermute x12, waiting for transfers between devices: 36.6 us -> 24 us  [body(): send = lambda array, pairs: lax.ppermute(array, 'ty', pairs)]
    ppermute x6 -> x10, starting transfers between devices: 15.2 us -> 27.4 us  [shift(): return lax.ppermute(array, axis, pairs)]
    ppermute x6 -> x10, waiting for transfers between devices: 10.4 us -> 3.53 us  [shift(): return lax.ppermute(array, axis, pairs)]
    pallas_call x1 -> x5, Pallas kernels: 9.79 us -> 12.3 us  [the longest x3 12.3 us: steps(): pl.pallas_call(functools.partial(steps_kernel, skipped, total_rows), grid...]
    unnamed x38 -> x40, local copies, waits for them, and re-layouts: 9.77 us -> 9.77 us
  transfers between devices with their start and end apart: 18 -> 22, of which waited for: 10 -> 7; matrix products, arithmetic and copies ran while one was open for 1% -> 0% of each run, Pallas kernels for 26% -> 34%
where the time goes in v3:
time: 115 us; the launch traced here: 114 us
  Pallas kernels  44.7 us (39%)
  starting transfers between devices  30.9 us (27%)
  waiting for transfers between devices  27.5 us (24%)
  local copies, waits for them, and re-layouts  9.77 us (8%)
    ppermute x10, starting transfers between devices, shift(): return lax.ppermute(array, axis, pairs)  27.4 us
    ppermute x12, waiting for transfers between devices, body(): send = lambda array, pairs: lax.ppermute(array, 'ty', pairs)  24 us
    pallas_call x12, Pallas kernels, patch_sums(): pl.pallas_call(functools.partial(sum_kernel, which, parity, patches), in_...  18.3 us
    pallas_call x3, Pallas kernels, steps(): pl.pallas_call(functools.partial(steps_kernel, skipped, total_rows), grid...  12.3 us
    pallas_call x1, Pallas kernels, terms(): pl.pallas_call(functools.partial(terms_kernel, cuts, group, capacity), in...  12 us
    unnamed x40, local copies, waits for them, and re-layouts  9.77 us
    ppermute x10, waiting for transfers between devices, shift(): return lax.ppermute(array, axis, pairs)  3.53 us
    ppermute x12, starting transfers between devices, body(): send = lambda array, pairs: lax.ppermute(array, 'ty', pairs)  3.48 us
  transfers between devices with their start and end apart: 22, of which 7 were waited for; matrix products, arithmetic and copies ran while one was open for 0% of the time, Pallas kernels for 34%

profile of v3, /device:TPU:1, one launch (start us, length us, event | category | flops | bytes accessed | tf_op | source)
XLA Modules:
  0.0 114.1 jit_solution(9414360047901279088)
XLA Ops:
  0.7 5.1 %collective-permute-start = (s32[4,108]{1,0:T(4,128)}, s32[4,108]{1,0:T(4,128)S(1)}, u32[]{:S(2)}, u32[]{:S(2)}) collective-permute-start(s32[4,108]{1,0:T(4,128)} %bitcast.10), channel_id=1, source_target_pairs={{0,7},{1,0},{2,1},{3,2},{4,3},{5,4},{6,5},{7,6},{8,15},{9,8},{10,9... | collective-permute-start | bytes 5192 | tf_op jit(solution)/shard_map/ppermute | solution.py:423
  6.0 12.0 %terms.1 = (f32[648,128]{1,0:T(8,128)}, f32[648,128]{1,0:T(8,128)}, f32[648,128]{1,0:T(8,128)}, f32[648,128]{1,0:T(8,128)}, f32[648,128]{1,0:T(8,128)}, /*index=...) custom-call(s32[2,144]{1,0:T(2,128)} %bitcast.12, ...), custom_call_target="tpu_custom_call" | custom-call | bytes 18874368 | tf_op jit(solution)/shard_map/terms/pallas_call | solution.py:121
  18.1 1.4 %collective-permute-start.2 = (f32[648,128]{1,0:T(8,128)}, f32[648,128]{1,0:T(8,128)S(1)}, u32[]{:S(2)}, u32[]{:S(2)}) collective-permute-start(f32[648,128]{1,0:T(8,128)} %get-tuple-element.106), channel_id=1, source_target_pairs={{0,2},{1,3},{2,4},{3,5},{4,6},{5,7},{6,0},{7,1},{8,10},{9,11},{10,... | collective-permute-start | bytes 995336 | tf_op jit(solution)/shard_map/ppermute | solution.py:456
  19.6 8.6 %collective-permute-done.2.refs_0_ = f32[648,128]{1,0:T(8,128)S(1)} collective-permute-done((f32[648,128]{1,0:T(8,128)}, f32[648,128]{1,0:T(8,128)S(1)}, u32[]{:S(2)}, u32[]{:S(2)}) %collective-permute-start.2) | collective-permute-done | bytes 331808 | tf_op jit(solution)/shard_map/ppermute | solution.py:456
  29.2 2.0 %patch_sums.12 = f32[864,128]{1,0:T(8,128)S(1)} custom-call(s32[4]{0:T(128)S(1)} %pad_add_fusion.odd.spot, s32[4,108]{1,0:T(4,128)S(1)} %fusion.2.places, f32[648,128]{1,0:T(8,128)S(1)} %collective-permute-done.2.refs_0_, f32[648,128]{1,0:T(8,128)S(1)} %copy-done.17), custom_call_target="tpu_custom_call" | custom-call | tf_op jit(solution)/shard_map/patch_sums/pallas_call | solution.py:183
  31.6 3.7 %collective-permute-done.3.refs_0_ = f32[648,128]{1,0:T(8,128)S(1)} collective-permute-done((f32[648,128]{1,0:T(8,128)}, f32[648,128]{1,0:T(8,128)S(1)}, u32[]{:S(2)}, u32[]{:S(2)}) %collective-permute-start.3) | collective-permute-done | bytes 331808 | tf_op jit(solution)/shard_map/ppermute | solution.py:456
  36.3 2.0 %patch_sums.13 = f32[864,128]{1,0:T(8,128)S(1)} custom-call(s32[4]{0:T(128)S(1)} %pad_add_fusion.odd.spot, s32[4,108]{1,0:T(4,128)S(1)} %fusion.2.places, f32[648,128]{1,0:T(8,128)S(1)} %collective-permute-done.3.refs_0_, f32[648,128]{1,0:T(8,128)S(1)} %copy-done.16), custom_call_target="tpu_custom_call" | custom-call | tf_op jit(solution)/shard_map/patch_sums/pallas_call | solution.py:183
  38.7 3.7 %collective-permute-done.4.refs_0_ = f32[648,128]{1,0:T(8,128)S(1)} collective-permute-done((f32[648,128]{1,0:T(8,128)}, f32[648,128]{1,0:T(8,128)S(1)}, u32[]{:S(2)}, u32[]{:S(2)}) %collective-permute-start.4) | collective-permute-done | bytes 331808 | tf_op jit(solution)/shard_map/ppermute | solution.py:456
  43.4 2.0 %patch_sums.14 = f32[864,128]{1,0:T(8,128)S(1)} custom-call(s32[4]{0:T(128)S(1)} %pad_add_fusion.odd.spot, s32[4,108]{1,0:T(4,128)S(1)} %fusion.2.places, f32[648,128]{1,0:T(8,128)S(1)} %collective-permute-done.4.refs_0_, f32[648,128]{1,0:T(8,128)S(1)} %copy-done.15), custom_call_target="tpu_custom_call" | custom-call | tf_op jit(solution)/shard_map/patch_sums/pallas_call | solution.py:183
  50.5 2.0 %patch_sums.16 = f32[864,128]{1,0:T(8,128)S(1)} custom-call(s32[4]{0:T(128)S(1)} %pad_add_fusion.odd.spot, s32[4,108]{1,0:T(4,128)S(1)} %fusion.2.places, f32[648,128]{1,0:T(8,128)S(1)} %collective-permute-done.6.refs_0_, f32[648,128]{1,0:T(8,128)S(1)} %copy-done.13), custom_call_target="tpu_custom_call" | custom-call | tf_op jit(solution)/shard_map/patch_sums/pallas_call | solution.py:183
  53.9 1.3 %patch_sums.17 = f32[864,128]{1,0:T(8,128)S(1)} custom-call(s32[4]{0:T(128)S(1)} %pad_add_fusion.odd.spot, s32[4,108]{1,0:T(4,128)S(1)} %fusion.1.places, f32[648,128]{1,0:T(8,128)S(1)} %copy-done.12, f32[864,128]{1,0:T(8,128)S(1)} %collective-permute-done.7.refs_1_), custom_call_target="tpu_custom_call" | custom-call | tf_op jit(solution)/shard_map/patch_sums/pallas_call | solution.py:183
  61.1 1.4 %patch_sums.20 = f32[864,128]{1,0:T(8,128)S(1)} custom-call(s32[4]{0:T(128)S(1)} %pad_add_fusion.odd.spot, s32[4,108]{1,0:T(4,128)S(1)} %fusion.1.places, f32[648,128]{1,0:T(8,128)S(1)} %copy-done.9, f32[864,128]{1,0:T(8,128)S(1)} %collective-permute-done.9.refs_1_), custom_call_target="tpu_custom_call" | custom-call | tf_op jit(solution)/shard_map/patch_sums/pallas_call | solution.py:183
  63.1 6.4 %collective-permute-done.15.refs_1_ = f32[864,128]{1,0:T(8,128)S(1)} collective-permute-done((f32[864,128]{1,0:T(8,128)S(1)}, f32[864,128]{1,0:T(8,128)S(1)}, u32[]{:S(2)}, u32[]{:S(2)}) %collective-permute-start.15) | collective-permute-done | bytes 442400 | tf_op jit(solution)/shard_map/ppermute | solution.py:456
  70.5 1.4 %patch_sums.21 = f32[864,128]{1,0:T(8,128)S(1)} custom-call(s32[4]{0:T(128)S(1)} %pad_add_fusion.odd.spot, s32[4,108]{1,0:T(4,128)S(1)} %fusion.1.places, f32[648,128]{1,0:T(8,128)S(1)} %copy-done.8, f32[864,128]{1,0:T(8,128)S(1)} %collective-permute-done.15.refs_1_), custom_call_target="tpu_custom_call" | custom-call | tf_op jit(solution)/shard_map/patch_sums/pallas_call | solution.py:183
  72.5 5.7 %collective-permute-start.11 = (f32[48,128]{1,0:T(8,128)S(1)}, f32[48,128]{1,0:T(8,128)S(1)}, u32[]{:S(2)}, u32[]{:S(2)}) collective-permute-start(f32[48,128]{1,0:T(8,128)S(1)} %get-tuple-element.149), channel_id=1, source_target_pairs={{0,8},{8,16},{16,24},{1,9},{9,17},{17,25},{2,10},{10,18},{18,26},{... | collective-permute-start | bytes 73736 | tf_op jit(solution)/shard_map/ppermute | solution.py:423
  78.2 1.9 %collective-permute-start.12 = (f32[48,128]{1,0:T(8,128)S(1)}, f32[48,128]{1,0:T(8,128)S(1)}, u32[]{:S(2)}, u32[]{:S(2)}) collective-permute-start(f32[48,128]{1,0:T(8,128)S(1)} %get-tuple-element.150), channel_id=1, source_target_pairs={{8,0},{16,8},{24,16},{9,1},{17,9},{25,17},{10,2},{18,10},{26,18},{... | collective-permute-start | bytes 73736 | tf_op jit(solution)/shard_map/ppermute | solution.py:423
  80.1 3.5 %collective-permute-done.12.right.refs_3_.refs_7_ = f32[48,128]{1,0:T(8,128)S(1)} collective-permute-done((f32[48,128]{1,0:T(8,128)S(1)}, f32[48,128]{1,0:T(8,128)S(1)}, u32[]{:S(2)}, u32[]{:S(2)}) %collective-permute-start.12) | collective-permute-done | bytes 24608 | tf_op jit(solution)/shard_map/ppermute | solution.py:423
  84.5 3.4 %collective-permute-start.14 = (f32[16,4,384]{2,1,0:T(4,128)S(1)}, f32[16,4,384]{2,1,0:T(4,128)S(1)}, u32[]{:S(2)}, u32[]{:S(2)}) collective-permute-start(f32[16,4,384]{2,1,0:T(4,128)S(1)} %get-tuple-element.154), channel_id=1, source_target_pairs={{0,7},{1,0},{2,1},{3,2},{4,3},{5,4},{6,5},{7,6},{8,15},{9,8},{10,9... | collective-permute-start | bytes 294920 | tf_op jit(solution)/shard_map/ppermute | solution.py:423
  91.5 4.1 %collective-permute-start.18 = (f32[48,128]{1,0:T(8,128)S(1)}, f32[48,128]{1,0:T(8,128)S(1)}, u32[]{:S(2)}, u32[]{:S(2)}) collective-permute-start(f32[48,128]{1,0:T(8,128)S(1)} %get-tuple-element.180), channel_id=1, source_target_pairs={{0,8},{8,16},{16,24},{1,9},{9,17},{17,25},{2,10},{10,18},{18,26},{... | collective-permute-start | bytes 73736 | tf_op jit(solution)/shard_map/ppermute | solution.py:423
  95.6 1.9 %collective-permute-start.19 = (f32[48,128]{1,0:T(8,128)S(1)}, f32[48,128]{1,0:T(8,128)S(1)}, u32[]{:S(2)}, u32[]{:S(2)}) collective-permute-start(f32[48,128]{1,0:T(8,128)S(1)} %get-tuple-element.181), channel_id=1, source_target_pairs={{8,0},{16,8},{24,16},{9,1},{17,9},{25,17},{10,2},{18,10},{26,18},{... | collective-permute-start | bytes 73736 | tf_op jit(solution)/shard_map/ppermute | solution.py:423
  97.6 3.4 %steps.3 = (f32[8,48,384]{2,1,0:T(8,128)}, f32[8,48,384]{2,1,0:T(8,128)}, f32[8,48,384]{2,1,0:T(8,128)}, f32[8,128]{1,0:T(8,128)S(1)}) custom-call(s32[4]{0:T(128)S(1)} %pad_add_fusion.odd.spot, s32[2,4]{1,0:T(2,128)S(1)} %copy-done.18, f32[2,48,384]{2,1,0:T(8,128)S(1)} %copy-done.3, f32[48,384]{1,0:T(8,128)S(1)} %copy-done.5, ...), custom_call_target="tpu_custom_call" | custom-call | tf_op jit(solution)/shard_map/steps/pallas_call | solution.py:397
  102.1 3.2 %collective-permute-start.21 = (f32[13,4,384]{2,1,0:T(4,128)S(1)}, f32[13,4,384]{2,1,0:T(4,128)S(1)}, u32[]{:S(2)}, u32[]{:S(2)}) collective-permute-start(f32[13,4,384]{2,1,0:T(4,128)S(1)} %get-tuple-element.189), channel_id=1, source_target_pairs={{0,7},{1,0},{2,1},{3,2},{4,3},{5,4},{6,5},{7,6},{8,15},{9,8},{10,9... | collective-permute-start | bytes 239624 | tf_op jit(solution)/shard_map/ppermute | solution.py:423
  105.3 3.4 %steps.4 = (f32[8,48,384]{2,1,0:T(8,128)}, f32[8,48,384]{2,1,0:T(8,128)}, f32[8,48,384]{2,1,0:T(8,128)}, f32[8,128]{1,0:T(8,128)}) custom-call(s32[4]{0:T(128)S(1)} %pad_add_fusion.odd.spot, s32[2,4]{1,0:T(2,128)S(1)} %copy-done.18, f32[2,48,384]{2,1,0:T(8,128)S(1)} %copy-done.3, ...), custom_call_target="tpu_custom_call", output_to_operand_aliasing={{0}: (15, {}), {1}: (16, {}), {2}: (17, {})} | custom-call | tf_op jit(solution)/shard_map/steps/pallas_call | solution.py:397
  108.6 5.5 %steps.5 = (f32[8,48,384]{2,1,0:T(8,128)}, f32[8,48,384]{2,1,0:T(8,128)}, f32[8,48,384]{2,1,0:T(8,128)}, f32[8,128]{1,0:T(8,128)}) custom-call(s32[4]{0:T(128)S(1)} %pad_add_fusion.odd.spot, s32[2,4]{1,0:T(2,128)S(1)} %copy-done.18, f32[2,48,384]{2,1,0:T(8,128)S(1)} %copy-done.3, ...), custom_call_target="tpu_custom_call", output_to_operand_aliasing={{0}: (15, {}), {1}: (16, {}), {2}: (17, {})} | custom-call | tf_op jit(solution)/shard_map/steps/pallas_call | solution.py:397
  (86 shorter events, 24.1 us)
Async XLA Ops:
  0.7 17.4 %collective-permute-start = (s32[4,108]{1,0:T(4,128)}, s32[4,108]{1,0:T(4,128)S(1)}, u32[]{:S(2)}, u32[]{:S(2)}) collective-permute-start(s32[4,108]{1,0:T(4,128)} %bitcast.10), channel_id=1, source_target_pairs={{0,7},{1,0},{2,1},{3,2},{4,3},{5,4},{6,5},{7,6},{8,15},{9,8},{10,9... | collective-permute-start | bytes 5192 | tf_op jit(solution)/shard_map/ppermute | solution.py:423
  5.8 12.3 %collective-permute-start.1 = (s32[4,108]{1,0:T(4,128)}, s32[4,108]{1,0:T(4,128)S(1)}, u32[]{:S(2)}, u32[]{:S(2)}) collective-permute-start(s32[4,108]{1,0:T(4,128)} %bitcast.11), channel_id=1, source_target_pairs={{0,6},{1,7},{2,0},{3,1},{4,2},{5,3},{6,4},{7,5},{8,14},{9,15},{10,... | collective-permute-start | bytes 5192 | tf_op jit(solution)/shard_map/ppermute | solution.py:423
  6.0 91.6 %copy-start.18 = (s32[2,4]{1,0:T(2,128)S(1)}, s32[2,4]{1,0:T(2,128)}, u32[]{:S(2)}) copy-start(s32[2,4]{1,0:T(2,128)} %rotation.5) | copy-start | bytes 100
  18.1 71.7 %copy-start.6 = (f32[648,128]{1,0:T(8,128)S(1)}, f32[648,128]{1,0:T(8,128)}, u32[]{:S(2)}) copy-start(f32[648,128]{1,0:T(8,128)} %get-tuple-element.161.refs_0_) | copy-start | bytes 995332
  18.1 10.1 %collective-permute-start.2 = (f32[648,128]{1,0:T(8,128)}, f32[648,128]{1,0:T(8,128)S(1)}, u32[]{:S(2)}, u32[]{:S(2)}) collective-permute-start(f32[648,128]{1,0:T(8,128)} %get-tuple-element.106), channel_id=1, source_target_pairs={{0,2},{1,3},{2,4},{3,5},{4,6},{5,7},{6,0},{7,1},{8,10},{9,11},{10,... | collective-permute-start | bytes 995336 | tf_op jit(solution)/shard_map/ppermute | solution.py:456
  19.5 15.8 %collective-permute-start.3 = (f32[648,128]{1,0:T(8,128)}, f32[648,128]{1,0:T(8,128)S(1)}, u32[]{:S(2)}, u32[]{:S(2)}) collective-permute-start(f32[648,128]{1,0:T(8,128)} %get-tuple-element.109), channel_id=1, source_target_pairs={{0,2},{1,3},{2,4},{3,5},{4,6},{5,7},{6,0},{7,1},{8,10},{9,11},{10,... | collective-permute-start | bytes 995336 | tf_op jit(solution)/shard_map/ppermute | solution.py:456
  19.6 22.9 %collective-permute-start.4 = (f32[648,128]{1,0:T(8,128)}, f32[648,128]{1,0:T(8,128)S(1)}, u32[]{:S(2)}, u32[]{:S(2)}) collective-permute-start(f32[648,128]{1,0:T(8,128)} %get-tuple-element.112), channel_id=1, source_target_pairs={{0,2},{1,3},{2,4},{3,5},{4,6},{5,7},{6,0},{7,1},{8,10},{9,11},{10,... | collective-permute-start | bytes 995336 | tf_op jit(solution)/shard_map/ppermute | solution.py:456
  31.2 14.7 %collective-permute-start.5 = (f32[864,128]{1,0:T(8,128)S(1)}, f32[864,128]{1,0:T(8,128)S(1)}, u32[]{:S(2)}, u32[]{:S(2)}) collective-permute-start(f32[864,128]{1,0:T(8,128)S(1)} %patch_sums.12), channel_id=1, source_target_pairs={{0,1},{2,3},{4,5},{6,7},{1,0},{3,2},{5,4},{7,6},{8,9},{10,11},{12,... | collective-permute-start | bytes 1327112 | tf_op jit(solution)/shard_map/ppermute | solution.py:456
  31.6 17.9 %collective-permute-start.6 = (f32[648,128]{1,0:T(8,128)}, f32[648,128]{1,0:T(8,128)S(1)}, u32[]{:S(2)}, u32[]{:S(2)}) collective-permute-start(f32[648,128]{1,0:T(8,128)} %get-tuple-element.119), channel_id=1, source_target_pairs={{0,2},{1,3},{2,4},{3,5},{4,6},{5,7},{6,0},{7,1},{8,10},{9,11},{10,... | collective-permute-start | bytes 995336 | tf_op jit(solution)/shard_map/ppermute | solution.py:456
  38.3 14.7 %collective-permute-start.7 = (f32[864,128]{1,0:T(8,128)S(1)}, f32[864,128]{1,0:T(8,128)S(1)}, u32[]{:S(2)}, u32[]{:S(2)}) collective-permute-start(f32[864,128]{1,0:T(8,128)S(1)} %patch_sums.13), channel_id=1, source_target_pairs={{0,1},{2,3},{4,5},{6,7},{1,0},{3,2},{5,4},{7,6},{8,9},{10,11},{12,... | collective-permute-start | bytes 1327112 | tf_op jit(solution)/shard_map/ppermute | solution.py:456
  45.4 14.7 %collective-permute-start.9 = (f32[864,128]{1,0:T(8,128)S(1)}, f32[864,128]{1,0:T(8,128)S(1)}, u32[]{:S(2)}, u32[]{:S(2)}) collective-permute-start(f32[864,128]{1,0:T(8,128)S(1)} %patch_sums.14), channel_id=1, source_target_pairs={{0,1},{2,3},{4,5},{6,7},{1,0},{3,2},{5,4},{7,6},{8,9},{10,11},{12,... | collective-permute-start | bytes 1327112 | tf_op jit(solution)/shard_map/ppermute | solution.py:456
  48.2 14.3 %collective-permute-start.10 = (f32[864,128]{1,0:T(8,128)S(1)}, f32[864,128]{1,0:T(8,128)S(1)}, u32[]{:S(2)}, u32[]{:S(2)}) collective-permute-start(f32[864,128]{1,0:T(8,128)S(1)} %patch_sums.15), channel_id=1, source_target_pairs={{0,2},{1,3},{2,4},{3,5},{4,6},{5,7},{6,0},{7,1},{8,10},{9,11},{10,... | collective-permute-start | bytes 1327112 | tf_op jit(solution)/shard_map/ppermute | solution.py:456
  52.5 17.1 %collective-permute-start.15 = (f32[864,128]{1,0:T(8,128)S(1)}, f32[864,128]{1,0:T(8,128)S(1)}, u32[]{:S(2)}, u32[]{:S(2)}) collective-permute-start(f32[864,128]{1,0:T(8,128)S(1)} %patch_sums.16), channel_id=1, source_target_pairs={{0,1},{2,3},{4,5},{6,7},{1,0},{3,2},{5,4},{7,6},{8,9},{10,11},{12,... | collective-permute-start | bytes 1327112 | tf_op jit(solution)/shard_map/ppermute | solution.py:456
  55.3 16.7 %collective-permute-start.8 = (f32[864,128]{1,0:T(8,128)S(1)}, f32[864,128]{1,0:T(8,128)S(1)}, u32[]{:S(2)}, u32[]{:S(2)}) collective-permute-start(f32[864,128]{1,0:T(8,128)S(1)} %patch_sums.17), channel_id=1, source_target_pairs={{0,2},{1,3},{2,4},{3,5},{4,6},{5,7},{6,0},{7,1},{8,10},{9,11},{10,... | collective-permute-start | bytes 1327112 | tf_op jit(solution)/shard_map/ppermute | solution.py:456
  62.4 26.7 %collective-permute-start.17 = (f32[864,128]{1,0:T(8,128)S(1)}, f32[864,128]{1,0:T(8,128)S(1)}, u32[]{:S(2)}, u32[]{:S(2)}) collective-permute-start(f32[864,128]{1,0:T(8,128)S(1)} %patch_sums.20), channel_id=1, source_target_pairs={{0,2},{1,3},{2,4},{3,5},{4,6},{5,7},{6,0},{7,1},{8,10},{9,11},{10,... | collective-permute-start | bytes 1327112 | tf_op jit(solution)/shard_map/ppermute | solution.py:456
  71.9 19.1 %collective-permute-start.16 = (f32[864,128]{1,0:T(8,128)S(1)}, f32[864,128]{1,0:T(8,128)S(1)}, u32[]{:S(2)}, u32[]{:S(2)}) collective-permute-start(f32[864,128]{1,0:T(8,128)S(1)} %patch_sums.21), channel_id=1, source_target_pairs={{0,2},{1,3},{2,4},{3,5},{4,6},{5,7},{6,0},{7,1},{8,10},{9,11},{10,... | collective-permute-start | bytes 1327112 | tf_op jit(solution)/shard_map/ppermute | solution.py:456
  72.5 7.7 %collective-permute-start.11 = (f32[48,128]{1,0:T(8,128)S(1)}, f32[48,128]{1,0:T(8,128)S(1)}, u32[]{:S(2)}, u32[]{:S(2)}) collective-permute-start(f32[48,128]{1,0:T(8,128)S(1)} %get-tuple-element.149), channel_id=1, source_target_pairs={{0,8},{8,16},{16,24},{1,9},{9,17},{17,25},{2,10},{10,18},{18,26},{... | collective-permute-start | bytes 73736 | tf_op jit(solution)/shard_map/ppermute | solution.py:423
  78.2 5.4 %collective-permute-start.12 = (f32[48,128]{1,0:T(8,128)S(1)}, f32[48,128]{1,0:T(8,128)S(1)}, u32[]{:S(2)}, u32[]{:S(2)}) collective-permute-start(f32[48,128]{1,0:T(8,128)S(1)} %get-tuple-element.150), channel_id=1, source_target_pairs={{8,0},{16,8},{24,16},{9,1},{17,9},{25,17},{10,2},{18,10},{26,18},{... | collective-permute-start | bytes 73736 | tf_op jit(solution)/shard_map/ppermute | solution.py:423
  83.7 13.9 %collective-permute-start.13 = (f32[16,4,384]{2,1,0:T(4,128)S(1)}, f32[16,4,384]{2,1,0:T(4,128)S(1)}, u32[]{:S(2)}, u32[]{:S(2)}) collective-permute-start(f32[16,4,384]{2,1,0:T(4,128)S(1)} %get-tuple-element.153), channel_id=1, source_target_pairs={{0,1},{1,2},{2,3},{3,4},{4,5},{5,6},{6,7},{7,0},{8,9},{9,10},{10,1... | collective-permute-start | bytes 294920 | tf_op jit(solution)/shard_map/ppermute | solution.py:423
  84.5 13.1 %collective-permute-start.14 = (f32[16,4,384]{2,1,0:T(4,128)S(1)}, f32[16,4,384]{2,1,0:T(4,128)S(1)}, u32[]{:S(2)}, u32[]{:S(2)}) collective-permute-start(f32[16,4,384]{2,1,0:T(4,128)S(1)} %get-tuple-element.154), channel_id=1, source_target_pairs={{0,7},{1,0},{2,1},{3,2},{4,3},{5,4},{6,5},{7,6},{8,15},{9,8},{10,9... | collective-permute-start | bytes 294920 | tf_op jit(solution)/shard_map/ppermute | solution.py:423
  91.5 9.5 %collective-permute-start.18 = (f32[48,128]{1,0:T(8,128)S(1)}, f32[48,128]{1,0:T(8,128)S(1)}, u32[]{:S(2)}, u32[]{:S(2)}) collective-permute-start(f32[48,128]{1,0:T(8,128)S(1)} %get-tuple-element.180), channel_id=1, source_target_pairs={{0,8},{8,16},{16,24},{1,9},{9,17},{17,25},{2,10},{10,18},{18,26},{... | collective-permute-start | bytes 73736 | tf_op jit(solution)/shard_map/ppermute | solution.py:423
  95.6 5.4 %collective-permute-start.19 = (f32[48,128]{1,0:T(8,128)S(1)}, f32[48,128]{1,0:T(8,128)S(1)}, u32[]{:S(2)}, u32[]{:S(2)}) collective-permute-start(f32[48,128]{1,0:T(8,128)S(1)} %get-tuple-element.181), channel_id=1, source_target_pairs={{8,0},{16,8},{24,16},{9,1},{17,9},{25,17},{10,2},{18,10},{26,18},{... | collective-permute-start | bytes 73736 | tf_op jit(solution)/shard_map/ppermute | solution.py:423
  101.0 7.6 %collective-permute-start.20 = (f32[13,4,384]{2,1,0:T(4,128)S(1)}, f32[13,4,384]{2,1,0:T(4,128)S(1)}, u32[]{:S(2)}, u32[]{:S(2)}) collective-permute-start(f32[13,4,384]{2,1,0:T(4,128)S(1)} %get-tuple-element.188), channel_id=1, source_target_pairs={{0,1},{1,2},{2,3},{3,4},{4,5},{5,6},{6,7},{7,0},{8,9},{9,10},{10,1... | collective-permute-start | bytes 239624 | tf_op jit(solution)/shard_map/ppermute | solution.py:423
  102.1 6.5 %collective-permute-start.21 = (f32[13,4,384]{2,1,0:T(4,128)S(1)}, f32[13,4,384]{2,1,0:T(4,128)S(1)}, u32[]{:S(2)}, u32[]{:S(2)}) collective-permute-start(f32[13,4,384]{2,1,0:T(4,128)S(1)} %get-tuple-element.189), channel_id=1, source_target_pairs={{0,7},{1,0},{2,1},{3,2},{4,3},{5,4},{6,5},{7,6},{8,15},{9,8},{10,9... | collective-permute-start | bytes 239624 | tf_op jit(solution)/shard_map/ppermute | solution.py:423
  (18 other events, 505.4 us)

commit v4 on v3

--- a/solution.py
+++ b/solution.py
@@ -25,7 +25,7 @@
     "P0", "P1", "P2", "J0", "P3", "J1", "S0", "S1", "J2", "F0", "J3", "S2", "S3", "F1", "F2", "H0", "F3", "H1",
 )
 GROUP = 16
-VMEM = 61 * 2**20
+VMEM = 48 * 2**20
 
 ROWS_BY_ROWS = (((1,), (1,)), ((), ()))
 

time: 115 us -> 113 us (0.983)
  local copies, waits for them, and re-layouts: 9.77 us -> 0.72 us
  waiting for transfers between devices: 27.5 us -> 35.3 us
    unnamed x40 -> x18, local copies, waits for them, and re-layouts: 9.77 us -> 0.72 us
    ppermute x12, waiting for transfers between devices: 24 us -> 31.7 us  [body(): send = lambda array, pairs: lax.ppermute(array, 'ty', pairs)]
where the time goes in v4:
time: 113 us
  Pallas kernels  44.2 us (39%)
  waiting for transfers between devices  35.3 us (31%)
  starting transfers between devices  31.2 us (28%)
    ppermute x12, waiting for transfers between devices, body(): send = lambda array, pairs: lax.ppermute(array, 'ty', pairs)  31.7 us
    ppermute x10, starting transfers between devices, shift(): return lax.ppermute(array, axis, pairs)  27.9 us
    pallas_call x12, Pallas kernels, patch_sums(): pl.pallas_call(functools.partial(sum_kernel, which, parity, patches), in_...  18.3 us
    pallas_call x3, Pallas kernels, steps(): pl.pallas_call(functools.partial(steps_kernel, skipped, total_rows), grid...  12.3 us
    pallas_call x1, Pallas kernels, terms(): pl.pallas_call(functools.partial(terms_kernel, cuts, group, capacity), in...  11.5 us
    ppermute x10, waiting for transfers between devices, shift(): return lax.ppermute(array, axis, pairs)  3.53 us
    ppermute x12, starting transfers between devices, body(): send = lambda array, pairs: lax.ppermute(array, 'ty', pairs)  3.3 us
  transfers between devices with their start and end apart: 22, of which 7 were waited for; matrix products, arithmetic and copies ran while one was open for 0% of the time, Pallas kernels for 34%

profile of v4, /device:TPU:1, one launch (start us, length us, event | category | flops | bytes accessed | tf_op | source)
XLA Modules:
  0.0 112.6 jit_solution(13681250399246424300)
XLA Ops:
  0.7 5.1 %collective-permute-start = (s32[4,108]{1,0:T(4,128)}, s32[4,108]{1,0:T(4,128)S(1)}, u32[]{:S(2)}, u32[]{:S(2)}) collective-permute-start(s32[4,108]{1,0:T(4,128)} %bitcast.11), channel_id=1, source_target_pairs={{0,7},{1,0},{2,1},{3,2},{4,3},{5,4},{6,5},{7,6},{8,15},{9,8},{10,9... | collective-permute-start | bytes 5192 | tf_op jit(solution)/shard_map/ppermute | solution.py:423
  6.7 11.5 %terms.1 = (f32[648,128]{1,0:T(8,128)S(1)}, f32[648,128]{1,0:T(8,128)S(1)}, f32[648,128]{1,0:T(8,128)S(1)}, f32[648,128]{1,0:T(8,128)S(1)}, f32[648,128]{1,0:T(8...) custom-call(s32[2,144]{1,0:T(2,128)S(1)} %bitcast.9, ...), custom_call_target="tpu_custom_call" | custom-call | bytes 18874368 | tf_op jit(solution)/shard_map/terms/pallas_call | solution.py:121
  19.7 8.4 %collective-permute-done.2.refs_0_ = f32[648,128]{1,0:T(8,128)S(1)} collective-permute-done((f32[648,128]{1,0:T(8,128)S(1)}, f32[648,128]{1,0:T(8,128)S(1)}, u32[]{:S(2)}, u32[]{:S(2)}) %collective-permute-start.2) | collective-permute-done | bytes 331808 | tf_op jit(solution)/shard_map/ppermute | solution.py:456
  28.1 2.0 %patch_sums.12 = f32[864,128]{1,0:T(8,128)S(1)} custom-call(s32[4]{0:T(128)S(1)} %pad_add_fusion.odd.spot, s32[4,108]{1,0:T(4,128)S(1)} %fusion.2.places, f32[648,128]{1,0:T(8,128)S(1)} %collective-permute-done.2.refs_0_, f32[648,128]{1,0:T(8,128)S(1)} %get-tuple-element.107.refs_1_), custom_call_target="tpu_custom_call" | custom-call | tf_op jit(solution)/shard_map/patch_sums/pallas_call | solution.py:183
  30.5 4.7 %collective-permute-done.3.refs_0_ = f32[648,128]{1,0:T(8,128)S(1)} collective-permute-done((f32[648,128]{1,0:T(8,128)S(1)}, f32[648,128]{1,0:T(8,128)S(1)}, u32[]{:S(2)}, u32[]{:S(2)}) %collective-permute-start.3) | collective-permute-done | bytes 331808 | tf_op jit(solution)/shard_map/ppermute | solution.py:456
  35.2 2.0 %patch_sums.13 = f32[864,128]{1,0:T(8,128)S(1)} custom-call(s32[4]{0:T(128)S(1)} %pad_add_fusion.odd.spot, s32[4,108]{1,0:T(4,128)S(1)} %fusion.2.places, f32[648,128]{1,0:T(8,128)S(1)} %collective-permute-done.3.refs_0_, f32[648,128]{1,0:T(8,128)S(1)} %get-tuple-element.110.refs_1_), custom_call_target="tpu_custom_call" | custom-call | tf_op jit(solution)/shard_map/patch_sums/pallas_call | solution.py:183
  37.6 4.7 %collective-permute-done.4.refs_0_ = f32[648,128]{1,0:T(8,128)S(1)} collective-permute-done((f32[648,128]{1,0:T(8,128)S(1)}, f32[648,128]{1,0:T(8,128)S(1)}, u32[]{:S(2)}, u32[]{:S(2)}) %collective-permute-start.4) | collective-permute-done | bytes 331808 | tf_op jit(solution)/shard_map/ppermute | solution.py:456
  42.3 2.0 %patch_sums.14 = f32[864,128]{1,0:T(8,128)S(1)} custom-call(s32[4]{0:T(128)S(1)} %pad_add_fusion.odd.spot, s32[4,108]{1,0:T(4,128)S(1)} %fusion.2.places, f32[648,128]{1,0:T(8,128)S(1)} %collective-permute-done.4.refs_0_, f32[648,128]{1,0:T(8,128)S(1)} %get-tuple-element.113.refs_1_), custom_call_target="tpu_custom_call" | custom-call | tf_op jit(solution)/shard_map/patch_sums/pallas_call | solution.py:183
  46.1 3.3 %collective-permute-done.6.refs_0_ = f32[648,128]{1,0:T(8,128)S(1)} collective-permute-done((f32[648,128]{1,0:T(8,128)S(1)}, f32[648,128]{1,0:T(8,128)S(1)}, u32[]{:S(2)}, u32[]{:S(2)}) %collective-permute-start.6) | collective-permute-done | bytes 331808 | tf_op jit(solution)/shard_map/ppermute | solution.py:456
  49.4 2.0 %patch_sums.16 = f32[864,128]{1,0:T(8,128)S(1)} custom-call(s32[4]{0:T(128)S(1)} %pad_add_fusion.odd.spot, s32[4,108]{1,0:T(4,128)S(1)} %fusion.2.places, f32[648,128]{1,0:T(8,128)S(1)} %collective-permute-done.6.refs_0_, f32[648,128]{1,0:T(8,128)S(1)} %get-tuple-element.120.refs_1_), custom_call_target="tpu_custom_call" | custom-call | tf_op jit(solution)/shard_map/patch_sums/pallas_call | solution.py:183
  55.8 3.2 %collective-permute-done.9.refs_1_ = f32[864,128]{1,0:T(8,128)S(1)} collective-permute-done((f32[864,128]{1,0:T(8,128)S(1)}, f32[864,128]{1,0:T(8,128)S(1)}, u32[]{:S(2)}, u32[]{:S(2)}) %collective-permute-start.9) | collective-permute-done | bytes 442400 | tf_op jit(solution)/shard_map/ppermute | solution.py:456
  59.0 1.4 %patch_sums.20 = f32[864,128]{1,0:T(8,128)S(1)} custom-call(s32[4]{0:T(128)S(1)} %pad_add_fusion.odd.spot, s32[4,108]{1,0:T(4,128)S(1)} %fusion.1.places, f32[648,128]{1,0:T(8,128)S(1)} %get-tuple-element.131.refs_0_, f32[864,128]{1,0:T(8,128)S(1)} %collective-permute-done.9.refs_1_), custom_call_target="tpu_custom_call" | custom-call | tf_op jit(solution)/shard_map/patch_sums/pallas_call | solution.py:183
  61.0 7.4 %collective-permute-done.15.refs_1_ = f32[864,128]{1,0:T(8,128)S(1)} collective-permute-done((f32[864,128]{1,0:T(8,128)S(1)}, f32[864,128]{1,0:T(8,128)S(1)}, u32[]{:S(2)}, u32[]{:S(2)}) %collective-permute-start.15) | collective-permute-done | bytes 442400 | tf_op jit(solution)/shard_map/ppermute | solution.py:456
  68.5 1.4 %patch_sums.21 = f32[864,128]{1,0:T(8,128)S(1)} custom-call(s32[4]{0:T(128)S(1)} %pad_add_fusion.odd.spot, s32[4,108]{1,0:T(4,128)S(1)} %fusion.1.places, f32[648,128]{1,0:T(8,128)S(1)} %get-tuple-element.156.refs_0_, f32[864,128]{1,0:T(8,128)S(1)} %collective-permute-done.15.refs_1_), custom_call_target="tpu_custom_call" | custom-call | tf_op jit(solution)/shard_map/patch_sums/pallas_call | solution.py:183
  70.4 6.5 %collective-permute-start.11 = (f32[48,128]{1,0:T(8,128)S(1)}, f32[48,128]{1,0:T(8,128)S(1)}, u32[]{:S(2)}, u32[]{:S(2)}) collective-permute-start(f32[48,128]{1,0:T(8,128)S(1)} %get-tuple-element.149), channel_id=1, source_target_pairs={{0,8},{8,16},{16,24},{1,9},{9,17},{17,25},{2,10},{10,18},{18,26},{... | collective-permute-start | bytes 73736 | tf_op jit(solution)/shard_map/ppermute | solution.py:423
  76.9 1.9 %collective-permute-start.12 = (f32[48,128]{1,0:T(8,128)S(1)}, f32[48,128]{1,0:T(8,128)S(1)}, u32[]{:S(2)}, u32[]{:S(2)}) collective-permute-start(f32[48,128]{1,0:T(8,128)S(1)} %get-tuple-element.150), channel_id=1, source_target_pairs={{8,0},{16,8},{24,16},{9,1},{17,9},{25,17},{10,2},{18,10},{26,18},{... | collective-permute-start | bytes 73736 | tf_op jit(solution)/shard_map/ppermute | solution.py:423
  78.8 3.5 %collective-permute-done.12.right.refs_3_.refs_7_ = f32[48,128]{1,0:T(8,128)S(1)} collective-permute-done((f32[48,128]{1,0:T(8,128)S(1)}, f32[48,128]{1,0:T(8,128)S(1)}, u32[]{:S(2)}, u32[]{:S(2)}) %collective-permute-start.12) | collective-permute-done | bytes 24608 | tf_op jit(solution)/shard_map/ppermute | solution.py:423
  82.4 4.1 %collective-permute-start.14 = (f32[16,4,384]{2,1,0:T(4,128)S(1)}, f32[16,4,384]{2,1,0:T(4,128)S(1)}, u32[]{:S(2)}, u32[]{:S(2)}) collective-permute-start(f32[16,4,384]{2,1,0:T(4,128)S(1)} %get-tuple-element.154), channel_id=1, source_target_pairs={{0,7},{1,0},{2,1},{3,2},{4,3},{5,4},{6,5},{7,6},{8,15},{9,8},{10,9... | collective-permute-start | bytes 294920 | tf_op jit(solution)/shard_map/ppermute | solution.py:423
  90.2 3.9 %collective-permute-start.18 = (f32[48,128]{1,0:T(8,128)S(1)}, f32[48,128]{1,0:T(8,128)S(1)}, u32[]{:S(2)}, u32[]{:S(2)}) collective-permute-start(f32[48,128]{1,0:T(8,128)S(1)} %get-tuple-element.180), channel_id=1, source_target_pairs={{0,8},{8,16},{16,24},{1,9},{9,17},{17,25},{2,10},{10,18},{18,26},{... | collective-permute-start | bytes 73736 | tf_op jit(solution)/shard_map/ppermute | solution.py:423
  94.1 1.9 %collective-permute-start.19 = (f32[48,128]{1,0:T(8,128)S(1)}, f32[48,128]{1,0:T(8,128)S(1)}, u32[]{:S(2)}, u32[]{:S(2)}) collective-permute-start(f32[48,128]{1,0:T(8,128)S(1)} %get-tuple-element.181), channel_id=1, source_target_pairs={{8,0},{16,8},{24,16},{9,1},{17,9},{25,17},{10,2},{18,10},{26,18},{... | collective-permute-start | bytes 73736 | tf_op jit(solution)/shard_map/ppermute | solution.py:423
  96.0 3.4 %steps.3 = (f32[8,48,384]{2,1,0:T(8,128)}, f32[8,48,384]{2,1,0:T(8,128)}, f32[8,48,384]{2,1,0:T(8,128)}, f32[8,128]{1,0:T(8,128)S(1)}) custom-call(s32[4]{0:T(128)S(1)} %pad_add_fusion.odd.spot, s32[2,4]{1,0:T(2,128)S(1)} %copy-done.6, f32[2,48,384]{2,1,0:T(8,128)S(1)} %copy-done.3, f32[48,384]{1,0:T(8,128)S(1)} %copy-done.5, ...), custom_call_target="tpu_custom_call" | custom-call | tf_op jit(solution)/shard_map/steps/pallas_call | solution.py:397
  100.0 3.7 %collective-permute-start.21 = (f32[13,4,384]{2,1,0:T(4,128)S(1)}, f32[13,4,384]{2,1,0:T(4,128)S(1)}, u32[]{:S(2)}, u32[]{:S(2)}) collective-permute-start(f32[13,4,384]{2,1,0:T(4,128)S(1)} %get-tuple-element.189), channel_id=1, source_target_pairs={{0,7},{1,0},{2,1},{3,2},{4,3},{5,4},{6,5},{7,6},{8,15},{9,8},{10,9... | collective-permute-start | bytes 239624 | tf_op jit(solution)/shard_map/ppermute | solution.py:423
  103.7 3.4 %steps.4 = (f32[8,48,384]{2,1,0:T(8,128)}, f32[8,48,384]{2,1,0:T(8,128)}, f32[8,48,384]{2,1,0:T(8,128)}, f32[8,128]{1,0:T(8,128)}) custom-call(s32[4]{0:T(128)S(1)} %pad_add_fusion.odd.spot, s32[2,4]{1,0:T(2,128)S(1)} %copy-done.6, f32[2,48,384]{2,1,0:T(8,128)S(1)} %copy-done.3, ...), custom_call_target="tpu_custom_call", output_to_operand_aliasing={{0}: (15, {}), {1}: (16, {}), {2}: (17, {})} | custom-call | tf_op jit(solution)/shard_map/steps/pallas_call | solution.py:397
  107.1 5.5 %steps.5 = (f32[8,48,384]{2,1,0:T(8,128)}, f32[8,48,384]{2,1,0:T(8,128)}, f32[8,48,384]{2,1,0:T(8,128)}, f32[8,128]{1,0:T(8,128)}) custom-call(s32[4]{0:T(128)S(1)} %pad_add_fusion.odd.spot, s32[2,4]{1,0:T(2,128)S(1)} %copy-done.6, f32[2,48,384]{2,1,0:T(8,128)S(1)} %copy-done.3, ...), custom_call_target="tpu_custom_call", output_to_operand_aliasing={{0}: (15, {}), {1}: (16, {}), {2}: (17, {})} | custom-call | tf_op jit(solution)/shard_map/steps/pallas_call | solution.py:397
  (64 shorter events, 14.8 us)
Async XLA Ops:
  0.6 59.8 %copy-start.4 = (f32[4,48,384]{2,1,0:T(8,128)S(1)}, f32[4,48,384]{2,1,0:T(8,128)}, u32[]{:S(2)}) copy-start(f32[4,48,384]{2,1,0:T(8,128)} %basis.7) | copy-start | bytes 884740
  0.7 17.5 %collective-permute-start = (s32[4,108]{1,0:T(4,128)}, s32[4,108]{1,0:T(4,128)S(1)}, u32[]{:S(2)}, u32[]{:S(2)}) collective-permute-start(s32[4,108]{1,0:T(4,128)} %bitcast.11), channel_id=1, source_target_pairs={{0,7},{1,0},{2,1},{3,2},{4,3},{5,4},{6,5},{7,6},{8,15},{9,8},{10,9... | collective-permute-start | bytes 5192 | tf_op jit(solution)/shard_map/ppermute | solution.py:423
  5.8 12.4 %collective-permute-start.1 = (s32[4,108]{1,0:T(4,128)}, s32[4,108]{1,0:T(4,128)S(1)}, u32[]{:S(2)}, u32[]{:S(2)}) collective-permute-start(s32[4,108]{1,0:T(4,128)} %bitcast.12), channel_id=1, source_target_pairs={{0,6},{1,7},{2,0},{3,1},{4,2},{5,3},{6,4},{7,5},{8,14},{9,15},{10,... | collective-permute-start | bytes 5192 | tf_op jit(solution)/shard_map/ppermute | solution.py:423
  18.2 77.9 %copy-start.6 = (s32[2,4]{1,0:T(2,128)S(1)}, s32[2,4]{1,0:T(2,128)}, u32[]{:S(2)}) copy-start(s32[2,4]{1,0:T(2,128)} %rotation.5) | copy-start | bytes 100
  18.2 9.9 %collective-permute-start.2 = (f32[648,128]{1,0:T(8,128)S(1)}, f32[648,128]{1,0:T(8,128)S(1)}, u32[]{:S(2)}, u32[]{:S(2)}) collective-permute-start(f32[648,128]{1,0:T(8,128)S(1)} %get-tuple-element.106), channel_id=1, source_target_pairs={{0,2},{1,3},{2,4},{3,5},{4,6},{5,7},{6,0},{7,1},{8,10},{9,11},{10,... | collective-permute-start | bytes 995336 | tf_op jit(solution)/shard_map/ppermute | solution.py:456
  19.6 15.6 %collective-permute-start.3 = (f32[648,128]{1,0:T(8,128)S(1)}, f32[648,128]{1,0:T(8,128)S(1)}, u32[]{:S(2)}, u32[]{:S(2)}) collective-permute-start(f32[648,128]{1,0:T(8,128)S(1)} %get-tuple-element.109), channel_id=1, source_target_pairs={{0,2},{1,3},{2,4},{3,5},{4,6},{5,7},{6,0},{7,1},{8,10},{9,11},{10,... | collective-permute-start | bytes 995336 | tf_op jit(solution)/shard_map/ppermute | solution.py:456
  19.6 22.7 %collective-permute-start.4 = (f32[648,128]{1,0:T(8,128)S(1)}, f32[648,128]{1,0:T(8,128)S(1)}, u32[]{:S(2)}, u32[]{:S(2)}) collective-permute-start(f32[648,128]{1,0:T(8,128)S(1)} %get-tuple-element.112), channel_id=1, source_target_pairs={{0,2},{1,3},{2,4},{3,5},{4,6},{5,7},{6,0},{7,1},{8,10},{9,11},{10,... | collective-permute-start | bytes 995336 | tf_op jit(solution)/shard_map/ppermute | solution.py:456
  30.1 14.6 %collective-permute-start.5 = (f32[864,128]{1,0:T(8,128)S(1)}, f32[864,128]{1,0:T(8,128)S(1)}, u32[]{:S(2)}, u32[]{:S(2)}) collective-permute-start(f32[864,128]{1,0:T(8,128)S(1)} %patch_sums.12), channel_id=1, source_target_pairs={{0,1},{2,3},{4,5},{6,7},{1,0},{3,2},{5,4},{7,6},{8,9},{10,11},{12,... | collective-permute-start | bytes 1327112 | tf_op jit(solution)/shard_map/ppermute | solution.py:456
  30.5 18.9 %collective-permute-start.6 = (f32[648,128]{1,0:T(8,128)S(1)}, f32[648,128]{1,0:T(8,128)S(1)}, u32[]{:S(2)}, u32[]{:S(2)}) collective-permute-start(f32[648,128]{1,0:T(8,128)S(1)} %get-tuple-element.119), channel_id=1, source_target_pairs={{0,2},{1,3},{2,4},{3,5},{4,6},{5,7},{6,0},{7,1},{8,10},{9,11},{10,... | collective-permute-start | bytes 995336 | tf_op jit(solution)/shard_map/ppermute | solution.py:456
  37.2 14.6 %collective-permute-start.7 = (f32[864,128]{1,0:T(8,128)S(1)}, f32[864,128]{1,0:T(8,128)S(1)}, u32[]{:S(2)}, u32[]{:S(2)}) collective-permute-start(f32[864,128]{1,0:T(8,128)S(1)} %patch_sums.13), channel_id=1, source_target_pairs={{0,1},{2,3},{4,5},{6,7},{1,0},{3,2},{5,4},{7,6},{8,9},{10,11},{12,... | collective-permute-start | bytes 1327112 | tf_op jit(solution)/shard_map/ppermute | solution.py:456
  44.3 14.7 %collective-permute-start.9 = (f32[864,128]{1,0:T(8,128)S(1)}, f32[864,128]{1,0:T(8,128)S(1)}, u32[]{:S(2)}, u32[]{:S(2)}) collective-permute-start(f32[864,128]{1,0:T(8,128)S(1)} %patch_sums.14), channel_id=1, source_target_pairs={{0,1},{2,3},{4,5},{6,7},{1,0},{3,2},{5,4},{7,6},{8,9},{10,11},{12,... | collective-permute-start | bytes 1327112 | tf_op jit(solution)/shard_map/ppermute | solution.py:456
  46.1 14.3 %collective-permute-start.10 = (f32[864,128]{1,0:T(8,128)S(1)}, f32[864,128]{1,0:T(8,128)S(1)}, u32[]{:S(2)}, u32[]{:S(2)}) collective-permute-start(f32[864,128]{1,0:T(8,128)S(1)} %patch_sums.15), channel_id=1, source_target_pairs={{0,2},{1,3},{2,4},{3,5},{4,6},{5,7},{6,0},{7,1},{8,10},{9,11},{10,... | collective-permute-start | bytes 1327112 | tf_op jit(solution)/shard_map/ppermute | solution.py:456
  51.4 17.1 %collective-permute-start.15 = (f32[864,128]{1,0:T(8,128)S(1)}, f32[864,128]{1,0:T(8,128)S(1)}, u32[]{:S(2)}, u32[]{:S(2)}) collective-permute-start(f32[864,128]{1,0:T(8,128)S(1)} %patch_sums.16), channel_id=1, source_target_pairs={{0,1},{2,3},{4,5},{6,7},{1,0},{3,2},{5,4},{7,6},{8,9},{10,11},{12,... | collective-permute-start | bytes 1327112 | tf_op jit(solution)/shard_map/ppermute | solution.py:456
  53.2 16.7 %collective-permute-start.8 = (f32[864,128]{1,0:T(8,128)S(1)}, f32[864,128]{1,0:T(8,128)S(1)}, u32[]{:S(2)}, u32[]{:S(2)}) collective-permute-start(f32[864,128]{1,0:T(8,128)S(1)} %patch_sums.17), channel_id=1, source_target_pairs={{0,2},{1,3},{2,4},{3,5},{4,6},{5,7},{6,0},{7,1},{8,10},{9,11},{10,... | collective-permute-start | bytes 1327112 | tf_op jit(solution)/shard_map/ppermute | solution.py:456
  60.3 27.5 %collective-permute-start.17 = (f32[864,128]{1,0:T(8,128)S(1)}, f32[864,128]{1,0:T(8,128)S(1)}, u32[]{:S(2)}, u32[]{:S(2)}) collective-permute-start(f32[864,128]{1,0:T(8,128)S(1)} %patch_sums.20), channel_id=1, source_target_pairs={{0,2},{1,3},{2,4},{3,5},{4,6},{5,7},{6,0},{7,1},{8,10},{9,11},{10,... | collective-permute-start | bytes 1327112 | tf_op jit(solution)/shard_map/ppermute | solution.py:456
  69.8 19.9 %collective-permute-start.16 = (f32[864,128]{1,0:T(8,128)S(1)}, f32[864,128]{1,0:T(8,128)S(1)}, u32[]{:S(2)}, u32[]{:S(2)}) collective-permute-start(f32[864,128]{1,0:T(8,128)S(1)} %patch_sums.21), channel_id=1, source_target_pairs={{0,2},{1,3},{2,4},{3,5},{4,6},{5,7},{6,0},{7,1},{8,10},{9,11},{10,... | collective-permute-start | bytes 1327112 | tf_op jit(solution)/shard_map/ppermute | solution.py:456
  70.4 8.4 %collective-permute-start.11 = (f32[48,128]{1,0:T(8,128)S(1)}, f32[48,128]{1,0:T(8,128)S(1)}, u32[]{:S(2)}, u32[]{:S(2)}) collective-permute-start(f32[48,128]{1,0:T(8,128)S(1)} %get-tuple-element.149), channel_id=1, source_target_pairs={{0,8},{8,16},{16,24},{1,9},{9,17},{17,25},{2,10},{10,18},{18,26},{... | collective-permute-start | bytes 73736 | tf_op jit(solution)/shard_map/ppermute | solution.py:423
  76.9 5.4 %collective-permute-start.12 = (f32[48,128]{1,0:T(8,128)S(1)}, f32[48,128]{1,0:T(8,128)S(1)}, u32[]{:S(2)}, u32[]{:S(2)}) collective-permute-start(f32[48,128]{1,0:T(8,128)S(1)} %get-tuple-element.150), channel_id=1, source_target_pairs={{8,0},{16,8},{24,16},{9,1},{17,9},{25,17},{10,2},{18,10},{26,18},{... | collective-permute-start | bytes 73736 | tf_op jit(solution)/shard_map/ppermute | solution.py:423
  82.4 13.6 %collective-permute-start.13 = (f32[16,4,384]{2,1,0:T(4,128)S(1)}, f32[16,4,384]{2,1,0:T(4,128)S(1)}, u32[]{:S(2)}, u32[]{:S(2)}) collective-permute-start(f32[16,4,384]{2,1,0:T(4,128)S(1)} %get-tuple-element.153), channel_id=1, source_target_pairs={{0,1},{1,2},{2,3},{3,4},{4,5},{5,6},{6,7},{7,0},{8,9},{9,10},{10,1... | collective-permute-start | bytes 294920 | tf_op jit(solution)/shard_map/ppermute | solution.py:423
  82.4 13.6 %collective-permute-start.14 = (f32[16,4,384]{2,1,0:T(4,128)S(1)}, f32[16,4,384]{2,1,0:T(4,128)S(1)}, u32[]{:S(2)}, u32[]{:S(2)}) collective-permute-start(f32[16,4,384]{2,1,0:T(4,128)S(1)} %get-tuple-element.154), channel_id=1, source_target_pairs={{0,7},{1,0},{2,1},{3,2},{4,3},{5,4},{6,5},{7,6},{8,15},{9,8},{10,9... | collective-permute-start | bytes 294920 | tf_op jit(solution)/shard_map/ppermute | solution.py:423
  90.2 9.3 %collective-permute-start.18 = (f32[48,128]{1,0:T(8,128)S(1)}, f32[48,128]{1,0:T(8,128)S(1)}, u32[]{:S(2)}, u32[]{:S(2)}) collective-permute-start(f32[48,128]{1,0:T(8,128)S(1)} %get-tuple-element.180), channel_id=1, source_target_pairs={{0,8},{8,16},{16,24},{1,9},{9,17},{17,25},{2,10},{10,18},{18,26},{... | collective-permute-start | bytes 73736 | tf_op jit(solution)/shard_map/ppermute | solution.py:423
  94.1 5.4 %collective-permute-start.19 = (f32[48,128]{1,0:T(8,128)S(1)}, f32[48,128]{1,0:T(8,128)S(1)}, u32[]{:S(2)}, u32[]{:S(2)}) collective-permute-start(f32[48,128]{1,0:T(8,128)S(1)} %get-tuple-element.181), channel_id=1, source_target_pairs={{8,0},{16,8},{24,16},{9,1},{17,9},{25,17},{10,2},{18,10},{26,18},{... | collective-permute-start | bytes 73736 | tf_op jit(solution)/shard_map/ppermute | solution.py:423
  99.5 7.6 %collective-permute-start.20 = (f32[13,4,384]{2,1,0:T(4,128)S(1)}, f32[13,4,384]{2,1,0:T(4,128)S(1)}, u32[]{:S(2)}, u32[]{:S(2)}) collective-permute-start(f32[13,4,384]{2,1,0:T(4,128)S(1)} %get-tuple-element.188), channel_id=1, source_target_pairs={{0,1},{1,2},{2,3},{3,4},{4,5},{5,6},{6,7},{7,0},{8,9},{9,10},{10,1... | collective-permute-start | bytes 239624 | tf_op jit(solution)/shard_map/ppermute | solution.py:423
  100.0 7.1 %collective-permute-start.21 = (f32[13,4,384]{2,1,0:T(4,128)S(1)}, f32[13,4,384]{2,1,0:T(4,128)S(1)}, u32[]{:S(2)}, u32[]{:S(2)}) collective-permute-start(f32[13,4,384]{2,1,0:T(4,128)S(1)} %get-tuple-element.189), channel_id=1, source_target_pairs={{0,7},{1,0},{2,1},{3,2},{4,3},{5,4},{6,5},{7,6},{8,15},{9,8},{10,9... | collective-permute-start | bytes 239624 | tf_op jit(solution)/shard_map/ppermute | solution.py:423
  (7 other events, 346.2 us)

commit v5 on v4

--- a/solution.py
+++ b/solution.py
@@ -19,7 +19,7 @@
 CHUNKS = (2, 2, 2, 2)
 PAIRS = ((0,), (1,), (2,), (3,))
 GROUPS = ((0, 1), (2, 3))
-LATE = ()
+AFTER = {0: (1,), 1: (2,)}
 EARLY = ((0, 2),)
 ORDER = (
     "P0", "P1", "P2", "J0", "P3", "J1", "S0", "S1", "J2", "F0", "J3", "S2", "S3", "F1", "F2", "H0", "F3", "H1",
@@ -71,10 +71,83 @@
         copy.wait()
 
 
-def terms_kernel(cuts, group, capacity, offsets, increments, weights, *refs):
+def far_terms_kernel(bounds, owner, offsets, increments, weights, *refs):
     fields, levels, rows, _ = increments.shape
     count, tops = fields * levels, offsets.shape[0]
-    outs = refs[:-9]
+    parts = len(bounds) - 1
+    outs, (held, source, left, right, order, source_sem, held_sem) = refs[:parts], refs[parts:]
+    capacity = held.shape[0]
+    first = pltpu.make_async_copy(increments, source, source_sem)
+    first.start()
+
+    def fetch(m, k):
+        return pltpu.make_async_copy(weights.at[m], held.at[k], held_sem.at[k])
+
+    def look(s, found):
+        for t in range(tops):
+            order[found] = s * tops + t
+            found = found + (offsets[t, s] == owner).astype(jnp.int32)
+        return found
+
+    found = lax.fori_loop(0, rows, look, 0, unroll=8)
+
+    @pl.loop(0, found)
+    def _(k):
+        fetch(order[k], k).start()
+
+    first.wait()
+    spread(source, left, right)
+    group = max(g for g in range(1, GROUP + 1) if capacity % g == 0)
+
+    @pl.loop(0, capacity // group)
+    def _(g):
+        for j in range(group):
+            k = g * group + j
+
+            @pl.when(k < found)
+            def _():
+                fetch(0, k).wait()
+
+        for j in range(group):
+            k = g * group + j
+            s = order[jnp.minimum(k, found - 1)] // tops
+            term = lax.dot_general(
+                row_block(left, right, s, count), held[k], ROWS_BY_ROWS, preferred_element_type=jnp.float32
+            )
+            term = jnp.where(k < found, term, 0.0)
+            for out, first, last in zip(outs, bounds[:-1], bounds[1:]):
+                size = fields * (last - first)
+                out[pl.ds(k, size, stride=capacity), :] = term[fields * first : fields * last]
+
+
+def far_terms(bounds, owners, capacity, offsets, increments, weights):
+    fields, levels, rows, width = increments.shape
+    tops, wide = offsets.shape[0], weights.shape[-1]
+    count, parts = fields * levels, len(bounds) - 1
+    sizes = [fields * (last - first) * capacity for first, last in zip(bounds[:-1], bounds[1:])]
+    return pl.pallas_call(
+        functools.partial(far_terms_kernel, bounds, owners - 1),
+        in_specs=in_smem(1) + in_hbm(2),
+        out_specs=in_vmem(parts),
+        out_shape=[jax.ShapeDtypeStruct((size, TPATCH), jnp.float32) for size in sizes],
+        scratch_shapes=[
+            pltpu.VMEM((capacity, TPATCH, wide), jnp.bfloat16),
+            pltpu.VMEM(increments.shape, jnp.bfloat16),
+            pltpu.VMEM((count * rows, width // 2), jnp.float32),
+            pltpu.VMEM((count * rows, width // 2), jnp.float32),
+            pltpu.SMEM((rows * tops + 1,), jnp.int32),
+            pltpu.SemaphoreType.DMA,
+            pltpu.SemaphoreType.DMA((capacity,)),
+        ],
+        compiler_params=params(62 * 2**20),
+        name="far_terms",
+    )(offsets, increments, weights.reshape(rows * tops, TPATCH, wide))
+
+
+def terms_kernel(cuts, later, group, capacity, offsets, increments, weights, *refs):
+    fields, levels, rows, _ = increments.shape
+    count, tops = fields * levels, offsets.shape[0]
+    outs = refs[later:-9]
     held, source, left, right, slots, used, source_sem, held_sem, out_sem = refs[-9:]
     groups = rows // group
     first = pltpu.make_async_copy(increments, source, source_sem)
@@ -88,7 +161,7 @@
     def _(g):
         fetch(g).start()
 
-    for o in range(len(cuts)):
+    for o in range(len(cuts) + 1):
         used[o] = 0
     slots[...] = jnp.zeros_like(slots)
     first.wait()
@@ -111,7 +184,7 @@
     write_out(cuts, fields, capacity, slots, outs, out_sem)
 
 
-def terms(cuts, capacity, offsets, increments, weights):
+def terms(cuts, capacity, offsets, increments, weights, later):
     fields, levels, rows, width = increments.shape
     tops, wide = offsets.shape[0], weights.shape[-1]
     count = fields * levels
@@ -119,8 +192,8 @@
     sizes = [last - first for cut in cuts for first, last in zip(cut[:-1], cut[1:])]
     weights = weights.reshape(rows, tops * TPATCH, wide)
     out = pl.pallas_call(
-        functools.partial(terms_kernel, cuts, group, capacity),
-        in_specs=in_smem(1) + in_hbm(2),
+        functools.partial(terms_kernel, cuts, len(later), group, capacity),
+        in_specs=in_smem(1) + in_hbm(2 + len(later)),
         out_specs=in_hbm(len(sizes)),
         out_shape=[jax.ShapeDtypeStruct((fields * size * capacity, TPATCH), jnp.float32) for size in sizes],
         scratch_shapes=[
@@ -128,8 +201,8 @@
             pltpu.VMEM(increments.shape, jnp.bfloat16),
             pltpu.VMEM((count * rows, width // 2), jnp.float32),
             pltpu.VMEM((count * rows, width // 2), jnp.float32),
-            pltpu.VMEM((len(cuts) * count * capacity, TPATCH), jnp.float32),
-            pltpu.SMEM((len(cuts),), jnp.int32),
+            pltpu.VMEM(((len(cuts) + 1) * count * capacity, TPATCH), jnp.float32),
+            pltpu.SMEM((len(cuts) + 1,), jnp.int32),
             pltpu.SemaphoreType.DMA,
             pltpu.SemaphoreType.DMA((rows // group,)),
             pltpu.SemaphoreType.DMA((len(sizes),)),
@@ -137,7 +210,7 @@
         compiler_params=params(),
         cost_estimate=pl.CostEstimate(flops=0, bytes_accessed=rows * tops * TPATCH * wide * 2, transcendentals=0),
         name="terms",
-    )(offsets, increments, weights)
+    )(offsets, increments, weights, *later)
     given = []
     for cut in cuts:
         given.append(out[: len(cut) - 1])
@@ -464,8 +537,9 @@
     offsets = dest_offset.transpose(0, 1, 3, 2).reshape(-1, dest_offset.shape[2])
     counts = [FIELDS * (last - first) for first, last in zip(bounds[:-1], bounds[1:])]
     wide = [bounds[pair[0]] for pair in PAIRS] + [levels]
-    cuts = [bounds, wide] + [bounds] * (owners - 3) + [wide]
-    own, first, second, far = terms(cuts, capacity, offsets, increments, remap_weights)
+    far = far_terms(bounds, owners, capacity, offsets, increments, remap_weights)
+    cuts = [bounds, wide] + [bounds] * (owners - 3)
+    own, first, second = terms(cuts, capacity, offsets, increments, remap_weights, [ahead[1]])
     *far, ahead[0], ahead[1] = together(*far, *ahead)
     places_next, places_second = ((p % blocks) * rows + p // blocks for p in ahead)
     thirds = [send(slots, to_next) for slots in far]
@@ -500,7 +574,7 @@
             fields, ends[g], sides[g] = first_fields(
                 place, bounds[n + 1] - bounds[n], patches, ready, last[n], basis, thickness, wind_first, wind_second,
                 metric, sides.get(g), fields, ends.get(g, []),
-                halos[0] if g and n in LATE else [],
+                [settled[j] for j in AFTER.get(n, ())],
             )
             token, *sides[g] = together(token, *sides[g])
         else:
@@ -511,7 +585,8 @@
                 for first, count in EARLY:
                     *results, finished = steps_on(0, first, count, results)
                     finished = [finished]
-            high_rows, low_rows = reversed(last_entries(1 if n else 1 + FIELDS, ends[n], *metric, beside, finished))
+            waited = finished if n else [settled[parts - 1], *sides.get(1, [])[:1]]
+            high_rows, low_rows = reversed(last_entries(1 if n else 1 + FIELDS, ends[n], *metric, beside, waited))
             halos.append([shift(high_rows, "ty", 1, True), shift(low_rows, "ty", -1, True), *beside])
 
     done = EARLY[-1][0] + EARLY[-1][1] if EARLY else 0

time: 113 us -> 111 us (0.982)
  waiting for transfers between devices: 35.3 us -> 17.7 us
  starting transfers between devices: 31.2 us -> 39.4 us
  Pallas kernels: 44.2 us -> 52 us
    ppermute x12, waiting for transfers between devices: 31.7 us -> 16 us  [body(): send = lambda array, pairs: lax.ppermute(array, 'ty', pairs)]
    ppermute x12, starting transfers between devices: 3.3 us -> 12.8 us  [body(): send = lambda array, pairs: lax.ppermute(array, 'ty', pairs)]
    pallas_call x1 -> x2, Pallas kernels: 11.5 us -> 19.3 us  [the longest x1 10.8 us: terms(): pl.pallas_call(functools.partial(terms_kernel, cuts, len(later), group, c...]
    ppermute x10, waiting for transfers between devices: 3.53 us -> 1.67 us  [shift(): return lax.ppermute(array, axis, pairs)]
    ppermute x10, starting transfers between devices: 27.9 us -> 26.6 us  [shift(): return lax.ppermute(array, axis, pairs)]
  transfers between devices with their start and end apart: 22 -> 22, of which waited for: 7 -> 5; matrix products, arithmetic and copies ran while one was open for 0% -> 0% of each run, Pallas kernels for 34% -> 42%
where the time goes in v5:
time: 111 us; the launch traced here: 110 us
  Pallas kernels  52 us (47%)
  starting transfers between devices  39.4 us (35%)
  waiting for transfers between devices  17.7 us (16%)
    ppermute x10, starting transfers between devices, shift(): return lax.ppermute(array, axis, pairs)  26.6 us
    pallas_call x12, Pallas kernels, patch_sums(): pl.pallas_call(functools.partial(sum_kernel, which, parity, patches), in_...  18.3 us
    ppermute x12, waiting for transfers between devices, body(): send = lambda array, pairs: lax.ppermute(array, 'ty', pairs)  16 us
    ppermute x12, starting transfers between devices, body(): send = lambda array, pairs: lax.ppermute(array, 'ty', pairs)  12.8 us
    pallas_call x3, Pallas kernels, steps(): pl.pallas_call(functools.partial(steps_kernel, skipped, total_rows), grid...  12.3 us
    pallas_call x1, Pallas kernels, terms(): pl.pallas_call(functools.partial(terms_kernel, cuts, len(later), group, c...  10.8 us
    pallas_call x1, Pallas kernels, far_terms(): pl.pallas_call(functools.partial(far_terms_kernel, bounds, owners - 1), i...  8.54 us
  transfers between devices with their start and end apart: 22, of which 5 were waited for; matrix products, arithmetic and copies ran while one was open for 0% of the time, Pallas kernels for 42%

profile of v5, /device:TPU:1, one launch (start us, length us, event | category | flops | bytes accessed | tf_op | source)
XLA Modules:
  0.0 110.3 jit_solution(1059053955046017826)
XLA Ops:
  0.6 4.2 %collective-permute-start.1 = (s32[4,108]{1,0:T(4,128)}, s32[4,108]{1,0:T(4,128)S(1)}, u32[]{:S(2)}, u32[]{:S(2)}) collective-permute-start(s32[4,108]{1,0:T(4,128)} %bitcast.14), channel_id=1, source_target_pairs={{0,6},{1,7},{2,0},{3,1},{4,2},{5,3},{6,4},{7,5},{8,14},{9,15},{10,... | collective-permute-start | bytes 5192 | tf_op jit(solution)/shard_map/ppermute | solution.py:496
  6.0 8.5 %far_terms.1 = (f32[648,128]{1,0:T(8,128)}, f32[648,128]{1,0:T(8,128)}, f32[648,128]{1,0:T(8,128)}, f32[648,128]{1,0:T(8,128)}) custom-call(s32[2,144]{1,0:T(2,128)} %bitcast.10, bf16[3,8,144,256]{3,2,1,0:T(8,128)(2,1)} %increments.3, bf16[288,128,256]{2,1,0:T(8,128)(2,1)} %bitcast.12), custom_call_target="tpu_custom_call" | custom-call | tf_op jit(solution)/shard_map/far_terms/pallas_call | solution.py:128
  16.1 10.8 %terms.1 = (f32[648,128]{1,0:T(8,128)S(1)}, f32[648,128]{1,0:T(8,128)S(1)}, f32[648,128]{1,0:T(8,128)S(1)}, f32[648,128]{1,0:T(8,128)S(1)}, f32[648,128]{1,0:T(8...) custom-call(s32[2,144]{1,0:T(2,128)S(1)} %bitcast.11, ...), custom_call_target="tpu_custom_call" | custom-call | bytes 18874368 | tf_op jit(solution)/shard_map/terms/pallas_call | solution.py:194
  26.9 2.0 %patch_sums.12 = f32[864,128]{1,0:T(8,128)S(1)} custom-call(s32[4]{0:T(128)S(1)} %pad_add_fusion.odd.spot, s32[4,108]{1,0:T(4,128)S(1)} %fusion.2.places, f32[648,128]{1,0:T(8,128)S(1)} %collective-permute-done.2.refs_0_, f32[648,128]{1,0:T(8,128)S(1)} %get-tuple-element.107.refs_1_), custom_call_target="tpu_custom_call" | custom-call | tf_op jit(solution)/shard_map/patch_sums/pallas_call | solution.py:256
  29.0 2.8 %collective-permute-start.6 = (f32[648,128]{1,0:T(8,128)S(1)}, f32[648,128]{1,0:T(8,128)S(1)}, u32[]{:S(2)}, u32[]{:S(2)}) collective-permute-start(f32[648,128]{1,0:T(8,128)S(1)} %copy-done.10), channel_id=1, source_target_pairs={{0,2},{1,3},{2,4},{3,5},{4,6},{5,7},{6,0},{7,1},{8,10},{9,11},{10,... | collective-permute-start | bytes 995336 | tf_op jit(solution)/shard_map/ppermute | solution.py:529
  31.8 2.0 %patch_sums.13 = f32[864,128]{1,0:T(8,128)S(1)} custom-call(s32[4]{0:T(128)S(1)} %pad_add_fusion.odd.spot, s32[4,108]{1,0:T(4,128)S(1)} %fusion.2.places, f32[648,128]{1,0:T(8,128)S(1)} %collective-permute-done.3.refs_0_, f32[648,128]{1,0:T(8,128)S(1)} %get-tuple-element.110.refs_1_), custom_call_target="tpu_custom_call" | custom-call | tf_op jit(solution)/shard_map/patch_sums/pallas_call | solution.py:256
  34.9 4.0 %collective-permute-done.4.refs_0_ = f32[648,128]{1,0:T(8,128)S(1)} collective-permute-done((f32[648,128]{1,0:T(8,128)}, f32[648,128]{1,0:T(8,128)S(1)}, u32[]{:S(2)}, u32[]{:S(2)}) %collective-permute-start.4) | collective-permute-done | bytes 331808 | tf_op jit(solution)/shard_map/ppermute | solution.py:529
  38.9 2.0 %patch_sums.14 = f32[864,128]{1,0:T(8,128)S(1)} custom-call(s32[4]{0:T(128)S(1)} %pad_add_fusion.odd.spot, s32[4,108]{1,0:T(4,128)S(1)} %fusion.2.places, f32[648,128]{1,0:T(8,128)S(1)} %collective-permute-done.4.refs_0_, f32[648,128]{1,0:T(8,128)S(1)} %get-tuple-element.113.refs_1_), custom_call_target="tpu_custom_call" | custom-call | tf_op jit(solution)/shard_map/patch_sums/pallas_call | solution.py:256
  42.8 3.2 %collective-permute-done.6.refs_0_ = f32[648,128]{1,0:T(8,128)S(1)} collective-permute-done((f32[648,128]{1,0:T(8,128)S(1)}, f32[648,128]{1,0:T(8,128)S(1)}, u32[]{:S(2)}, u32[]{:S(2)}) %collective-permute-start.6) | collective-permute-done | bytes 331808 | tf_op jit(solution)/shard_map/ppermute | solution.py:529
  46.0 2.0 %patch_sums.16 = f32[864,128]{1,0:T(8,128)S(1)} custom-call(s32[4]{0:T(128)S(1)} %pad_add_fusion.odd.spot, s32[4,108]{1,0:T(4,128)S(1)} %fusion.2.places, f32[648,128]{1,0:T(8,128)S(1)} %collective-permute-done.6.refs_0_, f32[648,128]{1,0:T(8,128)S(1)} %get-tuple-element.120.refs_1_), custom_call_target="tpu_custom_call" | custom-call | tf_op jit(solution)/shard_map/patch_sums/pallas_call | solution.py:256
  49.9 2.0 %collective-permute-start.8 = (f32[864,128]{1,0:T(8,128)S(1)}, f32[864,128]{1,0:T(8,128)S(1)}, u32[]{:S(2)}, u32[]{:S(2)}) collective-permute-start(f32[864,128]{1,0:T(8,128)S(1)} %patch_sums.17), channel_id=1, source_target_pairs={{0,2},{1,3},{2,4},{3,5},{4,6},{5,7},{6,0},{7,1},{8,10},{9,11},{10,... | collective-permute-start | bytes 1327112 | tf_op jit(solution)/shard_map/ppermute | solution.py:529
  54.4 3.4 %collective-permute-done.9.refs_1_ = f32[864,128]{1,0:T(8,128)S(1)} collective-permute-done((f32[864,128]{1,0:T(8,128)S(1)}, f32[864,128]{1,0:T(8,128)S(1)}, u32[]{:S(2)}, u32[]{:S(2)}) %collective-permute-start.9) | collective-permute-done | bytes 442400 | tf_op jit(solution)/shard_map/ppermute | solution.py:529
  59.2 2.1 %collective-permute-start.14 = (f32[864,128]{1,0:T(8,128)S(1)}, f32[864,128]{1,0:T(8,128)S(1)}, u32[]{:S(2)}, u32[]{:S(2)}) collective-permute-start(f32[864,128]{1,0:T(8,128)S(1)} %patch_sums.20), channel_id=1, source_target_pairs={{0,2},{1,3},{2,4},{3,5},{4,6},{5,7},{6,0},{7,1},{8,10},{9,11},{10,... | collective-permute-start | bytes 1327112 | tf_op jit(solution)/shard_map/ppermute | solution.py:529
  62.0 5.4 %collective-permute-done.11.refs_1_ = f32[864,128]{1,0:T(8,128)S(1)} collective-permute-done((f32[864,128]{1,0:T(8,128)S(1)}, f32[864,128]{1,0:T(8,128)S(1)}, u32[]{:S(2)}, u32[]{:S(2)}) %collective-permute-start.11) | collective-permute-done | bytes 442400 | tf_op jit(solution)/shard_map/ppermute | solution.py:529
  68.7 2.1 %collective-permute-start.17 = (f32[864,128]{1,0:T(8,128)S(1)}, f32[864,128]{1,0:T(8,128)S(1)}, u32[]{:S(2)}, u32[]{:S(2)}) collective-permute-start(f32[864,128]{1,0:T(8,128)S(1)} %patch_sums.21), channel_id=1, source_target_pairs={{0,2},{1,3},{2,4},{3,5},{4,6},{5,7},{6,0},{7,1},{8,10},{9,11},{10,... | collective-permute-start | bytes 1327112 | tf_op jit(solution)/shard_map/ppermute | solution.py:529
  72.6 6.3 %collective-permute-start.12 = (f32[48,128]{1,0:T(8,128)S(1)}, f32[48,128]{1,0:T(8,128)S(1)}, u32[]{:S(2)}, u32[]{:S(2)}) collective-permute-start(f32[48,128]{1,0:T(8,128)S(1)} %get-tuple-element.155), channel_id=1, source_target_pairs={{0,8},{8,16},{16,24},{1,9},{9,17},{17,25},{2,10},{10,18},{18,26},{... | collective-permute-start | bytes 73736 | tf_op jit(solution)/shard_map/ppermute | solution.py:496
  78.9 1.9 %collective-permute-start.13 = (f32[48,128]{1,0:T(8,128)S(1)}, f32[48,128]{1,0:T(8,128)S(1)}, u32[]{:S(2)}, u32[]{:S(2)}) collective-permute-start(f32[48,128]{1,0:T(8,128)S(1)} %get-tuple-element.156), channel_id=1, source_target_pairs={{8,0},{16,8},{24,16},{9,1},{17,9},{25,17},{10,2},{18,10},{26,18},{... | collective-permute-start | bytes 73736 | tf_op jit(solution)/shard_map/ppermute | solution.py:496
  84.8 3.8 %collective-permute-start.16 = (f32[16,4,384]{2,1,0:T(4,128)S(1)}, f32[16,4,384]{2,1,0:T(4,128)S(1)}, u32[]{:S(2)}, u32[]{:S(2)}) collective-permute-start(f32[16,4,384]{2,1,0:T(4,128)S(1)} %get-tuple-element.170), channel_id=1, source_target_pairs={{0,7},{1,0},{2,1},{3,2},{4,3},{5,4},{6,5},{7,6},{8,15},{9,8},{10,9... | collective-permute-start | bytes 294920 | tf_op jit(solution)/shard_map/ppermute | solution.py:496
  89.1 2.7 %collective-permute-start.18 = (f32[48,128]{1,0:T(8,128)S(1)}, f32[48,128]{1,0:T(8,128)S(1)}, u32[]{:S(2)}, u32[]{:S(2)}) collective-permute-start(f32[48,128]{1,0:T(8,128)S(1)} %get-tuple-element.180), channel_id=1, source_target_pairs={{0,8},{8,16},{16,24},{1,9},{9,17},{17,25},{2,10},{10,18},{18,26},{... | collective-permute-start | bytes 73736 | tf_op jit(solution)/shard_map/ppermute | solution.py:496
  91.8 1.9 %collective-permute-start.19 = (f32[48,128]{1,0:T(8,128)S(1)}, f32[48,128]{1,0:T(8,128)S(1)}, u32[]{:S(2)}, u32[]{:S(2)}) collective-permute-start(f32[48,128]{1,0:T(8,128)S(1)} %get-tuple-element.181), channel_id=1, source_target_pairs={{8,0},{16,8},{24,16},{9,1},{17,9},{25,17},{10,2},{18,10},{26,18},{... | collective-permute-start | bytes 73736 | tf_op jit(solution)/shard_map/ppermute | solution.py:496
  93.8 3.4 %steps.3 = (f32[8,48,384]{2,1,0:T(8,128)}, f32[8,48,384]{2,1,0:T(8,128)}, f32[8,48,384]{2,1,0:T(8,128)}, f32[8,128]{1,0:T(8,128)S(1)}) custom-call(s32[4]{0:T(128)S(1)} %pad_add_fusion.odd.spot, s32[2,4]{1,0:T(2,128)S(1)} %copy-done.7, f32[2,48,384]{2,1,0:T(8,128)S(1)} %copy-done.3, f32[48,384]{1,0:T(8,128)S(1)} %copy-done.6, ...), custom_call_target="tpu_custom_call" | custom-call | tf_op jit(solution)/shard_map/steps/pallas_call | solution.py:470
  97.3 4.1 %collective-permute-start.21 = (f32[13,4,384]{2,1,0:T(4,128)S(1)}, f32[13,4,384]{2,1,0:T(4,128)S(1)}, u32[]{:S(2)}, u32[]{:S(2)}) collective-permute-start(f32[13,4,384]{2,1,0:T(4,128)S(1)} %get-tuple-element.189), channel_id=1, source_target_pairs={{0,7},{1,0},{2,1},{3,2},{4,3},{5,4},{6,5},{7,6},{8,15},{9,8},{10,9... | collective-permute-start | bytes 239624 | tf_op jit(solution)/shard_map/ppermute | solution.py:496
  101.4 3.4 %steps.4 = (f32[8,48,384]{2,1,0:T(8,128)}, f32[8,48,384]{2,1,0:T(8,128)}, f32[8,48,384]{2,1,0:T(8,128)}, f32[8,128]{1,0:T(8,128)}) custom-call(s32[4]{0:T(128)S(1)} %pad_add_fusion.odd.spot, s32[2,4]{1,0:T(2,128)S(1)} %copy-done.7, f32[2,48,384]{2,1,0:T(8,128)S(1)} %copy-done.3, ...), custom_call_target="tpu_custom_call", output_to_operand_aliasing={{0}: (15, {}), {1}: (16, {}), {2}: (17, {})} | custom-call | tf_op jit(solution)/shard_map/steps/pallas_call | solution.py:470
  104.8 5.5 %steps.5 = (f32[8,48,384]{2,1,0:T(8,128)}, f32[8,48,384]{2,1,0:T(8,128)}, f32[8,48,384]{2,1,0:T(8,128)}, f32[8,128]{1,0:T(8,128)}) custom-call(s32[4]{0:T(128)S(1)} %pad_add_fusion.odd.spot, s32[2,4]{1,0:T(2,128)S(1)} %copy-done.7, f32[2,48,384]{2,1,0:T(8,128)S(1)} %copy-done.3, ...), custom_call_target="tpu_custom_call", output_to_operand_aliasing={{0}: (15, {}), {1}: (16, {}), {2}: (17, {})} | custom-call | tf_op jit(solution)/shard_map/steps/pallas_call | solution.py:470
  (69 shorter events, 19.6 us)
Async XLA Ops:
  0.6 13.9 %collective-permute-start.1 = (s32[4,108]{1,0:T(4,128)}, s32[4,108]{1,0:T(4,128)S(1)}, u32[]{:S(2)}, u32[]{:S(2)}) collective-permute-start(s32[4,108]{1,0:T(4,128)} %bitcast.14), channel_id=1, source_target_pairs={{0,6},{1,7},{2,0},{3,1},{4,2},{5,3},{6,4},{7,5},{8,14},{9,15},{10,... | collective-permute-start | bytes 5192 | tf_op jit(solution)/shard_map/ppermute | solution.py:496
  4.9 9.8 %collective-permute-start = (s32[4,108]{1,0:T(4,128)}, s32[4,108]{1,0:T(4,128)S(1)}, u32[]{:S(2)}, u32[]{:S(2)}) collective-permute-start(s32[4,108]{1,0:T(4,128)} %bitcast.15), channel_id=1, source_target_pairs={{0,7},{1,0},{2,1},{3,2},{4,3},{5,4},{6,5},{7,6},{8,15},{9,8},{10,9... | collective-permute-start | bytes 5192 | tf_op jit(solution)/shard_map/ppermute | solution.py:496
  14.5 46.9 %copy-start = (f32[8,48,384]{2,1,0:T(8,128)S(1)}, f32[8,48,384]{2,1,0:T(8,128)}, u32[]{:S(2)}) copy-start(f32[8,48,384]{2,1,0:T(8,128)} %thickness.7) | copy-start | bytes 1769476
  14.6 12.3 %collective-permute-start.2 = (f32[648,128]{1,0:T(8,128)}, f32[648,128]{1,0:T(8,128)S(1)}, u32[]{:S(2)}, u32[]{:S(2)}) collective-permute-start(f32[648,128]{1,0:T(8,128)} %get-tuple-element.106), channel_id=1, source_target_pairs={{0,2},{1,3},{2,4},{3,5},{4,6},{5,7},{6,0},{7,1},{8,10},{9,11},{10,... | collective-permute-start | bytes 995336 | tf_op jit(solution)/shard_map/ppermute | solution.py:529
  16.0 15.8 %collective-permute-start.3 = (f32[648,128]{1,0:T(8,128)}, f32[648,128]{1,0:T(8,128)S(1)}, u32[]{:S(2)}, u32[]{:S(2)}) collective-permute-start(f32[648,128]{1,0:T(8,128)} %get-tuple-element.109), channel_id=1, source_target_pairs={{0,2},{1,3},{2,4},{3,5},{4,6},{5,7},{6,0},{7,1},{8,10},{9,11},{10,... | collective-permute-start | bytes 995336 | tf_op jit(solution)/shard_map/ppermute | solution.py:529
  16.1 22.9 %collective-permute-start.4 = (f32[648,128]{1,0:T(8,128)}, f32[648,128]{1,0:T(8,128)S(1)}, u32[]{:S(2)}, u32[]{:S(2)}) collective-permute-start(f32[648,128]{1,0:T(8,128)} %get-tuple-element.112), channel_id=1, source_target_pairs={{0,2},{1,3},{2,4},{3,5},{4,6},{5,7},{6,0},{7,1},{8,10},{9,11},{10,... | collective-permute-start | bytes 995336 | tf_op jit(solution)/shard_map/ppermute | solution.py:529
  26.9 66.9 %copy-start.7 = (s32[2,4]{1,0:T(2,128)S(1)}, s32[2,4]{1,0:T(2,128)}, u32[]{:S(2)}) copy-start(s32[2,4]{1,0:T(2,128)} %rotation.5) | copy-start | bytes 100
  28.9 12.5 %collective-permute-start.5 = (f32[864,128]{1,0:T(8,128)S(1)}, f32[864,128]{1,0:T(8,128)S(1)}, u32[]{:S(2)}, u32[]{:S(2)}) collective-permute-start(f32[864,128]{1,0:T(8,128)S(1)} %patch_sums.12), channel_id=1, source_target_pairs={{0,1},{2,3},{4,5},{6,7},{1,0},{3,2},{5,4},{7,6},{8,9},{10,11},{12,... | collective-permute-start | bytes 1327112 | tf_op jit(solution)/shard_map/ppermute | solution.py:529
  29.0 17.0 %collective-permute-start.6 = (f32[648,128]{1,0:T(8,128)S(1)}, f32[648,128]{1,0:T(8,128)S(1)}, u32[]{:S(2)}, u32[]{:S(2)}) collective-permute-start(f32[648,128]{1,0:T(8,128)S(1)} %copy-done.10), channel_id=1, source_target_pairs={{0,2},{1,3},{2,4},{3,5},{4,6},{5,7},{6,0},{7,1},{8,10},{9,11},{10,... | collective-permute-start | bytes 995336 | tf_op jit(solution)/shard_map/ppermute | solution.py:529
  33.8 14.7 %collective-permute-start.7 = (f32[864,128]{1,0:T(8,128)S(1)}, f32[864,128]{1,0:T(8,128)S(1)}, u32[]{:S(2)}, u32[]{:S(2)}) collective-permute-start(f32[864,128]{1,0:T(8,128)S(1)} %patch_sums.13), channel_id=1, source_target_pairs={{0,1},{2,3},{4,5},{6,7},{1,0},{3,2},{5,4},{7,6},{8,9},{10,11},{12,... | collective-permute-start | bytes 1327112 | tf_op jit(solution)/shard_map/ppermute | solution.py:529
  40.9 17.0 %collective-permute-start.9 = (f32[864,128]{1,0:T(8,128)S(1)}, f32[864,128]{1,0:T(8,128)S(1)}, u32[]{:S(2)}, u32[]{:S(2)}) collective-permute-start(f32[864,128]{1,0:T(8,128)S(1)} %patch_sums.14), channel_id=1, source_target_pairs={{0,1},{2,3},{4,5},{6,7},{1,0},{3,2},{5,4},{7,6},{8,9},{10,11},{12,... | collective-permute-start | bytes 1327112 | tf_op jit(solution)/shard_map/ppermute | solution.py:529
  42.8 18.6 %collective-permute-start.10 = (f32[864,128]{1,0:T(8,128)S(1)}, f32[864,128]{1,0:T(8,128)S(1)}, u32[]{:S(2)}, u32[]{:S(2)}) collective-permute-start(f32[864,128]{1,0:T(8,128)S(1)} %patch_sums.15), channel_id=1, source_target_pairs={{0,2},{1,3},{2,4},{3,5},{4,6},{5,7},{6,0},{7,1},{8,10},{9,11},{10,... | collective-permute-start | bytes 1327112 | tf_op jit(solution)/shard_map/ppermute | solution.py:529
  48.0 19.4 %collective-permute-start.11 = (f32[864,128]{1,0:T(8,128)S(1)}, f32[864,128]{1,0:T(8,128)S(1)}, u32[]{:S(2)}, u32[]{:S(2)}) collective-permute-start(f32[864,128]{1,0:T(8,128)S(1)} %patch_sums.16), channel_id=1, source_target_pairs={{0,1},{2,3},{4,5},{6,7},{1,0},{3,2},{5,4},{7,6},{8,9},{10,11},{12,... | collective-permute-start | bytes 1327112 | tf_op jit(solution)/shard_map/ppermute | solution.py:529
  49.9 22.3 %collective-permute-start.8 = (f32[864,128]{1,0:T(8,128)S(1)}, f32[864,128]{1,0:T(8,128)S(1)}, u32[]{:S(2)}, u32[]{:S(2)}) collective-permute-start(f32[864,128]{1,0:T(8,128)S(1)} %patch_sums.17), channel_id=1, source_target_pairs={{0,2},{1,3},{2,4},{3,5},{4,6},{5,7},{6,0},{7,1},{8,10},{9,11},{10,... | collective-permute-start | bytes 1327112 | tf_op jit(solution)/shard_map/ppermute | solution.py:529
  59.2 21.6 %collective-permute-start.14 = (f32[864,128]{1,0:T(8,128)S(1)}, f32[864,128]{1,0:T(8,128)S(1)}, u32[]{:S(2)}, u32[]{:S(2)}) collective-permute-start(f32[864,128]{1,0:T(8,128)S(1)} %patch_sums.20), channel_id=1, source_target_pairs={{0,2},{1,3},{2,4},{3,5},{4,6},{5,7},{6,0},{7,1},{8,10},{9,11},{10,... | collective-permute-start | bytes 1327112 | tf_op jit(solution)/shard_map/ppermute | solution.py:529
  68.7 19.9 %collective-permute-start.17 = (f32[864,128]{1,0:T(8,128)S(1)}, f32[864,128]{1,0:T(8,128)S(1)}, u32[]{:S(2)}, u32[]{:S(2)}) collective-permute-start(f32[864,128]{1,0:T(8,128)S(1)} %patch_sums.21), channel_id=1, source_target_pairs={{0,2},{1,3},{2,4},{3,5},{4,6},{5,7},{6,0},{7,1},{8,10},{9,11},{10,... | collective-permute-start | bytes 1327112 | tf_op jit(solution)/shard_map/ppermute | solution.py:529
  72.6 10.1 %collective-permute-start.12 = (f32[48,128]{1,0:T(8,128)S(1)}, f32[48,128]{1,0:T(8,128)S(1)}, u32[]{:S(2)}, u32[]{:S(2)}) collective-permute-start(f32[48,128]{1,0:T(8,128)S(1)} %get-tuple-element.155), channel_id=1, source_target_pairs={{0,8},{8,16},{16,24},{1,9},{9,17},{17,25},{2,10},{10,18},{18,26},{... | collective-permute-start | bytes 73736 | tf_op jit(solution)/shard_map/ppermute | solution.py:496
  78.9 5.4 %collective-permute-start.13 = (f32[48,128]{1,0:T(8,128)S(1)}, f32[48,128]{1,0:T(8,128)S(1)}, u32[]{:S(2)}, u32[]{:S(2)}) collective-permute-start(f32[48,128]{1,0:T(8,128)S(1)} %get-tuple-element.156), channel_id=1, source_target_pairs={{8,0},{16,8},{24,16},{9,1},{17,9},{25,17},{10,2},{18,10},{26,18},{... | collective-permute-start | bytes 73736 | tf_op jit(solution)/shard_map/ppermute | solution.py:496
  84.4 9.3 %collective-permute-start.15 = (f32[16,4,384]{2,1,0:T(4,128)S(1)}, f32[16,4,384]{2,1,0:T(4,128)S(1)}, u32[]{:S(2)}, u32[]{:S(2)}) collective-permute-start(f32[16,4,384]{2,1,0:T(4,128)S(1)} %get-tuple-element.169), channel_id=1, source_target_pairs={{0,1},{1,2},{2,3},{3,4},{4,5},{5,6},{6,7},{7,0},{8,9},{9,10},{10,1... | collective-permute-start | bytes 294920 | tf_op jit(solution)/shard_map/ppermute | solution.py:496
  84.8 8.9 %collective-permute-start.16 = (f32[16,4,384]{2,1,0:T(4,128)S(1)}, f32[16,4,384]{2,1,0:T(4,128)S(1)}, u32[]{:S(2)}, u32[]{:S(2)}) collective-permute-start(f32[16,4,384]{2,1,0:T(4,128)S(1)} %get-tuple-element.170), channel_id=1, source_target_pairs={{0,7},{1,0},{2,1},{3,2},{4,3},{5,4},{6,5},{7,6},{8,15},{9,8},{10,9... | collective-permute-start | bytes 294920 | tf_op jit(solution)/shard_map/ppermute | solution.py:496
  89.1 8.1 %collective-permute-start.18 = (f32[48,128]{1,0:T(8,128)S(1)}, f32[48,128]{1,0:T(8,128)S(1)}, u32[]{:S(2)}, u32[]{:S(2)}) collective-permute-start(f32[48,128]{1,0:T(8,128)S(1)} %get-tuple-element.180), channel_id=1, source_target_pairs={{0,8},{8,16},{16,24},{1,9},{9,17},{17,25},{2,10},{10,18},{18,26},{... | collective-permute-start | bytes 73736 | tf_op jit(solution)/shard_map/ppermute | solution.py:496
  91.8 5.4 %collective-permute-start.19 = (f32[48,128]{1,0:T(8,128)S(1)}, f32[48,128]{1,0:T(8,128)S(1)}, u32[]{:S(2)}, u32[]{:S(2)}) collective-permute-start(f32[48,128]{1,0:T(8,128)S(1)} %get-tuple-element.181), channel_id=1, source_target_pairs={{8,0},{16,8},{24,16},{9,1},{17,9},{25,17},{10,2},{18,10},{26,18},{... | collective-permute-start | bytes 73736 | tf_op jit(solution)/shard_map/ppermute | solution.py:496
  97.2 7.6 %collective-permute-start.20 = (f32[13,4,384]{2,1,0:T(4,128)S(1)}, f32[13,4,384]{2,1,0:T(4,128)S(1)}, u32[]{:S(2)}, u32[]{:S(2)}) collective-permute-start(f32[13,4,384]{2,1,0:T(4,128)S(1)} %get-tuple-element.188), channel_id=1, source_target_pairs={{0,1},{1,2},{2,3},{3,4},{4,5},{5,6},{6,7},{7,0},{8,9},{9,10},{10,1... | collective-permute-start | bytes 239624 | tf_op jit(solution)/shard_map/ppermute | solution.py:496
  97.3 7.5 %collective-permute-start.21 = (f32[13,4,384]{2,1,0:T(4,128)S(1)}, f32[13,4,384]{2,1,0:T(4,128)S(1)}, u32[]{:S(2)}, u32[]{:S(2)}) collective-permute-start(f32[13,4,384]{2,1,0:T(4,128)S(1)} %get-tuple-element.189), channel_id=1, source_target_pairs={{0,7},{1,0},{2,1},{3,2},{4,3},{5,4},{6,5},{7,6},{8,15},{9,8},{10,9... | collective-permute-start | bytes 239624 | tf_op jit(solution)/shard_map/ppermute | solution.py:496
  (9 other events, 317.1 us)

commit v6 on v5

--- a/solution.py
+++ b/solution.py
@@ -383,10 +383,15 @@
     return face * jnp.where(face > 0.0, behind, ahead)
 
 
-def steps_kernel(skipped, total_rows, spot, rotation, diag, cross, *refs):
-    metric_halos, halos, parts = refs[:4], refs[4:8], refs[8 : 8 + FIELDS]
-    outs, done, rimmed, wall = refs[-FIELDS - 3 : -3], refs[-3], refs[-2], refs[-1]
-    done[...] = jnp.zeros_like(done)
+def steps_kernel(skipped, total_rows, given, *refs):
+    if given == 2:
+        spot, rotation, *refs = refs
+    metric, refs = refs[:given], refs[given:]
+    halos, parts = refs[:4], refs[4 : 4 + FIELDS]
+    if given == 2:
+        outs, (rimmed, factors, wall) = refs[-FIELDS - 3 : -3], refs[-3:]
+    else:
+        outs, (rimmed, factors, wall) = refs[-FIELDS:], metric
     rows, cols = parts[0].shape[1:]
     ext_rows, ext_cols = rows + SUB, cols + TPATCH
     panel_rows = total_rows // PANELS
@@ -402,24 +407,30 @@
 
     @pl.when(pl.program_id(0) == 0)
     def _():
-        below, above = metric_halos[:2]
-        sides, entry = columns(*metric_halos), below.shape[0] - 1 - FIELDS
-        for f in range(FIELDS):
-            core = cross[...] if f == FIELDS - 1 else diag[f]
-            lanes = TPATCH - (FIELDS - f) * HALO
-            rimmed[f] = with_rim(core, above[entry + f], below[entry + f], lanes, sides) * (COURANT * 0.5)
-        column = lax.broadcasted_iota(jnp.int32, wall.shape, 1)
-        walled = ((spot[2] == 0) & (column == 0)) | ((spot[2] == spot[3] - 1) & (column == cols))
-        wall[...] = jnp.where(walled, 0.0, 1.0)
-
-    turns = []
-    for edge in (0, rows):
-        upper = lax.rem(spot[1] * rows + edge, total_rows)
-        lower = lax.rem(upper + total_rows - 1, total_rows)
-        joint = lax.rem(upper, panel_rows) == 0
-        codes = [rotation[0, upper // panel_rows], rotation[1, lower // panel_rows]]
-        turns.append([factor for code in codes for factor in quarter_turn(jnp.where(joint, code, 0))])
-
+        if given == 2:
+            diag, cross = metric
+            below, above = halos[:2]
+            sides, entry = columns(*halos), below.shape[0] - 1 - FIELDS
+            for f in range(FIELDS):
+                core = cross[...] if f == FIELDS - 1 else diag[f]
+                lanes = TPATCH - (FIELDS - f) * HALO
+                rimmed[f] = with_rim(core, above[entry + f], below[entry + f], lanes, sides) * (COURANT * 0.5)
+            column = lax.broadcasted_iota(jnp.int32, wall.shape, 1)
+            walled = ((spot[2] == 0) & (column == 0)) | ((spot[2] == spot[3] - 1) & (column == cols))
+            wall[...] = jnp.where(walled, 0.0, 1.0)
+            row = lax.broadcasted_iota(jnp.int32, factors.shape, 0)
+            value, n = jnp.zeros(factors.shape, jnp.float32), 0
+            for edge in (0, rows):
+                upper = lax.rem(spot[1] * rows + edge, total_rows)
+                lower = lax.rem(upper + total_rows - 1, total_rows)
+                joint = lax.rem(upper, panel_rows) == 0
+                for code in (rotation[0, upper // panel_rows], rotation[1, lower // panel_rows]):
+                    for factor in quarter_turn(jnp.where(joint, code, 0)):
+                        value, n = jnp.where(row == n, factor, value), n + 1
+            factors[...] = value
+
+    wide = lambda n: jnp.concatenate([factors[n : n + 1, :]] * (ext_cols // TPATCH), axis=1)
+    turns = [[wide(4 * joint + n) for n in range(4)] for joint in range(2)]
     sides = columns(*halos)
     depth, cov_first, cov_second = (
         with_rim(
@@ -460,28 +471,28 @@
         ref[0] = value[:rows, :cols]
 
 
-def steps(first, count, skipped, total_rows, spot, rotation, diag, cross, metric_halos, halos, parts, so_far):
+def steps(first, count, skipped, total_rows, spot, rotation, metric, halos, parts, so_far):
     levels, rows, cols = parts[0].shape
     assert total_rows // PANELS % rows == 0
-    fixed = lambda array: pl.BlockSpec(array.shape, lambda l: (0,) * array.ndim)
+    fixed = lambda shape: pl.BlockSpec(shape, lambda l: (0,) * len(shape))
     of_level = pl.BlockSpec((1, rows, cols), lambda l: (first + l, 0, 0))
-    given = (diag, cross, *metric_halos, *halos)
-    before = 2 + len(given) + len(parts)
+    given = (*metric, *halos)
+    before = (2 if len(metric) == 2 else 0) + len(given) + len(parts)
+    new = len(metric) == 2
+    kept = [(FIELDS, rows + SUB, cols + TPATCH), (SUB, TPATCH), (SUB, cols + TPATCH)] if new else []
     return pl.pallas_call(
-        functools.partial(steps_kernel, skipped, total_rows),
+        functools.partial(steps_kernel, skipped, total_rows, len(metric)),
         grid=(count,),
-        in_specs=in_smem(2) + [fixed(array) for array in given] + [of_level] * FIELDS + in_hbm(len(so_far)),
-        out_specs=[of_level] * FIELDS + [pl.BlockSpec((SUB, TPATCH), lambda l: (0, 0))],
-        out_shape=[jax.ShapeDtypeStruct((levels, rows, cols), jnp.float32)] * FIELDS
-        + [jax.ShapeDtypeStruct((SUB, TPATCH), jnp.float32)],
+        in_specs=in_smem(2 if new else 0)
+        + [fixed(array.shape) for array in given]
+        + [of_level] * FIELDS
+        + in_hbm(len(so_far)),
+        out_specs=[of_level] * FIELDS + [fixed(shape) for shape in kept],
+        out_shape=[jax.ShapeDtypeStruct(shape, jnp.float32) for shape in [(levels, rows, cols)] * FIELDS + kept],
         input_output_aliases={before + i: i for i in range(len(so_far))},
-        scratch_shapes=[
-            pltpu.VMEM((FIELDS, rows + SUB, cols + TPATCH), jnp.float32),
-            pltpu.VMEM((SUB, cols + TPATCH), jnp.float32),
-        ],
         compiler_params=params(32 * 2**20),
         name="steps",
-    )(spot, rotation, *given, *parts, *so_far)
+    )(*((spot, rotation) if new else ()), *given, *parts, *so_far)
 
 
 def quarter_turn(code):
@@ -546,9 +557,12 @@
     metric = (inv_metric_diag, inv_metric_cross)
     token, results, finished = spot, [], []
 
-    def steps_on(n, first, count, results):
+    def steps_on(n, first, count, results, rimmed):
         skipped = first - bounds[GROUPS[n][0]]
-        return steps(first, count, skipped, rows * ty_count, spot, rotation, *metric, halos[0], halos[n], fields, results)
+        out = steps(
+            first, count, skipped, rows * ty_count, spot, rotation, rimmed or metric, halos[n], fields, results
+        )
+        return out[:FIELDS], rimmed or out[FIELDS:]
 
     across, last, settled, ends, sides, fields, halos = {}, {}, {}, {}, {}, [], []
     for step in ORDER:
@@ -583,16 +597,15 @@
 
             if n == len(GROUPS) - 1:
                 for first, count in EARLY:
-                    *results, finished = steps_on(0, first, count, results)
-                    finished = [finished]
+                    results, finished = steps_on(0, first, count, results, finished)
             waited = finished if n else [settled[parts - 1], *sides.get(1, [])[:1]]
-            high_rows, low_rows = reversed(last_entries(1 if n else 1 + FIELDS, ends[n], *metric, beside, waited))
+            high_rows, low_rows = reversed(last_entries(1 if n else 1 + FIELDS, ends[n], *metric, beside, waited[:1] if n else waited))
             halos.append([shift(high_rows, "ty", 1, True), shift(low_rows, "ty", -1, True), *beside])
 
     done = EARLY[-1][0] + EARLY[-1][1] if EARLY else 0
     for n, group in enumerate(GROUPS):
         first, end = max(done, bounds[group[0]]), bounds[group[-1] + 1]
-        *results, _ = steps_on(n, first, end - first, results)
+        results, finished = steps_on(n, first, end - first, results, finished)
     return tuple(results)
 
 

time: 111 us -> 109 us (0.982)
    pallas_call x3, Pallas kernels: 12.3 us -> 11.2 us  [steps(): pl.pallas_call(functools.partial(steps_kernel, skipped, total_rows, len(m...]
  transfers between devices with their start and end apart: 22 -> 22, of which waited for: 5 -> 7; matrix products, arithmetic and copies ran while one was open for 0% -> 0% of each run, Pallas kernels for 42% -> 42%
where the time goes in v6:
time: 109 us
  Pallas kernels  50.9 us (47%)
  starting transfers between devices  38.7 us (36%)
  waiting for transfers between devices  18.4 us (17%)
    ppermute x10, starting transfers between devices, shift(): return lax.ppermute(array, axis, pairs)  26.6 us
    pallas_call x12, Pallas kernels, patch_sums(): pl.pallas_call(functools.partial(sum_kernel, which, parity, patches), in_...  18.3 us
    ppermute x12, waiting for transfers between devices, body(): send = lambda array, pairs: lax.ppermute(array, 'ty', pairs)  16.7 us
    ppermute x12, starting transfers between devices, body(): send = lambda array, pairs: lax.ppermute(array, 'ty', pairs)  12.1 us
    pallas_call x3, Pallas kernels, steps(): pl.pallas_call(functools.partial(steps_kernel, skipped, total_rows, len(m...  11.2 us
    pallas_call x1, Pallas kernels, terms(): pl.pallas_call(functools.partial(terms_kernel, cuts, len(later), group, c...  10.8 us
    pallas_call x1, Pallas kernels, far_terms(): pl.pallas_call(functools.partial(far_terms_kernel, bounds, owners - 1), i...  8.56 us
  transfers between devices with their start and end apart: 22, of which 7 were waited for; matrix products, arithmetic and copies ran while one was open for 0% of the time, Pallas kernels for 42%

profile of v6, /device:TPU:1, one launch (start us, length us, event | category | flops | bytes accessed | tf_op | source)
XLA Modules:
  0.0 109.2 jit_solution(15977708267586632156)
XLA Ops:
  0.6 4.2 %collective-permute-start.1 = (s32[4,108]{1,0:T(4,128)}, s32[4,108]{1,0:T(4,128)S(1)}, u32[]{:S(2)}, u32[]{:S(2)}) collective-permute-start(s32[4,108]{1,0:T(4,128)} %bitcast.14), channel_id=1, source_target_pairs={{0,6},{1,7},{2,0},{3,1},{4,2},{5,3},{6,4},{7,5},{8,14},{9,15},{10,... | collective-permute-start | bytes 5192 | tf_op jit(solution)/shard_map/ppermute | solution.py:507
  6.0 8.6 %far_terms.1 = (f32[648,128]{1,0:T(8,128)}, f32[648,128]{1,0:T(8,128)}, f32[648,128]{1,0:T(8,128)}, f32[648,128]{1,0:T(8,128)}) custom-call(s32[2,144]{1,0:T(2,128)} %bitcast.10, bf16[3,8,144,256]{3,2,1,0:T(8,128)(2,1)} %increments.3, bf16[288,128,256]{2,1,0:T(8,128)(2,1)} %bitcast.12), custom_call_target="tpu_custom_call" | custom-call | tf_op jit(solution)/shard_map/far_terms/pallas_call | solution.py:128
  16.1 10.8 %terms.1 = (f32[648,128]{1,0:T(8,128)S(1)}, f32[648,128]{1,0:T(8,128)S(1)}, f32[648,128]{1,0:T(8,128)S(1)}, f32[648,128]{1,0:T(8,128)S(1)}, f32[648,128]{1,0:T(8...) custom-call(s32[2,144]{1,0:T(2,128)S(1)} %bitcast.11, ...), custom_call_target="tpu_custom_call" | custom-call | bytes 18874368 | tf_op jit(solution)/shard_map/terms/pallas_call | solution.py:194
  26.9 2.0 %patch_sums.12 = f32[864,128]{1,0:T(8,128)S(1)} custom-call(s32[4]{0:T(128)S(1)} %pad_add_fusion.odd.refs_0_, s32[4,108]{1,0:T(4,128)S(1)} %fusion.2.places, f32[648,128]{1,0:T(8,128)S(1)} %collective-permute-done.2.refs_0_, f32[648,128]{1,0:T(8,128)S(1)} %get-tuple-element.106.refs_1_), custom_call_target="tpu_custom_call" | custom-call | tf_op jit(solution)/shard_map/patch_sums/pallas_call | solution.py:256
  29.0 2.7 %collective-permute-start.6 = (f32[648,128]{1,0:T(8,128)S(1)}, f32[648,128]{1,0:T(8,128)S(1)}, u32[]{:S(2)}, u32[]{:S(2)}) collective-permute-start(f32[648,128]{1,0:T(8,128)S(1)} %copy-done.10), channel_id=1, source_target_pairs={{0,2},{1,3},{2,4},{3,5},{4,6},{5,7},{6,0},{7,1},{8,10},{9,11},{10,... | collective-permute-start | bytes 995336 | tf_op jit(solution)/shard_map/ppermute | solution.py:540
  31.8 2.0 %patch_sums.13 = f32[864,128]{1,0:T(8,128)S(1)} custom-call(s32[4]{0:T(128)S(1)} %pad_add_fusion.odd.refs_0_, s32[4,108]{1,0:T(4,128)S(1)} %fusion.2.places, f32[648,128]{1,0:T(8,128)S(1)} %collective-permute-done.3.refs_0_, f32[648,128]{1,0:T(8,128)S(1)} %get-tuple-element.109.refs_1_), custom_call_target="tpu_custom_call" | custom-call | tf_op jit(solution)/shard_map/patch_sums/pallas_call | solution.py:256
  35.0 4.0 %collective-permute-done.4.refs_0_ = f32[648,128]{1,0:T(8,128)S(1)} collective-permute-done((f32[648,128]{1,0:T(8,128)}, f32[648,128]{1,0:T(8,128)S(1)}, u32[]{:S(2)}, u32[]{:S(2)}) %collective-permute-start.4) | collective-permute-done | bytes 331808 | tf_op jit(solution)/shard_map/ppermute | solution.py:540
  39.0 2.0 %patch_sums.14 = f32[864,128]{1,0:T(8,128)S(1)} custom-call(s32[4]{0:T(128)S(1)} %pad_add_fusion.odd.refs_0_, s32[4,108]{1,0:T(4,128)S(1)} %fusion.2.places, f32[648,128]{1,0:T(8,128)S(1)} %collective-permute-done.4.refs_0_, f32[648,128]{1,0:T(8,128)S(1)} %get-tuple-element.112.refs_1_), custom_call_target="tpu_custom_call" | custom-call | tf_op jit(solution)/shard_map/patch_sums/pallas_call | solution.py:256
  42.5 3.5 %collective-permute-done.6.refs_0_ = f32[648,128]{1,0:T(8,128)S(1)} collective-permute-done((f32[648,128]{1,0:T(8,128)S(1)}, f32[648,128]{1,0:T(8,128)S(1)}, u32[]{:S(2)}, u32[]{:S(2)}) %collective-permute-start.6) | collective-permute-done | bytes 331808 | tf_op jit(solution)/shard_map/ppermute | solution.py:540
  46.1 2.0 %patch_sums.16 = f32[864,128]{1,0:T(8,128)S(1)} custom-call(s32[4]{0:T(128)S(1)} %pad_add_fusion.odd.refs_0_, s32[4,108]{1,0:T(4,128)S(1)} %fusion.2.places, f32[648,128]{1,0:T(8,128)S(1)} %collective-permute-done.6.refs_0_, f32[648,128]{1,0:T(8,128)S(1)} %get-tuple-element.119.refs_1_), custom_call_target="tpu_custom_call" | custom-call | tf_op jit(solution)/shard_map/patch_sums/pallas_call | solution.py:256
  49.7 2.2 %collective-permute-start.8 = (f32[864,128]{1,0:T(8,128)S(1)}, f32[864,128]{1,0:T(8,128)S(1)}, u32[]{:S(2)}, u32[]{:S(2)}) collective-permute-start(f32[864,128]{1,0:T(8,128)S(1)} %patch_sums.17), channel_id=1, source_target_pairs={{0,2},{1,3},{2,4},{3,5},{4,6},{5,7},{6,0},{7,1},{8,10},{9,11},{10,... | collective-permute-start | bytes 1327112 | tf_op jit(solution)/shard_map/ppermute | solution.py:540
  54.4 3.4 %collective-permute-done.9.refs_1_ = f32[864,128]{1,0:T(8,128)S(1)} collective-permute-done((f32[864,128]{1,0:T(8,128)S(1)}, f32[864,128]{1,0:T(8,128)S(1)}, u32[]{:S(2)}, u32[]{:S(2)}) %collective-permute-start.9) | collective-permute-done | bytes 442400 | tf_op jit(solution)/shard_map/ppermute | solution.py:540
  59.2 2.2 %collective-permute-start.14 = (f32[864,128]{1,0:T(8,128)S(1)}, f32[864,128]{1,0:T(8,128)S(1)}, u32[]{:S(2)}, u32[]{:S(2)}) collective-permute-start(f32[864,128]{1,0:T(8,128)S(1)} %patch_sums.20), channel_id=1, source_target_pairs={{0,2},{1,3},{2,4},{3,5},{4,6},{5,7},{6,0},{7,1},{8,10},{9,11},{10,... | collective-permute-start | bytes 1327112 | tf_op jit(solution)/shard_map/ppermute | solution.py:540
  62.0 5.3 %collective-permute-done.11.refs_1_ = f32[864,128]{1,0:T(8,128)S(1)} collective-permute-done((f32[864,128]{1,0:T(8,128)S(1)}, f32[864,128]{1,0:T(8,128)S(1)}, u32[]{:S(2)}, u32[]{:S(2)}) %collective-permute-start.11) | collective-permute-done | bytes 442400 | tf_op jit(solution)/shard_map/ppermute | solution.py:540
  68.7 2.2 %collective-permute-start.17 = (f32[864,128]{1,0:T(8,128)S(1)}, f32[864,128]{1,0:T(8,128)S(1)}, u32[]{:S(2)}, u32[]{:S(2)}) collective-permute-start(f32[864,128]{1,0:T(8,128)S(1)} %patch_sums.21), channel_id=1, source_target_pairs={{0,2},{1,3},{2,4},{3,5},{4,6},{5,7},{6,0},{7,1},{8,10},{9,11},{10,... | collective-permute-start | bytes 1327112 | tf_op jit(solution)/shard_map/ppermute | solution.py:540
  72.6 6.3 %collective-permute-start.12 = (f32[48,128]{1,0:T(8,128)S(1)}, f32[48,128]{1,0:T(8,128)S(1)}, u32[]{:S(2)}, u32[]{:S(2)}) collective-permute-start(f32[48,128]{1,0:T(8,128)S(1)} %get-tuple-element.154), channel_id=1, source_target_pairs={{0,8},{8,16},{16,24},{1,9},{9,17},{17,25},{2,10},{10,18},{18,26},{... | collective-permute-start | bytes 73736 | tf_op jit(solution)/shard_map/ppermute | solution.py:507
  78.9 1.9 %collective-permute-start.13 = (f32[48,128]{1,0:T(8,128)S(1)}, f32[48,128]{1,0:T(8,128)S(1)}, u32[]{:S(2)}, u32[]{:S(2)}) collective-permute-start(f32[48,128]{1,0:T(8,128)S(1)} %get-tuple-element.155), channel_id=1, source_target_pairs={{8,0},{16,8},{24,16},{9,1},{17,9},{25,17},{10,2},{18,10},{26,18},{... | collective-permute-start | bytes 73736 | tf_op jit(solution)/shard_map/ppermute | solution.py:507
  84.8 3.8 %collective-permute-start.16 = (f32[16,4,384]{2,1,0:T(4,128)S(1)}, f32[16,4,384]{2,1,0:T(4,128)S(1)}, u32[]{:S(2)}, u32[]{:S(2)}) collective-permute-start(f32[16,4,384]{2,1,0:T(4,128)S(1)} %get-tuple-element.169), channel_id=1, source_target_pairs={{0,7},{1,0},{2,1},{3,2},{4,3},{5,4},{6,5},{7,6},{8,15},{9,8},{10,9... | collective-permute-start | bytes 294920 | tf_op jit(solution)/shard_map/ppermute | solution.py:507
  89.1 2.7 %collective-permute-start.18 = (f32[48,128]{1,0:T(8,128)S(1)}, f32[48,128]{1,0:T(8,128)S(1)}, u32[]{:S(2)}, u32[]{:S(2)}) collective-permute-start(f32[48,128]{1,0:T(8,128)S(1)} %get-tuple-element.185), channel_id=1, source_target_pairs={{0,8},{8,16},{16,24},{1,9},{9,17},{17,25},{2,10},{10,18},{18,26},{... | collective-permute-start | bytes 73736 | tf_op jit(solution)/shard_map/ppermute | solution.py:507
  91.8 1.9 %collective-permute-start.19 = (f32[48,128]{1,0:T(8,128)S(1)}, f32[48,128]{1,0:T(8,128)S(1)}, u32[]{:S(2)}, u32[]{:S(2)}) collective-permute-start(f32[48,128]{1,0:T(8,128)S(1)} %get-tuple-element.186), channel_id=1, source_target_pairs={{8,0},{16,8},{24,16},{9,1},{17,9},{25,17},{10,2},{18,10},{26,18},{... | collective-permute-start | bytes 73736 | tf_op jit(solution)/shard_map/ppermute | solution.py:507
  93.8 3.5 %steps.3 = (f32[8,48,384]{2,1,0:T(8,128)}, f32[8,48,384]{2,1,0:T(8,128)}, f32[8,48,384]{2,1,0:T(8,128)}, f32[3,56,512]{2,1,0:T(8,128)S(1)}, f32[8,128]{1,0:T(8,128)S(1)}, /*index=5*/f32[8,512]{1,0:T(8,128)S(1)}) custom-call(s32[4]{0:T(128)S(1)} %pad_add_fusion.odd.refs_0_, s32[2,4]{1,0:T(2,128)S(1)} %copy-done.8, f32[2,48,384]{2,1,0:T(8,128)S(1)} %copy-done.5, ...), custom_call_target="tpu_custom_call" | custom-call | tf_op jit(solution)/shard_map/steps/pallas_call | solution.py:483
  97.4 4.1 %collective-permute-start.21 = (f32[13,4,384]{2,1,0:T(4,128)S(1)}, f32[13,4,384]{2,1,0:T(4,128)S(1)}, u32[]{:S(2)}, u32[]{:S(2)}) collective-permute-start(f32[13,4,384]{2,1,0:T(4,128)S(1)} %get-tuple-element.190), channel_id=1, source_target_pairs={{0,7},{1,0},{2,1},{3,2},{4,3},{5,4},{6,5},{7,6},{8,15},{9,8},{10,9... | collective-permute-start | bytes 239624 | tf_op jit(solution)/shard_map/ppermute | solution.py:507
  101.5 2.7 %steps.4 = (f32[8,48,384]{2,1,0:T(8,128)}, f32[8,48,384]{2,1,0:T(8,128)}, f32[8,48,384]{2,1,0:T(8,128)}) custom-call(f32[3,56,512]{2,1,0:T(8,128)S(1)} %get-tuple-element.180.refs_2_.refs_0_, f32[8,128]{1,0:T(8,128)S(1)} %get-tuple-element.181.refs_1_, ...), custom_call_target="tpu_custom_call", output_to_operand_aliasing={{0}: (10, {}), {1}: (11, {}), {2}: (12, {})} | custom-call | tf_op jit(solution)/shard_map/steps/pallas_call | solution.py:483
  104.3 4.9 %steps.5 = (f32[8,48,384]{2,1,0:T(8,128)}, f32[8,48,384]{2,1,0:T(8,128)}, f32[8,48,384]{2,1,0:T(8,128)}) custom-call(f32[3,56,512]{2,1,0:T(8,128)S(1)} %get-tuple-element.180.refs_2_.refs_0_, f32[8,128]{1,0:T(8,128)S(1)} %get-tuple-element.181.refs_1_, ...), custom_call_target="tpu_custom_call", output_to_operand_aliasing={{0}: (10, {}), {1}: (11, {}), {2}: (12, {})} | custom-call | tf_op jit(solution)/shard_map/steps/pallas_call | solution.py:483
  (69 shorter events, 19.3 us)
Async XLA Ops:
  0.6 14.0 %collective-permute-start.1 = (s32[4,108]{1,0:T(4,128)}, s32[4,108]{1,0:T(4,128)S(1)}, u32[]{:S(2)}, u32[]{:S(2)}) collective-permute-start(s32[4,108]{1,0:T(4,128)} %bitcast.14), channel_id=1, source_target_pairs={{0,6},{1,7},{2,0},{3,1},{4,2},{5,3},{6,4},{7,5},{8,14},{9,15},{10,... | collective-permute-start | bytes 5192 | tf_op jit(solution)/shard_map/ppermute | solution.py:507
  4.9 9.8 %collective-permute-start = (s32[4,108]{1,0:T(4,128)}, s32[4,108]{1,0:T(4,128)S(1)}, u32[]{:S(2)}, u32[]{:S(2)}) collective-permute-start(s32[4,108]{1,0:T(4,128)} %bitcast.15), channel_id=1, source_target_pairs={{0,7},{1,0},{2,1},{3,2},{4,3},{5,4},{6,5},{7,6},{8,15},{9,8},{10,9... | collective-permute-start | bytes 5192 | tf_op jit(solution)/shard_map/ppermute | solution.py:507
  14.5 46.8 %copy-start = (f32[8,48,384]{2,1,0:T(8,128)S(1)}, f32[8,48,384]{2,1,0:T(8,128)}, u32[]{:S(2)}) copy-start(f32[8,48,384]{2,1,0:T(8,128)} %thickness.7) | copy-start | bytes 1769476
  14.6 12.3 %collective-permute-start.2 = (f32[648,128]{1,0:T(8,128)}, f32[648,128]{1,0:T(8,128)S(1)}, u32[]{:S(2)}, u32[]{:S(2)}) collective-permute-start(f32[648,128]{1,0:T(8,128)} %get-tuple-element.105), channel_id=1, source_target_pairs={{0,2},{1,3},{2,4},{3,5},{4,6},{5,7},{6,0},{7,1},{8,10},{9,11},{10,... | collective-permute-start | bytes 995336 | tf_op jit(solution)/shard_map/ppermute | solution.py:540
  16.0 15.8 %collective-permute-start.3 = (f32[648,128]{1,0:T(8,128)}, f32[648,128]{1,0:T(8,128)S(1)}, u32[]{:S(2)}, u32[]{:S(2)}) collective-permute-start(f32[648,128]{1,0:T(8,128)} %get-tuple-element.108), channel_id=1, source_target_pairs={{0,2},{1,3},{2,4},{3,5},{4,6},{5,7},{6,0},{7,1},{8,10},{9,11},{10,... | collective-permute-start | bytes 995336 | tf_op jit(solution)/shard_map/ppermute | solution.py:540
  16.1 22.9 %collective-permute-start.4 = (f32[648,128]{1,0:T(8,128)}, f32[648,128]{1,0:T(8,128)S(1)}, u32[]{:S(2)}, u32[]{:S(2)}) collective-permute-start(f32[648,128]{1,0:T(8,128)} %get-tuple-element.111), channel_id=1, source_target_pairs={{0,2},{1,3},{2,4},{3,5},{4,6},{5,7},{6,0},{7,1},{8,10},{9,11},{10,... | collective-permute-start | bytes 995336 | tf_op jit(solution)/shard_map/ppermute | solution.py:540
  26.9 66.9 %copy-start.8 = (s32[2,4]{1,0:T(2,128)S(1)}, s32[2,4]{1,0:T(2,128)}, u32[]{:S(2)}) copy-start(s32[2,4]{1,0:T(2,128)} %refs_1_.5) | copy-start | bytes 100
  28.9 12.2 %collective-permute-start.5 = (f32[864,128]{1,0:T(8,128)S(1)}, f32[864,128]{1,0:T(8,128)S(1)}, u32[]{:S(2)}, u32[]{:S(2)}) collective-permute-start(f32[864,128]{1,0:T(8,128)S(1)} %patch_sums.12), channel_id=1, source_target_pairs={{0,1},{2,3},{4,5},{6,7},{1,0},{3,2},{5,4},{7,6},{8,9},{10,11},{12,... | collective-permute-start | bytes 1327112 | tf_op jit(solution)/shard_map/ppermute | solution.py:540
  29.0 17.1 %collective-permute-start.6 = (f32[648,128]{1,0:T(8,128)S(1)}, f32[648,128]{1,0:T(8,128)S(1)}, u32[]{:S(2)}, u32[]{:S(2)}) collective-permute-start(f32[648,128]{1,0:T(8,128)S(1)} %copy-done.10), channel_id=1, source_target_pairs={{0,2},{1,3},{2,4},{3,5},{4,6},{5,7},{6,0},{7,1},{8,10},{9,11},{10,... | collective-permute-start | bytes 995336 | tf_op jit(solution)/shard_map/ppermute | solution.py:540
  33.8 14.6 %collective-permute-start.7 = (f32[864,128]{1,0:T(8,128)S(1)}, f32[864,128]{1,0:T(8,128)S(1)}, u32[]{:S(2)}, u32[]{:S(2)}) collective-permute-start(f32[864,128]{1,0:T(8,128)S(1)} %patch_sums.13), channel_id=1, source_target_pairs={{0,1},{2,3},{4,5},{6,7},{1,0},{3,2},{5,4},{7,6},{8,9},{10,11},{12,... | collective-permute-start | bytes 1327112 | tf_op jit(solution)/shard_map/ppermute | solution.py:540
  40.9 16.9 %collective-permute-start.9 = (f32[864,128]{1,0:T(8,128)S(1)}, f32[864,128]{1,0:T(8,128)S(1)}, u32[]{:S(2)}, u32[]{:S(2)}) collective-permute-start(f32[864,128]{1,0:T(8,128)S(1)} %patch_sums.14), channel_id=1, source_target_pairs={{0,1},{2,3},{4,5},{6,7},{1,0},{3,2},{5,4},{7,6},{8,9},{10,11},{12,... | collective-permute-start | bytes 1327112 | tf_op jit(solution)/shard_map/ppermute | solution.py:540
  42.5 18.9 %collective-permute-start.10 = (f32[864,128]{1,0:T(8,128)S(1)}, f32[864,128]{1,0:T(8,128)S(1)}, u32[]{:S(2)}, u32[]{:S(2)}) collective-permute-start(f32[864,128]{1,0:T(8,128)S(1)} %patch_sums.15), channel_id=1, source_target_pairs={{0,2},{1,3},{2,4},{3,5},{4,6},{5,7},{6,0},{7,1},{8,10},{9,11},{10,... | collective-permute-start | bytes 1327112 | tf_op jit(solution)/shard_map/ppermute | solution.py:540
  48.0 19.3 %collective-permute-start.11 = (f32[864,128]{1,0:T(8,128)S(1)}, f32[864,128]{1,0:T(8,128)S(1)}, u32[]{:S(2)}, u32[]{:S(2)}) collective-permute-start(f32[864,128]{1,0:T(8,128)S(1)} %patch_sums.16), channel_id=1, source_target_pairs={{0,1},{2,3},{4,5},{6,7},{1,0},{3,2},{5,4},{7,6},{8,9},{10,11},{12,... | collective-permute-start | bytes 1327112 | tf_op jit(solution)/shard_map/ppermute | solution.py:540
  49.7 22.4 %collective-permute-start.8 = (f32[864,128]{1,0:T(8,128)S(1)}, f32[864,128]{1,0:T(8,128)S(1)}, u32[]{:S(2)}, u32[]{:S(2)}) collective-permute-start(f32[864,128]{1,0:T(8,128)S(1)} %patch_sums.17), channel_id=1, source_target_pairs={{0,2},{1,3},{2,4},{3,5},{4,6},{5,7},{6,0},{7,1},{8,10},{9,11},{10,... | collective-permute-start | bytes 1327112 | tf_op jit(solution)/shard_map/ppermute | solution.py:540
  59.2 21.7 %collective-permute-start.14 = (f32[864,128]{1,0:T(8,128)S(1)}, f32[864,128]{1,0:T(8,128)S(1)}, u32[]{:S(2)}, u32[]{:S(2)}) collective-permute-start(f32[864,128]{1,0:T(8,128)S(1)} %patch_sums.20), channel_id=1, source_target_pairs={{0,2},{1,3},{2,4},{3,5},{4,6},{5,7},{6,0},{7,1},{8,10},{9,11},{10,... | collective-permute-start | bytes 1327112 | tf_op jit(solution)/shard_map/ppermute | solution.py:540
  68.7 19.9 %collective-permute-start.17 = (f32[864,128]{1,0:T(8,128)S(1)}, f32[864,128]{1,0:T(8,128)S(1)}, u32[]{:S(2)}, u32[]{:S(2)}) collective-permute-start(f32[864,128]{1,0:T(8,128)S(1)} %patch_sums.21), channel_id=1, source_target_pairs={{0,2},{1,3},{2,4},{3,5},{4,6},{5,7},{6,0},{7,1},{8,10},{9,11},{10,... | collective-permute-start | bytes 1327112 | tf_op jit(solution)/shard_map/ppermute | solution.py:540
  72.6 10.1 %collective-permute-start.12 = (f32[48,128]{1,0:T(8,128)S(1)}, f32[48,128]{1,0:T(8,128)S(1)}, u32[]{:S(2)}, u32[]{:S(2)}) collective-permute-start(f32[48,128]{1,0:T(8,128)S(1)} %get-tuple-element.154), channel_id=1, source_target_pairs={{0,8},{8,16},{16,24},{1,9},{9,17},{17,25},{2,10},{10,18},{18,26},{... | collective-permute-start | bytes 73736 | tf_op jit(solution)/shard_map/ppermute | solution.py:507
  78.9 5.4 %collective-permute-start.13 = (f32[48,128]{1,0:T(8,128)S(1)}, f32[48,128]{1,0:T(8,128)S(1)}, u32[]{:S(2)}, u32[]{:S(2)}) collective-permute-start(f32[48,128]{1,0:T(8,128)S(1)} %get-tuple-element.155), channel_id=1, source_target_pairs={{8,0},{16,8},{24,16},{9,1},{17,9},{25,17},{10,2},{18,10},{26,18},{... | collective-permute-start | bytes 73736 | tf_op jit(solution)/shard_map/ppermute | solution.py:507
  84.4 9.3 %collective-permute-start.15 = (f32[16,4,384]{2,1,0:T(4,128)S(1)}, f32[16,4,384]{2,1,0:T(4,128)S(1)}, u32[]{:S(2)}, u32[]{:S(2)}) collective-permute-start(f32[16,4,384]{2,1,0:T(4,128)S(1)} %get-tuple-element.168), channel_id=1, source_target_pairs={{0,1},{1,2},{2,3},{3,4},{4,5},{5,6},{6,7},{7,0},{8,9},{9,10},{10,1... | collective-permute-start | bytes 294920 | tf_op jit(solution)/shard_map/ppermute | solution.py:507
  84.8 8.9 %collective-permute-start.16 = (f32[16,4,384]{2,1,0:T(4,128)S(1)}, f32[16,4,384]{2,1,0:T(4,128)S(1)}, u32[]{:S(2)}, u32[]{:S(2)}) collective-permute-start(f32[16,4,384]{2,1,0:T(4,128)S(1)} %get-tuple-element.169), channel_id=1, source_target_pairs={{0,7},{1,0},{2,1},{3,2},{4,3},{5,4},{6,5},{7,6},{8,15},{9,8},{10,9... | collective-permute-start | bytes 294920 | tf_op jit(solution)/shard_map/ppermute | solution.py:507
  89.1 8.2 %collective-permute-start.18 = (f32[48,128]{1,0:T(8,128)S(1)}, f32[48,128]{1,0:T(8,128)S(1)}, u32[]{:S(2)}, u32[]{:S(2)}) collective-permute-start(f32[48,128]{1,0:T(8,128)S(1)} %get-tuple-element.185), channel_id=1, source_target_pairs={{0,8},{8,16},{16,24},{1,9},{9,17},{17,25},{2,10},{10,18},{18,26},{... | collective-permute-start | bytes 73736 | tf_op jit(solution)/shard_map/ppermute | solution.py:507
  91.8 5.5 %collective-permute-start.19 = (f32[48,128]{1,0:T(8,128)S(1)}, f32[48,128]{1,0:T(8,128)S(1)}, u32[]{:S(2)}, u32[]{:S(2)}) collective-permute-start(f32[48,128]{1,0:T(8,128)S(1)} %get-tuple-element.186), channel_id=1, source_target_pairs={{8,0},{16,8},{24,16},{9,1},{17,9},{25,17},{10,2},{18,10},{26,18},{... | collective-permute-start | bytes 73736 | tf_op jit(solution)/shard_map/ppermute | solution.py:507
  97.3 7.0 %collective-permute-start.20 = (f32[13,4,384]{2,1,0:T(4,128)S(1)}, f32[13,4,384]{2,1,0:T(4,128)S(1)}, u32[]{:S(2)}, u32[]{:S(2)}) collective-permute-start(f32[13,4,384]{2,1,0:T(4,128)S(1)} %get-tuple-element.189), channel_id=1, source_target_pairs={{0,1},{1,2},{2,3},{3,4},{4,5},{5,6},{6,7},{7,0},{8,9},{9,10},{10,1... | collective-permute-start | bytes 239624 | tf_op jit(solution)/shard_map/ppermute | solution.py:507
  97.4 6.9 %collective-permute-start.21 = (f32[13,4,384]{2,1,0:T(4,128)S(1)}, f32[13,4,384]{2,1,0:T(4,128)S(1)}, u32[]{:S(2)}, u32[]{:S(2)}) collective-permute-start(f32[13,4,384]{2,1,0:T(4,128)S(1)} %get-tuple-element.190), channel_id=1, source_target_pairs={{0,7},{1,0},{2,1},{3,2},{4,3},{5,4},{6,5},{7,6},{8,15},{9,8},{10,9... | collective-permute-start | bytes 239624 | tf_op jit(solution)/shard_map/ppermute | solution.py:507
  (9 other events, 316.9 us)
